TPU v7x, 32 devices: a whole 2x2x4 slice. The times are simulated.
32 devices in a mesh: ctx: 8 (over y, x, core), fsdp: 4 (over z).
Axes of the slice: x: 2, y: 2, z: 4, core: 2. Of those that a mesh axis runs over, the one named last changes fastest.
Arguments:
- inputs: float32 [4, 1024, 1536], P('fsdp', 'ctx'), may hold values from -6 to 6
- teacher: float32 [4, 1024, 1536], P('fsdp', 'ctx'), may hold values from -6 to 6
- lengths: int32 [4], P('fsdp'), may hold values from 897 to 1024, as said below
- w_query: bfloat16 [1536, 1536], P('fsdp'), may hold values from -0.15625 to 0.15625
- w_key: bfloat16 [1536, 768], P('fsdp'), may hold values from -0.15625 to 0.15625
- w_value: bfloat16 [1536, 768], P('fsdp'), may hold values from -0.15625 to 0.15625
- w_out: bfloat16 [1536, 1536], P('fsdp'), may hold values from -1.25 to 1.25
- w_gate: bfloat16 [1536, 4096], P('fsdp'), may hold values from -0.15625 to 0.15625
- w_up: bfloat16 [1536, 4096], P('fsdp'), may hold values from -0.15625 to 0.15625
- w_down: bfloat16 [4096, 1536], P('fsdp'), may hold values from -0.09375 to 0.09375
- gain_attn: bfloat16 [1536], P('fsdp'), may hold values from 0.5 to 1.5
- gain_ffn: bfloat16 [1536], P('fsdp'), may hold values from 0.5 to 1.5
Outputs:
- output: float32 [4, 1024, 1536], P('fsdp', 'ctx')
- loss_value: float32 [], replicated
- grad_inputs: float32 [4, 1024, 1536], P('fsdp', 'ctx')
- grad_query: float32 [1536, 1536], P('fsdp')
- grad_key: float32 [1536, 768], P('fsdp')
- grad_value: float32 [1536, 768], P('fsdp')
- grad_out: float32 [1536, 1536], P('fsdp')
- grad_gate: float32 [1536, 4096], P('fsdp')
- grad_up: float32 [1536, 4096], P('fsdp')
- grad_down: float32 [4096, 1536], P('fsdp')
- grad_gain_attn: float32 [1536], P('fsdp')
- grad_gain_ffn: float32 [1536], P('fsdp')
Inputs may be any that keep to these rules, and one draw needn't show every extreme that they name: `lengths`: each sequence has more than 896 valid tokens, and some sequence fills all 1024.
All inputs are finite; a program needn't handle non-finite values.
Results may differ from a plain program's by a relative error of at most 0.023.
Values may be sent and summed in bfloat16 or wider, within the bound.
No kernel may reach another device: no remote copies, remote signals or barrier semaphores. Data moves between devices by JAX's collectives and lax.ppermute only.
A program may use at most 320 MiB of HBM per device.

v0:
```python
import functools

import jax
import jax.numpy as jnp
from jax import lax
from jax.experimental import pallas as pl
from jax.experimental.pallas import tpu as pltpu
from jax.sharding import PartitionSpec as P

HEADS = 16
KV_HEADS = 8
HEAD_DIM = 96
LANES = 128

eps_norm = 1e-05
rope_base = 100000.0
masked_value = -1e30

f32 = jnp.float32
bf16 = jnp.bfloat16

VMEM = pl.BlockSpec(memory_space=pltpu.VMEM)
SMEM = pl.BlockSpec(memory_space=pltpu.SMEM)
HBM = pl.BlockSpec(memory_space=pltpu.HBM)
MIB = 1024 * 1024


def cost(multiply_adds, values):
    return pl.CostEstimate(flops=1, bytes_accessed=1, transcendentals=0)


def in_hbm(*xs):
    return [pltpu.with_memory_space_constraint(x, pltpu.HBM) for x in xs]


def started(sems, first, *pairs):
    copies = [pltpu.make_async_copy(a, b, sems.at[first + n]) for n, (a, b) in enumerate(pairs)]
    for copy in copies:
        copy.start()
    return copies


def times(left, right):
    return jnp.dot(left, right, preferred_element_type=f32)


def times_transposed(left, right):
    return lax.dot_general(left, right, (((1,), (1,)), ((), ())), preferred_element_type=f32)


def transposed_times(left, right):
    return lax.dot_general(left, right, (((0,), (0,)), ((), ())), preferred_element_type=f32)


def norm_scale(features):
    return lax.rsqrt(jnp.mean(features * features, axis=-1, keepdims=True) + eps_norm)


def norm_back(upstream, features, row_scale, gain_vector):
    weighted = upstream * gain_vector
    inner_mean = jnp.mean(weighted * features, axis=-1, keepdims=True)
    grad_rows = row_scale * weighted - features * (row_scale * row_scale * row_scale) * inner_mean
    return (grad_rows, jnp.sum(upstream * (features * row_scale), axis=0))


def partner(x, axis, mask):
    return lax.ppermute(x, axis, [(i, i ^ mask) for i in range(lax.axis_size(axis))])


def plane_sends(x):
    return [partner(x, "ctx", 2 * s) for s in range(1, lax.axis_size("ctx") // 2)]


def core_blocks(mine):
    blocks = []
    for x in mine:
        blocks += [x, partner(x, "ctx", 1)]
    return blocks


def plane_blocks(x):
    return core_blocks([x] + plane_sends(x))


def near_sends(x):
    return [partner(x, "ctx", 2), partner(x, "ctx", 4)]


def far_sends(near):
    half = near[0].shape[0] // 2
    return [partner(near[0][:half], "ctx", 4), partner(near[1][half:], "ctx", 2)]


def square_pieces(x, near, far):
    half = x.shape[0] // 2
    mine = [(0, 0, x), (1, 0, near[0]), (2, 0, near[1]), (3, 0, far[0]), (3, half, far[1])]
    other = together([partner(block, "ctx", 1) for _, _, block in mine])
    pieces = []
    for (s, first, block), swapped in zip(mine, other, strict=True):
        pieces += [(2 * s, first, block), (2 * s + 1, first, swapped)]
    return pieces


def line_sends(x):
    return [partner(x, "fsdp", s) for s in range(1, lax.axis_size("fsdp"))]


def plane_reduce(keep, give):
    chips = chip_sums(keep, give)
    return total(chips[0], chip_sends(chips))


def chip_sums(keep, give):
    got = [partner(x, "ctx", 1) for x in give[::-1]][::-1]
    own = keep[0].astype(f32) + got[0].astype(f32)
    return [own] + [
        (a.astype(f32) + b.astype(f32)).astype(bf16) for a, b in zip(keep[1:], got[1:], strict=True)
    ]


def chip_sends(chips):
    return together([partner(chips[s], "ctx", 2 * s) for s in range(len(chips) - 1, 0, -1)])


def total(own, got):
    for x in got:
        own = own + x.astype(f32)
    return own


def tree_sum(x, axis):
    mask = 1
    while mask < lax.axis_size(axis):
        x = x + partner(x, axis, mask)
        mask *= 2
    return x


def line_blocks(x):
    return [x] + together(line_sends(x))


def line_reduce(parts):
    got = together([partner(parts[s], "fsdp", s) for s in range(1, len(parts))])
    return total(parts[0].astype(f32), got)


def together(xs):
    return list(lax.optimization_barrier(tuple(xs)))


def after(x, *done):
    return lax.optimization_barrier((x, done))[0]


def pick(x, index, axis=0):
    return lax.dynamic_index_in_dim(x, index, axis, False)


def unsort(blocks, me):
    stacked = jnp.stack(blocks)
    return [pick(stacked, me ^ b) for b in range(len(blocks))]


def rope_tables(count):
    half_dim = HEAD_DIM // 2
    frequencies = rope_base ** (-(jnp.arange(half_dim, dtype=f32) * 2.0) / HEAD_DIM)
    angles = jnp.arange(count, dtype=f32)[:, None] * frequencies[None, :]
    cosines, sines = jnp.cos(angles), jnp.sin(angles)
    pad = jnp.zeros((count, LANES - HEAD_DIM), f32)
    return (
        jnp.concatenate([cosines, cosines, pad], axis=1),
        jnp.concatenate([-sines, sines, pad], axis=1),
    )


def turned(x):
    lane = lax.broadcasted_iota(jnp.int32, x.shape, 1)
    half_dim = HEAD_DIM // 2
    return jnp.where(
        lane < half_dim, pltpu.roll(x, LANES - half_dim, 1), pltpu.roll(x, half_dim, 1)
    )


def head_of(x, head):
    if head:
        x = pltpu.roll(x, x.shape[1] - head * HEAD_DIM, 1)
    return x[:, :LANES]


def packed(heads):
    wide = -(-len(heads) * HEAD_DIM // LANES) * LANES
    total = None
    for index, head in enumerate(heads):
        if wide > LANES:
            head = jnp.concatenate([head, jnp.zeros((head.shape[0], wide - LANES), f32)], axis=1)
        if index:
            head = pltpu.roll(head, index * HEAD_DIM, 1)
        total = head if total is None else total + head
    return total


def attention_forward_kernel(C, Z, tokens, q_heads, kv_heads, block, info_ref, *refs):
    R = C // 2
    n_refs, w_parts = refs[:C], refs[C : C + Z]
    cos_hbm, sin_hbm = refs[C + Z : C + Z + 2]
    n_hbm, w_hbm, qkv_hbm, att_hbm, lse_hbm = refs[C + Z + 2 : C + Z + 7]
    block_refs = refs[C + Z + 7 : C + Z + 7 + R]
    n_all_ref, w_ref, lin_ref, qkv_ref, att_ref, lse_ref, cos_ref, sin_ref, sems = refs[C + Z + 7 + R :]
    me, length = info_ref[0], info_ref[1]
    seq = C * tokens
    group = q_heads // kv_heads
    width_low = q_heads * HEAD_DIM
    rows_z = w_ref.shape[0] // Z
    pairs = []
    for j in range(Z):
        at = pl.multiple_of((info_ref[2] ^ j) * rows_z, rows_z)
        pairs.append((w_parts[j].at[:rows_z, :], w_ref.at[pl.ds(at, rows_z), :]))
    tables = started(sems, 0, (cos_hbm, cos_ref), (sin_hbm, sin_ref), *pairs)
    for i in range(C):
        n_all_ref[i * tokens : (i + 1) * tokens, :] = n_refs[i][...]
    for copy in tables[2:]:
        copy.wait()
    saved = started(sems, 2, (n_all_ref, n_hbm), (w_ref, w_hbm))
    step = 4 * tokens
    for start in range(0, seq, step):
        lin_ref[start : start + step, :] = times(n_all_ref[start : start + step, :], w_ref[...])
    for copy in tables[:2]:
        copy.wait()
    lane = lax.broadcasted_iota(jnp.int32, (tokens, LANES), 1)
    for i in range(C):
        rows = pl.ds(pl.multiple_of((me ^ i) * tokens, tokens), tokens)
        lin = lin_ref[i * tokens : (i + 1) * tokens, :]
        cosines, sines = cos_ref[rows, :], sin_ref[rows, :]
        for head in range(q_heads + 2 * kv_heads):
            x = head_of(lin, head)
            if head < q_heads + kv_heads:
                x = x * cosines + turned(x) * sines
            else:
                x = jnp.where(lane < HEAD_DIM, x, 0.0)
            qkv_ref[rows, head * LANES : (head + 1) * LANES] = x.astype(bf16)
    saved += started(sems, 4, (qkv_ref, qkv_hbm))
    scale = HEAD_DIM ** (-0.5)
    for head in range(q_heads):
        k_at = (q_heads + head // group) * LANES
        v_at = k_at + kv_heads * LANES
        for start in range(0, seq, block):
            end = start + block
            q = qkv_ref[start:end, head * LANES : (head + 1) * LANES]
            scores = times_transposed(q, qkv_ref[:end, k_at : k_at + LANES]) * scale
            row = start + lax.broadcasted_iota(jnp.int32, (block, end), 0)
            col = lax.broadcasted_iota(jnp.int32, (block, end), 1)
            scores = jnp.where((col <= row) & (col < length), scores, masked_value)
            row_max = jnp.max(scores, axis=1, keepdims=True)
            weights = jnp.exp(scores - row_max)
            row_sum = jnp.sum(weights, axis=1, keepdims=True)
            probs = (weights * (1.0 / row_sum)).astype(bf16)
            att_ref[start:end, head * LANES : (head + 1) * LANES] = times(
                probs, qkv_ref[:end, v_at : v_at + LANES]
            )
            lse_ref[start:end, head : head + 1] = row_max + jnp.log(row_sum)
    saved += started(sems, 5, (att_ref, att_hbm), (lse_ref, lse_hbm))
    for i in range(C):
        rows = pl.ds(pl.multiple_of((me ^ i) * tokens, tokens), tokens)
        x = att_ref[rows, :]
        low = packed([x[:, h * LANES : (h + 1) * LANES] for h in range(q_heads)])
        at = (i % 2) * tokens
        block_refs[i // 2][at : at + tokens, :] = low[:, :width_low].astype(bf16)
    for copy in saved:
        copy.wait()


def attention_forward(blocks, w_parts, tables, me, length, line, q_heads, kv_heads):
    C, Z = len(blocks), len(w_parts)
    tokens, width = blocks[0].shape
    seq = C * tokens
    heads = q_heads + 2 * kv_heads
    cols = w_parts[0].shape[1]
    saved = [
        ((seq, width), bf16),
        ((width, cols), bf16),
        ((seq, heads * LANES), bf16),
        ((seq, q_heads * LANES), f32),
        ((seq, LANES), f32),
    ]
    part = jax.ShapeDtypeStruct((2 * tokens, q_heads * HEAD_DIM), bf16)
    result = pl.pallas_call(
        functools.partial(attention_forward_kernel, C, Z, tokens, q_heads, kv_heads, 2 * tokens),
        out_shape=[pltpu.HBM(*x) for x in saved] + [part] * (C // 2),
        in_specs=[SMEM] + [VMEM] * C + [HBM] * (Z + 2),
        out_specs=[HBM] * len(saved) + [VMEM] * (C // 2),
        scratch_shapes=[pltpu.VMEM(*saved[0]), pltpu.VMEM(*saved[1]), pltpu.VMEM((seq, cols), f32)]
        + [pltpu.VMEM(*x) for x in saved[2:]]
        + [pltpu.VMEM((seq, LANES), f32)] * 2
        + [pltpu.SemaphoreType.DMA((7 + Z,))],
        compiler_params=pltpu.CompilerParams(vmem_limit_bytes=22 * MIB),
        cost_estimate=cost(seq * width * cols + 2 * seq * seq * heads * LANES, 3 * seq * width),
        name="attention_forward",
    )(jnp.stack([me, length, line]).astype(jnp.int32), *blocks, *in_hbm(*w_parts, *tables))
    return result[: len(saved)], result[len(saved) :]


def attention_backward_kernel(C, tokens, q_heads, kv_heads, block, info_ref, *refs):
    R = C // 2
    mine_refs, other_refs = refs[:R], refs[R:C]
    hbm_refs = refs[C : C + 7]
    dqkv_ref, gain_ref = refs[C + 7 : C + 9]
    keep_refs = refs[C + 9 : C + 9 + R]
    give_refs = refs[C + 9 + R : C + 9 + C]
    refs = refs[C + 9 + C :]
    qkv_ref, att_ref, lse_ref, cos_ref, sin_ref, w_ref, n_all_ref = refs[:7]
    wide_ref, grad_ref, dq_ref, dkv_ref, sems = refs[7:]
    copies = started(sems, 0, *zip(hbm_refs, refs[:7], strict=True))
    me, length = info_ref[0], info_ref[1]
    core = me % 2
    seq = C * tokens
    group = q_heads // kv_heads
    width_low = q_heads * HEAD_DIM
    lane = lax.broadcasted_iota(jnp.int32, (tokens, LANES), 1)
    wide_ref[...] = jnp.zeros_like(wide_ref)
    for i in range(C):
        rows = pl.ds(pl.multiple_of((me ^ i) * tokens, tokens), tokens)
        wide_ref[:, : 2 * width_low] = (other_refs if i % 2 else mine_refs)[i // 2][...].astype(f32)
        wide = wide_ref[...]
        wide = jnp.where(core == 0, wide, pltpu.roll(wide, wide.shape[1] - width_low, 1))
        for head in range(q_heads):
            x = jnp.where(lane < HEAD_DIM, head_of(wide, head), 0.0)
            grad_ref[rows, head * LANES : (head + 1) * LANES] = x.astype(bf16)
    dkv_ref[...] = jnp.zeros_like(dkv_ref)
    scale = HEAD_DIM ** (-0.5)
    for copy in copies[:5]:
        copy.wait()
    for start in range(0, seq, block):
        end = start + block
        lane_b = lax.broadcasted_iota(jnp.int32, (block, LANES), 1)
        delta = jnp.zeros((block, LANES), f32)
        for head in range(q_heads):
            at = slice(head * LANES, (head + 1) * LANES)
            one = jnp.sum(
                grad_ref[start:end, at].astype(f32) * att_ref[start:end, at], axis=1, keepdims=True
            )
            delta = jnp.where(lane_b == head, one, delta)
        delta_t = delta.T
        lse_t = lse_ref[start:end, :].T
        key = lax.broadcasted_iota(jnp.int32, (end, block), 0)
        query = start + lax.broadcasted_iota(jnp.int32, (end, block), 1)
        allowed = (key <= query) & (key < length)
        for head in range(q_heads):
            at = slice(head * LANES, (head + 1) * LANES)
            kv = head // group
            k_at = slice((q_heads + kv) * LANES, (q_heads + kv + 1) * LANES)
            v_at = slice((q_heads + kv_heads + kv) * LANES, (q_heads + kv_heads + kv + 1) * LANES)
            q, grad = qkv_ref[start:end, at], grad_ref[start:end, at]
            k, v = qkv_ref[:end, k_at], qkv_ref[:end, v_at]
            scores = times_transposed(k, q) * scale
            probs = jnp.where(allowed, jnp.exp(scores - lse_t[head : head + 1, :]), 0.0)
            grad_probs = times_transposed(v, grad)
            grad_scores = (probs * (grad_probs - delta_t[head : head + 1, :])).astype(bf16)
            dq_ref[start:end, at] = transposed_times(grad_scores, k) * scale
            dk_at = slice(kv * LANES, (kv + 1) * LANES)
            dv_at = slice((kv_heads + kv) * LANES, (kv_heads + kv + 1) * LANES)
            dkv_ref[:end, dk_at] += times(grad_scores, q) * scale
            dkv_ref[:end, dv_at] += times(probs.astype(bf16), grad)
    for i in range(C):
        rows = pl.ds(pl.multiple_of((me ^ i) * tokens, tokens), tokens)
        cosines, sines = cos_ref[rows, :], sin_ref[rows, :]
        heads = []
        for head in range(q_heads + 2 * kv_heads):
            if head < q_heads:
                x = dq_ref[rows, head * LANES : (head + 1) * LANES]
            else:
                x = dkv_ref[rows, (head - q_heads) * LANES : (head - q_heads + 1) * LANES]
            if head < q_heads + kv_heads:
                x = x * cosines - turned(x) * sines
            heads.append(x)
        dqkv_ref[i * tokens : (i + 1) * tokens, :] = packed(heads).astype(bf16)
    for copy in copies[5:]:
        copy.wait()

    def rows_of(at):
        part = times_transposed(dqkv_ref[...], w_ref[at, :])
        gain = jnp.sum(part * n_all_ref[:, at].astype(f32), axis=0, keepdims=True)
        gain_ref[:, at] = jnp.broadcast_to(gain, (gain_ref.shape[0], gain.shape[1]))
        return part

    parts_of(rows_of, keep_refs, give_refs)


def attention_backward(mine, other, saved, tables, me, length, q_heads, kv_heads):
    C = 2 * len(mine)
    tokens, pair = mine[0].shape
    normed_all, w_qkv, qkv, attended, lse = saved
    width, cols = w_qkv.shape
    loaded = (qkv, attended, lse, *tables, w_qkv, normed_all)
    seq = C * tokens
    heads = q_heads + 2 * kv_heads
    part = jax.ShapeDtypeStruct((tokens, width), bf16)
    result = pl.pallas_call(
        functools.partial(attention_backward_kernel, C, tokens, q_heads, kv_heads, 2 * tokens),
        out_shape=[
            jax.ShapeDtypeStruct((seq, cols), bf16),
            jax.ShapeDtypeStruct((8, width), f32),
        ]
        + [part] * C,
        in_specs=[SMEM] + [VMEM] * C + [HBM] * 7,
        out_specs=[VMEM] * (C + 2),
        scratch_shapes=[pltpu.VMEM(x.shape, x.dtype) for x in loaded]
        + [
            pltpu.VMEM((tokens, -(-pair // LANES) * LANES), f32),
            pltpu.VMEM((seq, q_heads * LANES), bf16),
            pltpu.VMEM((seq, q_heads * LANES), f32),
            pltpu.VMEM((seq, 2 * kv_heads * LANES), f32),
            pltpu.SemaphoreType.DMA((7,)),
        ],
        compiler_params=pltpu.CompilerParams(vmem_limit_bytes=26 * MIB),
        cost_estimate=cost(seq * width * cols + 4 * seq * seq * heads * LANES, 3 * seq * width),
        name="attention_backward",
    )(jnp.stack([me, length]).astype(jnp.int32), *mine, *other, *in_hbm(*loaded))
    return result[0], result[1], result[2 : 2 + C // 2], result[2 + C // 2 :]


def gather_rows(block_refs, all_ref):
    tokens = block_refs[0].shape[0]

    @pl.loop(0, tokens // 16)
    def _(n):
        for i, ref in enumerate(block_refs):
            at = pl.ds(pl.multiple_of(n * 16, 16), 16)
            to = pl.ds(pl.multiple_of(i * tokens + n * 16, 16), 16)
            all_ref[to, :] = ref[at, :]


def parts_of(rows_of, keep_refs, give_refs):
    tokens, width = keep_refs[0].shape
    strip = 4 * LANES

    @pl.loop(0, width // strip)
    def _(n):
        at = pl.ds(pl.multiple_of(n * strip, strip), strip)
        part = rows_of(at)
        for i in range(2 * len(keep_refs)):
            ref = (give_refs if i % 2 else keep_refs)[i // 2]
            ref[:, at] = part[i * tokens : (i + 1) * tokens, :].astype(bf16)


def ffn_forward_kernel(C, cuts, *refs):
    n_refs = refs[:C]
    gu_hbm, down_hbm, n_hbm, act_hbm, coef_hbm = refs[C : C + 5]
    keep_refs = refs[C + 5 : C + 5 + C // 2]
    give_refs = refs[C + 5 + C // 2 : 2 * C + 5]
    gu_ref, down_ref, n_all_ref, act_ref, coef_ref, sems = refs[2 * C + 5 :]
    tokens = n_refs[0].shape[0]
    pairs = [(n_refs[i], n_all_ref.at[i * tokens : (i + 1) * tokens, :]) for i in range(C)]
    weights = started(sems, 3, (gu_hbm, gu_ref), (down_hbm, down_ref), *pairs)
    w = down_ref.shape[0] // cuts
    for copy in weights[2:]:
        copy.wait()
    saved = started(sems, 0, (n_all_ref, n_hbm))
    weights[0].wait()

    @pl.loop(0, cuts)
    def _(j):
        at = pl.ds(pl.multiple_of(j * 2 * w, 2 * w), 2 * w)
        both = times(n_all_ref[...], gu_ref[:, at])
        gate, up = both[:, :w], both[:, w:]
        sigmoid = jax.nn.sigmoid(gate)
        silu = gate * sigmoid
        act_ref[:, pl.ds(pl.multiple_of(j * w, w), w)] = (silu * up).astype(bf16)
        slope = up * (sigmoid * (1.0 + gate * (1.0 - sigmoid)))
        coef_ref[:, at] = jnp.concatenate([slope, silu], axis=1).astype(bf16)

    saved += started(sems, 1, (act_ref, act_hbm), (coef_ref, coef_hbm))
    weights[1].wait()
    parts_of(lambda at: times(act_ref[...], down_ref[:, at]), keep_refs, give_refs)
    for copy in saved:
        copy.wait()


def ffn_forward(blocks, gate_up, down, cuts):
    C = len(blocks)
    tokens, width = blocks[0].shape
    seq, own = C * tokens, down.shape[0]
    saved = [((seq, width), bf16), ((seq, own), bf16), ((seq, 2 * own), bf16)]
    part = jax.ShapeDtypeStruct((tokens, width), bf16)
    result = pl.pallas_call(
        functools.partial(ffn_forward_kernel, C, cuts),
        out_shape=[pltpu.HBM(*x) for x in saved] + [part] * C,
        in_specs=[HBM] * (C + 2),
        out_specs=[HBM] * 3 + [VMEM] * C,
        scratch_shapes=[
            pltpu.VMEM((width, 2 * own), bf16),
            pltpu.VMEM((own, width), bf16),
            *[pltpu.VMEM(*x) for x in saved],
            pltpu.SemaphoreType.DMA((5 + C,)),
        ],
        compiler_params=pltpu.CompilerParams(vmem_limit_bytes=24 * MIB),
        cost_estimate=cost(3 * seq * width * own, 3 * seq * width),
        name="ffn_forward",
    )(*in_hbm(*blocks, gate_up, down))
    return result[:3], result[3 : 3 + C // 2], result[3 + C // 2 :]


def ffn_backward_kernel(C, cuts, *refs):
    g_refs = refs[:C]
    gu_hbm, down_hbm, coef_hbm, g_all_ref, dgu_ref = refs[C : C + 5]
    keep_refs = refs[C + 5 : C + 5 + C // 2]
    give_refs = refs[C + 5 + C // 2 : 2 * C + 5]
    gu_ref, down_ref, coef_ref, sems = refs[2 * C + 5 :]
    copies = started(sems, 0, (down_hbm, down_ref), (coef_hbm, coef_ref), (gu_hbm, gu_ref))
    gather_rows(g_refs, g_all_ref)
    for copy in copies[:2]:
        copy.wait()
    w = down_ref.shape[0] // cuts
    many = 2 if cuts % 2 == 0 else 1

    @pl.loop(0, cuts // many)
    def _(j):
        rows = pl.ds(pl.multiple_of(j * many * w, many * w), many * w)
        grad_act = times_transposed(g_all_ref[...], down_ref[rows, :])
        at = pl.ds(pl.multiple_of(j * many * 2 * w, many * 2 * w), many * 2 * w)
        parts = [grad_act[:, (n // 2) * w : (n // 2 + 1) * w] for n in range(2 * many)]
        both = jnp.concatenate(parts, axis=1)
        dgu_ref[:, at] = (both * coef_ref[:, at].astype(f32)).astype(bf16)

    copies[2].wait()
    parts_of(lambda at: times_transposed(dgu_ref[...], gu_ref[at, :]), keep_refs, give_refs)


def ffn_backward(blocks, gate_up, down, coef, cuts):
    C = len(blocks)
    tokens, width = blocks[0].shape
    seq, own = C * tokens, coef.shape[1] // 2
    part = jax.ShapeDtypeStruct((tokens, width), bf16)
    result = pl.pallas_call(
        functools.partial(ffn_backward_kernel, C, cuts),
        out_shape=[
            jax.ShapeDtypeStruct((seq, width), bf16),
            jax.ShapeDtypeStruct((seq, 2 * own), bf16),
        ]
        + [part] * C,
        in_specs=[VMEM] * C + [HBM] * 3,
        out_specs=[VMEM] * (C + 2),
        scratch_shapes=[
            pltpu.VMEM((width, 2 * own), bf16),
            pltpu.VMEM((own, width), bf16),
            pltpu.VMEM(coef.shape, bf16),
            pltpu.SemaphoreType.DMA((3,)),
        ],
        compiler_params=pltpu.CompilerParams(vmem_limit_bytes=24 * MIB),
        cost_estimate=cost(3 * seq * width * own, 3 * seq * width),
        name="ffn_backward",
    )(*blocks, *in_hbm(gate_up, down, coef))
    return result[:2], result[2 : 2 + C // 2], result[2 + C // 2 :]


def ffn_slices_kernel(C, Z, piece, me_ref, gate_hbm, up_hbm, down_hbm, *refs):
    gu_hbm, rows_hbm, gu_ref, rows_ref, sems = refs
    me = me_ref[0]
    pairs = []
    for j in range(Z):
        for a, ref in enumerate((gate_hbm, up_hbm)):
            at = pl.multiple_of((j * C + me) * piece, piece)
            to = (2 * j + a) * piece
            pairs.append((ref.at[:, pl.ds(at, piece)], gu_ref.at[:, to : to + piece]))
    at = pl.multiple_of(me * piece, piece)
    pairs.append((down_hbm.at[pl.ds(at, piece), :], rows_ref))
    for copy in started(sems, 0, *pairs):
        copy.wait()
    for copy in started(sems, 0, (gu_ref, gu_hbm), (rows_ref, rows_hbm)):
        copy.wait()


def ffn_slices(w_gate, w_up, w_down, me, C, Z):
    rows, ff = w_gate.shape
    width = w_down.shape[1]
    piece = ff // (Z * C)
    shapes = (rows, 2 * Z * piece), (piece, width)
    return pl.pallas_call(
        functools.partial(ffn_slices_kernel, C, Z, piece),
        out_shape=[pltpu.HBM(x, bf16) for x in shapes],
        in_specs=[SMEM, HBM, HBM, HBM],
        out_specs=[HBM, HBM],
        scratch_shapes=[pltpu.VMEM(x, bf16) for x in shapes]
        + [pltpu.SemaphoreType.DMA((2 * Z + 1,))],
        compiler_params=pltpu.CompilerParams(vmem_limit_bytes=8 * MIB),
        cost_estimate=cost(0, 6 * rows * ff // C),
        name="ffn_slices",
    )(me.reshape(1), *in_hbm(w_gate, w_up, w_down))


def arrived(pieces, low_ref, sems):
    pairs = []
    for i, first, ref in pieces:
        pairs.append((ref, low_ref.at[i, pl.ds(first, ref.shape[0]), :]))
    copies = started(sems, 0, *pairs)
    return [[copy for copy, piece in zip(copies, pieces) if piece[0] == i] for i in range(low_ref.shape[0])]


def column_grads_kernel(C, Z, piece, places, me_ref, *refs):
    gate_hbm, up_hbm, low_ref, wide_ref, in_sems, sems = refs[len(places) :]
    me = me_ref[0]
    stride = gate_hbm.shape[1] // Z
    arriving = arrived([(*place, ref) for place, ref in zip(places, refs)], low_ref, in_sems)
    flying = [(), ()]
    for i in range(C):
        slot = i % 2
        for copy in (*flying[slot], *arriving[i]):
            copy.wait()

        @pl.loop(0, low_ref.shape[1] // 16)
        def _(n):
            at = pl.ds(pl.multiple_of(n * 16, 16), 16)
            wide_ref[slot, at, :] = low_ref[i, at, :].astype(f32)

        pairs = []
        for j in range(Z):
            at = pl.multiple_of(j * stride + (me ^ i) * piece, piece)
            for a, ref in enumerate((gate_hbm, up_hbm)):
                to = (2 * j + a) * piece
                pairs.append((wide_ref.at[slot, :, to : to + piece], ref.at[:, pl.ds(at, piece)]))
        flying[slot] = started(sems.at[slot], 0, *pairs)
    for copies in flying:
        for copy in copies:
            copy.wait()


def column_grads(pieces, me, C, Z):
    rows, cols = pieces[0][2].shape
    piece = cols // (2 * Z)
    ff = Z * C * piece
    return pl.pallas_call(
        functools.partial(column_grads_kernel, C, Z, piece, [x[:2] for x in pieces]),
        out_shape=[pltpu.HBM((rows, ff), f32)] * 2,
        in_specs=[SMEM] + [HBM] * len(pieces),
        out_specs=[HBM] * 2,
        scratch_shapes=[
            pltpu.VMEM((C, rows, cols), bf16),
            pltpu.VMEM((2, rows, cols), f32),
            pltpu.SemaphoreType.DMA((len(pieces),)),
            pltpu.SemaphoreType.DMA((2, 2 * Z)),
        ],
        compiler_params=pltpu.CompilerParams(vmem_limit_bytes=16 * MIB),
        cost_estimate=cost(0, 6 * rows * ff),
        name="column_grads",
    )(me.reshape(1), *in_hbm(*[x[2] for x in pieces]))


def row_grads_kernel(C, places, me_ref, *refs):
    out_hbm, low_ref, tall_ref, in_sems, sems = refs[len(places) :]
    me = me_ref[0]
    piece = low_ref.shape[1]
    arriving = arrived([(*place, ref) for place, ref in zip(places, refs)], low_ref, in_sems)
    flying = []
    for i in range(C):
        for copy in arriving[i]:
            copy.wait()

        @pl.loop(0, piece // 16)
        def _(n):
            at = pl.ds(pl.multiple_of(n * 16, 16), 16)
            tall_ref[i, at, :] = low_ref[i, at, :].astype(f32)

        at = pl.multiple_of((me ^ i) * piece, piece)
        flying += started(sems, i, (tall_ref.at[i], out_hbm.at[pl.ds(at, piece), :]))
    for copy in flying:
        copy.wait()


def row_grads(pieces, me, C):
    piece, width = pieces[0][2].shape
    return pl.pallas_call(
        functools.partial(row_grads_kernel, C, [x[:2] for x in pieces]),
        out_shape=pltpu.HBM((C * piece, width), f32),
        in_specs=[SMEM] + [HBM] * len(pieces),
        out_specs=HBM,
        scratch_shapes=[
            pltpu.VMEM((C, piece, width), bf16),
            pltpu.VMEM((C, piece, width), f32),
            pltpu.SemaphoreType.DMA((len(pieces),)),
            pltpu.SemaphoreType.DMA((C,)),
        ],
        compiler_params=pltpu.CompilerParams(vmem_limit_bytes=16 * MIB),
        cost_estimate=cost(0, 4 * C * piece * width),
        name="row_grads",
    )(me.reshape(1), *in_hbm(*[x[2] for x in pieces]))


def middle_forward_kernel(C, Z, piece, info_ref, *refs):
    R = C // 2
    mine_refs, other_refs, w_refs = refs[:R], refs[R:C], refs[C : 2 * C]
    own_hbm, hidden_ref, gain_ref = refs[2 * C : 2 * C + 3]
    middle_ref, normed_ref, att_ref, out_hbm = refs[2 * C + 3 : 2 * C + 7]
    out_ref, low_ref, high_ref, sems = refs[2 * C + 7 :]
    me, line = info_ref[0], info_ref[1]
    rows_z = C * piece
    own_at = pl.ds(pl.multiple_of(line * rows_z, rows_z), rows_z)
    here = started(sems, 1, (own_hbm, out_ref.at[own_at, :]))
    core = me % 2
    tokens, half = hidden_ref.shape[0], mine_refs[0].shape[1]
    cols = w_refs[0].shape[1]
    strips = out_ref.shape[1] // cols
    for i in range(C):
        for j in range(1, Z):
            at = pl.multiple_of((line ^ j) * rows_z + (me ^ i) * piece, piece)
            for c in range(strips):
                first = ((j - 1) * strips + c) * piece
                out_ref[pl.ds(at, piece), c * cols : (c + 1) * cols] = w_refs[i][first : first + piece, :]
    for copy in here:
        copy.wait()
    saved = started(sems, 0, (out_ref, out_hbm))
    low_ref[...] = jnp.zeros_like(low_ref)
    high_ref[...] = jnp.zeros_like(high_ref)
    for s in range(R):
        own = mine_refs[s][:tokens, :].astype(f32)
        other = other_refs[s][tokens:, :].astype(f32)
        low_ref[:, :half] = jnp.where(core == 0, own, other)
        high_ref[:, :half] = jnp.where(core == 0, other, own)
        pair = low_ref[...] + pltpu.roll(high_ref[...], half, 1)
        at = pl.multiple_of(((me // 2) ^ s) * 2 * half, 2 * half)
        att_ref[:, pl.ds(at, 2 * half)] = pair.astype(bf16)
    middle = hidden_ref[...] + times(att_ref[...], out_ref[...])
    middle_ref[...] = middle
    normed_ref[...] = (middle * norm_scale(middle) * gain_ref[...]).astype(bf16)
    for copy in saved:
        copy.wait()


def middle_forward(mine, other, w_blocks, w_own, hidden, gain, me, line, Z):
    C = len(w_blocks)
    tokens, width = hidden.shape
    half = mine[0].shape[1]
    cols = w_blocks[0].shape[1]
    strips = width // cols
    piece = w_own.shape[0] // C
    if piece % 16 or (2 * half) % LANES:
        rows = [x.reshape(Z - 1, strips, piece, cols).transpose(0, 2, 1, 3) for x in w_blocks]
        rows = jnp.stack(unsort([x.reshape(Z - 1, piece, width) for x in rows], me), axis=1)
        rows = jnp.concatenate([w_own[None], rows.reshape(Z - 1, C * piece, width)])
        out_all = jnp.concatenate([pick(rows, line ^ j) for j in range(Z)], axis=0)
        heads = []
        for a, b in zip(mine, other, strict=True):
            heads += [a[:tokens], b[tokens:]]
        attended = jnp.concatenate(unsort(heads, me), axis=1)
        middle = hidden + times(attended, out_all)
        return middle, (middle * norm_scale(middle) * gain).astype(bf16), attended, out_all
    return pl.pallas_call(
        functools.partial(middle_forward_kernel, C, Z, piece),
        out_shape=[
            jax.ShapeDtypeStruct((tokens, width), f32),
            jax.ShapeDtypeStruct((tokens, width), bf16),
            jax.ShapeDtypeStruct((tokens, width), bf16),
            pltpu.HBM((width, width), bf16),
        ],
        in_specs=[SMEM] + [VMEM] * 2 * C + [HBM] + [VMEM] * 2,
        out_specs=[VMEM] * 3 + [HBM],
        scratch_shapes=[
            pltpu.VMEM((width, width), bf16),
            pltpu.VMEM((tokens, 2 * half), f32),
            pltpu.VMEM((tokens, 2 * half), f32),
            pltpu.SemaphoreType.DMA((2,)),
        ],
        compiler_params=pltpu.CompilerParams(vmem_limit_bytes=16 * MIB),
        cost_estimate=cost(tokens * width * width, 3 * width * width),
        name="middle_forward",
    )(jnp.stack([me, line]), *mine, *other, *w_blocks, *in_hbm(w_own), hidden, gain.reshape(1, width))


def middle_backward_kernel(R, info_ref, *refs):
    own_ref, got_refs = refs[0], refs[1:R]
    middle_ref, gain_ref, grad_out_ref, out_hbm = refs[R : R + 4]
    grad_ref, low_ref, gain_grad_ref = refs[R + 4 : R + 7]
    pair_refs, (att_ref, out_ref, sems) = refs[R + 7 : 2 * R + 7], refs[2 * R + 7 :]
    copies = started(sems, 0, (out_hbm, out_ref))
    upstream = own_ref[...]
    for ref in got_refs:
        upstream = upstream + ref[...].astype(f32)
    middle = middle_ref[...]
    back, gain_grad = norm_back(upstream, middle, norm_scale(middle), gain_ref[...])
    gain_grad_ref[...] = gain_grad.reshape(gain_grad_ref.shape)
    grad = grad_out_ref[...] + back
    grad_ref[...] = grad
    low = grad.astype(bf16)
    low_ref[...] = low
    for copy in copies:
        copy.wait()
    att_ref[...] = times_transposed(low, out_ref[...]).astype(bf16)
    pair_cols = pair_refs[0].shape[1]
    for s in range(R):
        at = pl.multiple_of(((info_ref[0] // 2) ^ s) * pair_cols, pair_cols)
        pair_refs[s][...] = att_ref[:, pl.ds(at, pair_cols)]


def middle_backward(own, got, middle, gain, grad_output, out_all, me):
    R = len(got) + 1
    tokens, width = middle.shape
    pair_cols = width // R
    if pair_cols % LANES:
        upstream = total(own, got)
        back, gain_grad = norm_back(upstream, middle, norm_scale(middle), gain)
        grad = grad_output + back
        low = grad.astype(bf16)
        cut = times_transposed(low, out_all).astype(bf16).reshape(tokens, R, pair_cols)
        return grad, low, gain_grad[None], *[pick(cut, (me // 2) ^ s, 1) for s in range(R)]
    result = pl.pallas_call(
        functools.partial(middle_backward_kernel, R),
        out_shape=[
            jax.ShapeDtypeStruct((tokens, width), f32),
            jax.ShapeDtypeStruct((tokens, width), bf16),
            jax.ShapeDtypeStruct((1, width), f32),
        ]
        + [pltpu.VMEM((tokens, pair_cols), bf16)] * R,
        in_specs=[SMEM] + [VMEM] * (R + 3) + [HBM],
        out_specs=[VMEM] * (3 + R),
        scratch_shapes=[
            pltpu.VMEM((tokens, width), bf16),
            pltpu.VMEM((width, width), bf16),
            pltpu.SemaphoreType.DMA((1,)),
        ],
        compiler_params=pltpu.CompilerParams(vmem_limit_bytes=16 * MIB),
        cost_estimate=cost(tokens * width * width, 3 * width * width),
        name="middle_backward",
    )(me.reshape(1), own, *got, middle, gain.reshape(1, width), grad_output, *in_hbm(out_all))
    return result


def out_grads_kernel(C, Z, piece, info_ref, att_ref, low_ref, *refs):
    keep_refs, give_refs, sum_ref = refs[: C // 2], refs[C // 2 : C], refs[C]
    me = info_ref[0]
    rows_z = C * piece
    sum_ref[...] = transposed_times(att_ref[...], low_ref[...])
    for i in range(C):
        ref = (give_refs if i % 2 else keep_refs)[i // 2]
        for j in range(Z):
            at = pl.multiple_of(j * rows_z + (me ^ i) * piece, piece)
            ref[j * piece : (j + 1) * piece, :] = sum_ref[pl.ds(at, piece), :].astype(bf16)


def out_grads(attended, low, me, C, Z):
    width = attended.shape[1]
    piece = width // (C * Z)
    if piece % 16:
        grad = transposed_times(attended, low).astype(bf16).reshape(Z, C, piece, width)
        grad = [pick(grad, me ^ i, 1).reshape(Z * piece, width) for i in range(C)]
        return grad[0::2], grad[1::2]
    result = pl.pallas_call(
        functools.partial(out_grads_kernel, C, Z, piece),
        out_shape=[pltpu.VMEM((Z * piece, width), bf16)] * C,
        in_specs=[SMEM, VMEM, VMEM],
        out_specs=[VMEM] * C,
        scratch_shapes=[pltpu.VMEM((width, width), f32)],
        compiler_params=pltpu.CompilerParams(vmem_limit_bytes=18 * MIB),
        cost_estimate=cost(2 * attended.shape[0] * width * width, 3 * width * width),
        name="out_grads",
    )(me.reshape(1), attended, low)
    return result[: C // 2], result[C // 2 :]


EXTRA = 16


def attention_packs_kernel(Z, C, info_ref, *refs):
    R = C // 2
    n_hbm, dqkv_ref, out_refs = refs[0], refs[1], refs[2 : R + 2]
    gain_one_ref, gain_two_ref, error_ref, pack_hbm = refs[R + 2 : R + 6]
    n_ref, sum_ref, tall_ref, sems = refs[R + 6 :]
    arriving = started(sems, 0, (n_hbm, n_ref))
    width, cols = n_ref.shape[1], tall_ref.shape[1]
    rows, tall = width // Z, tall_ref.shape[0] // Z
    piece = sum_ref.shape[0] // Z
    out = out_refs[0][...]
    for ref in out_refs[1:]:
        out = out + ref[...].astype(f32)
    sum_ref[...] = out.astype(bf16)
    line = info_ref[0]
    row = lax.broadcasted_iota(jnp.int32, (EXTRA, cols), 0)
    lane = lax.broadcasted_iota(jnp.int32, (EXTRA, cols), 1)
    error = error_ref[0, 0]
    high = error.astype(bf16).astype(f32)
    error = jnp.where(lane == 2 * line, high, jnp.where(lane == 2 * line + 1, error - high, 0.0))
    for j in range(Z):
        under = j * tall + rows
        for n in range(width // cols):
            at = slice(n * cols, (n + 1) * cols)
            tall_ref[under + n * piece : under + (n + 1) * piece, :] = sum_ref[
                j * piece : (j + 1) * piece, at
            ]
        at = slice(j * rows, (j + 1) * rows)
        extra = jnp.where(row == 0, gain_one_ref[0:1, at], jnp.where(row == 1, gain_two_ref[0:1, at], 0.0))
        extra = jnp.where(row == 2, error, extra)
        tall_ref[(j + 1) * tall - EXTRA : (j + 1) * tall, :] = extra.astype(bf16)
    for copy in arriving:
        copy.wait()

    @pl.loop(0, Z)
    def _(j):
        at = pl.ds(pl.multiple_of(j * rows, LANES), rows)
        to = pl.ds(pl.multiple_of(j * tall, 16), rows)
        tall_ref[to, :] = transposed_times(n_ref[:, at], dqkv_ref[...]).astype(bf16)

    for copy in started(sems, 0, (tall_ref, pack_hbm)):
        copy.wait()


def attention_packs(normed_all, grad_qkv, out_parts, gain_one, gain_two, error, line, Z, C):
    width = normed_all.shape[1]
    cols = grad_qkv.shape[1]
    rows = width // Z
    tall, parts = out_parts[0].shape[0], C // 2
    piece = tall // Z
    if rows != cols or piece % 16:
        grad = transposed_times(normed_all, grad_qkv).astype(bf16)
        grad_out = total(out_parts[0], out_parts[1:]).astype(bf16)
        lane = jnp.arange(cols, dtype=jnp.int32)
        high = error.astype(bf16)
        low = (error - high.astype(f32)).astype(bf16)
        zero = jnp.zeros((), bf16)
        error_row = jnp.where(lane == 2 * line, high, jnp.where(lane == 2 * line + 1, low, zero))
        packs = []
        for j in range(Z):
            at = slice(j * rows, (j + 1) * rows)
            out = grad_out[j * piece : (j + 1) * piece]
            gains = [jnp.pad(x[at].astype(bf16), (0, cols - rows)) for x in (gain_one[0], gain_two[0])]
            extra = jnp.pad(jnp.stack([*gains, error_row]), ((0, EXTRA - 3), (0, 0)))
            packs += [grad[at], *[out[:, c : c + cols] for c in range(0, width, cols)], extra]
        return jnp.concatenate(packs, axis=0)
    shape = (Z * (rows + piece * width // cols + EXTRA), cols)
    return pl.pallas_call(
        functools.partial(attention_packs_kernel, Z, C),
        out_shape=pltpu.HBM(shape, bf16),
        in_specs=[SMEM, HBM] + [VMEM] * (parts + 4),
        out_specs=HBM,
        scratch_shapes=[
            pltpu.VMEM(normed_all.shape, bf16),
            pltpu.VMEM((tall, width), bf16),
            pltpu.VMEM(shape, bf16),
            pltpu.SemaphoreType.DMA((1,)),
        ],
        compiler_params=pltpu.CompilerParams(vmem_limit_bytes=16 * MIB),
        cost_estimate=cost(normed_all.shape[0] * width * cols, 3 * width * width),
        name="attention_packs",
    )(line.reshape(1), *in_hbm(normed_all), grad_qkv, *out_parts, gain_one, gain_two, error.reshape(1, 1))


def attention_grads_kernel(C, rows, q_cols, kv_cols, places, me_ref, *refs):
    count = len(places)
    gain_ref, valid_ref = refs[count : count + 2]
    query_ref, key_ref, value_ref, out_ref, gains_ref, loss_ref = refs[count + 2 : count + 8]
    low_ref, sort_ref, extra_ref, in_sems = refs[count + 8 :]
    me = me_ref[0]
    cols = sort_ref.shape[2]
    strips = out_ref.shape[1] // cols
    piece = (low_ref.shape[1] - rows - EXTRA) // strips
    arriving = arrived([(*place, ref) for place, ref in zip(places, refs)], low_ref, in_sems)
    for i in range(C):
        for copy in arriving[i]:
            copy.wait()

        @pl.loop(0, rows // 16)
        def _(n):
            rows_n = pl.ds(pl.multiple_of(n * 16, 16), 16)
            sort_ref[me ^ i, rows_n, :] = low_ref[i, rows_n, :].astype(f32)

        at = pl.ds(pl.multiple_of((me ^ i) * piece, piece), piece)
        for c in range(strips):
            strip = low_ref[i, rows + c * piece : rows + (c + 1) * piece, :]
            out_ref[at, c * cols : (c + 1) * cols] = strip.astype(f32)
        extra_ref[me ^ i] = low_ref[i, low_ref.shape[1] - EXTRA :, :].astype(f32)
    extra = extra_ref[0]
    for b in range(1, C):
        extra = extra + extra_ref[b]
    row = lax.broadcasted_iota(jnp.int32, gains_ref.shape, 0)
    gains_ref[...] = extra[:8, :] / jnp.where(row == 0, gain_ref[...], 1.0)
    loss_ref[...] = jnp.sum(extra[2:3, :], axis=1, keepdims=True) / valid_ref[0, 0]
    lane = lax.broadcasted_iota(jnp.int32, sort_ref.shape[1:], 1)
    for ref, first, size in (
        (query_ref, 0, q_cols),
        (key_ref, q_cols, kv_cols),
        (value_ref, q_cols + kv_cols, kv_cols),
    ):
        many = cols // size
        for group in range(C // many):
            whole = None
            for j in range(many):
                x = sort_ref[group * many + j]
                shift = (j * size - first) % cols
                x = pltpu.roll(x, shift, 1) if shift else x
                whole = x if whole is None else jnp.where(lane < j * size, whole, x)
            ref[:, group * cols : (group + 1) * cols] = whole


def attention_grads(pieces, me, gain, valid_count, C, rows, width, q_cols, kv_cols, kv_copies):
    tall, cols = pieces[0][2].shape
    strips = width // cols
    piece = (tall - rows - EXTRA) // strips
    many = C // kv_copies
    if kv_copies > 1 or cols % q_cols or cols % kv_cols or q_cols + 2 * kv_cols != cols or rows != cols or piece % 16:
        parts = unsort([x[2] for x in pieces], me)

        def kv_final(start):
            own = [part[:rows, start : start + kv_cols].astype(f32) for part in parts]
            own = [sum(own[n : n + kv_copies]) for n in range(0, C, kv_copies)]
            return jnp.concatenate(own, axis=1)

        query = jnp.concatenate([part[:rows, :q_cols] for part in parts], axis=1).astype(f32)
        outs = [part[rows : tall - EXTRA].reshape(strips, piece, cols).transpose(1, 0, 2) for part in parts]
        out = jnp.concatenate([x.reshape(piece, width) for x in outs], axis=0).astype(f32)
        extra = sum([part[tall - EXTRA :].astype(f32) for part in parts])
        gains = extra[0, :rows] / gain, extra[1, :rows]
        loss = jnp.sum(extra[2]) / valid_count
        return query, kv_final(q_cols), kv_final(q_cols + kv_cols), out, *gains, loss
    *grads, gains, loss = pl.pallas_call(
        functools.partial(
            attention_grads_kernel, C, rows, q_cols, kv_cols, [x[:2] for x in pieces]
        ),
        out_shape=[
            jax.ShapeDtypeStruct((rows, C * q_cols), f32),
            jax.ShapeDtypeStruct((rows, many * kv_cols), f32),
            jax.ShapeDtypeStruct((rows, many * kv_cols), f32),
            jax.ShapeDtypeStruct((C * piece, width), f32),
            jax.ShapeDtypeStruct((8, cols), f32),
            jax.ShapeDtypeStruct((1, 1), f32),
        ],
        in_specs=[SMEM] + [HBM] * len(pieces) + [VMEM] * 2,
        out_specs=[VMEM] * 6,
        scratch_shapes=[
            pltpu.VMEM((C, tall, cols), bf16),
            pltpu.VMEM((C, rows, cols), f32),
            pltpu.VMEM((C, EXTRA, cols), f32),
            pltpu.SemaphoreType.DMA((len(pieces),)),
        ],
        compiler_params=pltpu.CompilerParams(vmem_limit_bytes=24 * MIB),
        cost_estimate=cost(0, 8 * rows * C * cols),
        name="attention_grads",
    )(
        me.reshape(1),
        *in_hbm(*[x[2] for x in pieces]),
        gain.reshape(1, rows),
        valid_count.reshape(1, 1),
    )
    return *grads, gains[0], gains[1], loss[0, 0]


def local(
    inputs,
    teacher,
    lengths,
    w_query,
    w_key,
    w_value,
    w_out,
    w_gate,
    w_up,
    w_down,
    gain_attn,
    gain_ffn,
):
    hidden_in = inputs[0]
    target = teacher[0]
    seq_length = lengths[0]
    tokens, width = hidden_in.shape
    C = lax.axis_size("ctx")
    Z = lax.axis_size("fsdp")
    R = C // 2
    p = lax.axis_index("ctx")
    z = lax.axis_index("fsdp")
    core = p % 2
    rows_z = width // Z
    seq = C * tokens
    q_heads = HEADS // C
    kv_heads = max(1, KV_HEADS // C)
    kv_copies = max(1, C // KV_HEADS)
    q_cols = q_heads * HEAD_DIM
    kv_cols = kv_heads * HEAD_DIM
    qkv_cols = q_cols + 2 * kv_cols
    positions = p * tokens + jnp.arange(tokens, dtype=jnp.int32)

    small = jnp.concatenate(
        [gain_attn.astype(f32), gain_ffn.astype(f32), jnp.full((LANES,), seq_length).astype(f32)]
    )
    small = jnp.stack(unsort(line_blocks(small.reshape(1, -1)), z)).reshape(Z, -1)
    gain_one = small[:, :rows_z].reshape(width)
    gain_two = small[:, rows_z : 2 * rows_z].reshape(width)
    valid_count = jnp.sum(small[:, 2 * rows_z])
    ff = w_gate.shape[1]
    ff_piece, own = ff // (Z * C), ff // C
    packed_ffn = ff_piece % LANES == 0
    if packed_ffn:
        cuts = Z
        gate_up_own, down_own = ffn_slices(w_gate, w_up, w_down, p, C, Z)
    else:
        cuts = 1
        gate_up_own = jnp.concatenate(
            [pick(w.reshape(rows_z, Z, C, ff_piece), p, 2).reshape(rows_z, own) for w in (w_gate, w_up)],
            axis=1,
        )
        down_own = lax.dynamic_slice_in_dim(w_down, p * ff_piece, ff_piece, 0)
    kv_start = (p * KV_HEADS // C) * HEAD_DIM
    out_piece = rows_z // C
    qkv_own = jnp.concatenate(
        [
            lax.dynamic_slice_in_dim(w_query, p * q_cols, q_cols, 1),
            lax.dynamic_slice_in_dim(w_key, kv_start, kv_cols, 1),
            lax.dynamic_slice_in_dim(w_value, kv_start, kv_cols, 1),
            jnp.zeros((rows_z, -qkv_cols % LANES), bf16),
        ],
        axis=1,
    )
    out_own = lax.dynamic_slice_in_dim(w_out, p * out_piece, out_piece, 0)
    cols = qkv_own.shape[1]
    out_own = jnp.concatenate([out_own[:, c : c + cols] for c in range(0, width, cols)], axis=0)

    scale_one = norm_scale(hidden_in)
    normed_one = (hidden_in * scale_one * gain_one).astype(bf16)
    weights_own = jnp.concatenate([qkv_own, out_own], axis=0)
    tables = rope_tables(seq)
    normed_got, weights, tables = lax.optimization_barrier(
        (plane_sends(normed_one), line_sends(weights_own), tables)
    )
    normed_blocks = together(core_blocks([normed_one] + normed_got))
    gate_up_own, down_own = after((gate_up_own, down_own), weights)
    gate_up = lax.all_gather(gate_up_own, "fsdp", axis=0, tiled=True)
    down_rows = lax.all_gather(down_own, "fsdp", axis=0, tiled=True)
    out_line = jnp.concatenate([x[rows_z:] for x in weights], axis=0)
    out_got = plane_sends(out_line)
    (normed_all, *saved), mine = attention_forward(
        normed_blocks, [weights_own] + weights, tables, p, seq_length, z, q_heads, kv_heads
    )

    out_blocks = together(core_blocks([out_line] + after(out_got, normed_all)))
    mine = after(mine, out_blocks)
    mine = [mine[0]] + together([partner(mine[s], "ctx", 2 * s) for s in range(1, R)])
    other = [partner(x, "ctx", 1) for x in mine]
    middle, normed_two_own, attended_tokens, out_all = middle_forward(
        mine, other, out_blocks, w_out, hidden_in, gain_two, p, z, Z
    )

    normed_two_blocks = plane_blocks(normed_two_own)
    (normed_two, activated, coef), keep, give = ffn_forward(
        normed_two_blocks, gate_up, down_rows, cuts
    )
    output = middle + plane_reduce(keep, give)

    valid_rows = (positions < seq_length).astype(f32)
    residual_error = output - target
    squares = jnp.sum(valid_rows[:, None] * residual_error * residual_error)
    grad_output = valid_rows[:, None] * (2.0 * residual_error) / valid_count

    (grad_low, grad_gu), keep, give = ffn_backward(
        plane_blocks(grad_output.astype(bf16)), gate_up, down_rows, coef, cuts
    )
    chips = chip_sums(keep, give)
    grad_gate_up = transposed_times(normed_two, after(grad_gu, chips)).astype(bf16)
    grad_down = transposed_times(activated, after(grad_low, grad_gate_up)).astype(bf16)
    shard_gate_up = lax.psum_scatter(grad_gate_up, "fsdp", scatter_dimension=0, tiled=True)
    shard_down = lax.psum_scatter(grad_down, "fsdp", scatter_dimension=0, tiled=True)
    grad_middle, m_low, grad_gain_two, *pairs = middle_backward(
        chips[0], after(chip_sends(chips), grad_down), middle, gain_two, grad_output, out_all, p
    )

    out_keep, out_give = out_grads(attended_tokens, after(m_low, pairs), p, C, Z)
    mine = [pairs[0]] + together([partner(pairs[s], "ctx", 2 * s) for s in range(1, R)])
    other = [partner(x, "ctx", 1) for x in mine]
    out_chips = chip_sums(out_keep, out_give)
    mine = after(mine, out_chips)
    grad_qkv, gain_part, keep, give = attention_backward(
        mine, other, (normed_all, *saved), tables, p, seq_length, q_heads, kv_heads
    )
    chips = chip_sums(keep, give)
    square = packed_ffn and C == 8
    out_got, grad_qkv = lax.optimization_barrier((chip_sends(out_chips), grad_qkv))
    packs = attention_packs(
        normed_all, grad_qkv, [out_chips[0]] + out_got, gain_part, grad_gain_two, squares, z, Z, C
    )
    shard_packs = lax.psum_scatter(packs, "fsdp", scatter_dimension=0, tiled=True)
    normed_got = [partner(x, "ctx", 2 * (s + 1)) for s, x in enumerate(after(chips[1:], out_got))]
    near = near_sends(after(shard_gate_up, out_got)) if square else []
    normed_got, near = lax.optimization_barrier((normed_got, near))
    grad_normed_one = total(chips[0], normed_got)
    back_one, _ = norm_back(grad_normed_one, hidden_in, scale_one, gain_one)
    grad_hidden = grad_middle + back_one


    if square:
        down_sent = after(shard_down, normed_got)
        far, down_got = lax.optimization_barrier((far_sends(near), plane_sends(down_sent)))
        pieces = square_pieces(shard_gate_up, near, far)
        down_blocks = together(core_blocks([shard_down] + down_got))
        pack_got = plane_sends(after(shard_packs, down_blocks))
        final_gate, final_up = column_grads(pieces, p, C, Z)
        final_down = row_grads([(i, 0, x) for i, x in enumerate(down_blocks)], p, C)
        pack_got, final_gate, final_down = lax.optimization_barrier((pack_got, final_gate, final_down))
        pack_blocks = together(core_blocks([shard_packs] + pack_got))
    else:
        pack_blocks = plane_blocks(shard_packs)
        gate_up, down = [
            jnp.stack(unsort(plane_blocks(x), p)).astype(f32) for x in (shard_gate_up, shard_down)
        ]
        gate_up = gate_up.reshape(C, rows_z, 2, Z, ff_piece).transpose(2, 1, 3, 0, 4)
        final_gate, final_up = gate_up.reshape(2, rows_z, ff)
        final_down = down.reshape(C * ff_piece, width)
    pieces = [(i, 0, block) for i, block in enumerate(pack_blocks)]
    final_query, final_key, final_value, final_out, *final_gains, loss_value = attention_grads(
        pieces,
        p,
        gain_attn.astype(f32),
        valid_count,
        C,
        rows_z,
        width,
        q_cols,
        kv_cols,
        kv_copies,
    )

    return (
        output[None],
        loss_value,
        grad_hidden[None],
        final_query,
        final_key,
        final_value,
        final_out,
        final_gate,
        final_up,
        final_down,
        *final_gains,
    )


def solution(mesh):
    return jax.shard_map(
        local,
        mesh=mesh,
        in_specs=(
            P("fsdp", "ctx", None),
            P("fsdp", "ctx", None),
            P("fsdp"),
            P("fsdp", None),
            P("fsdp", None),
            P("fsdp", None),
            P("fsdp", None),
            P("fsdp", None),
            P("fsdp", None),
            P("fsdp", None),
            P("fsdp"),
            P("fsdp"),
        ),
        out_specs=(
            P("fsdp", "ctx", None),
            P(),
            P("fsdp", "ctx", None),
            P("fsdp", None),
            P("fsdp", None),
            P("fsdp", None),
            P("fsdp", None),
            P("fsdp", None),
            P("fsdp", None),
            P("fsdp", None),
            P("fsdp"),
            P("fsdp"),
        ),
        check_vma=False,
    )
```

profile of v0, /device:TPU:0, one launch (start us, length us, event | category | flops | bytes accessed | tf_op | source)
XLA Modules:
  0.0 435.1 jit_solution(12717022981346374057)
XLA Ops:
  9.4 3.1 collective-permute-start
  24.7 3.1 collective-permute-start.8
  37.0 11.2 %collective-permute-done.5.refs_4_ = bf16[128,1536]{1,0:T(8,128)(2,1)S(1)} collective-permute-done((bf16[128,1536]{1,0:T(8,128)(2,1)S(1)}, bf16[128,1536]{1,0:T(8,128)(2,1)S(1)}, u32[]{:S(2)}, u32[]{:S(2)}) %collective-permute-start.5) | collective-permute-done | bytes 393248 | tf_op jit(solution)/shard_map/ppermute | solution.py:67
  48.2 9.8 %collective-permute-done.8.refs_10_ = bf16[576,384]{1,0:T(8,128)(2,1)} collective-permute-done((bf16[576,384]{1,0:T(8,128)(2,1)S(1)}, bf16[576,384]{1,0:T(8,128)(2,1)}, u32[]{:S(2)}, u32[]{:S(2)}) %collective-permute-start.8) | collective-permute-done | bytes 442400 | tf_op jit(solution)/shard_map/ppermute | solution.py:67
  69.1 11.2 %attention_forward.1 = (bf16[1024,1536]{1,0:T(8,128)(2,1)}, bf16[1536,384]{1,0:T(8,128)(2,1)}, bf16[1024,512]{1,0:T(8,128)(2,1)}, f32[1024,256]{1,0:T(8,128)}, f...) custom-call(s32[3]{0:T(128)S(1)} %pad_add_fusion.1.info_ref, ...), custom_call_target="tpu_custom_call" | custom-call | flops 1 | bytes 1 | tf_op jit(solution)/shard_map/attention_forward/pallas_call | solution.py:287
  80.3 3.9 collective-permute-done.15.refs_12_
  99.7 4.2 middle_forward.1
  108.1 8.5 %collective-permute-done.28.refs_2_ = bf16[128,1536]{1,0:T(8,128)(2,1)S(1)} collective-permute-done((bf16[128,1536]{1,0:T(8,128)(2,1)S(1)}, bf16[128,1536]{1,0:T(8,128)(2,1)S(1)}, u32[]{:S(2)}, u32[]{:S(2)}) %collective-permute-start.28) | collective-permute-done | bytes 393248 | tf_op jit(solution)/shard_map/ppermute | solution.py:67
  116.6 7.0 %collective-permute-done.30.refs_4_ = bf16[128,1536]{1,0:T(8,128)(2,1)S(1)} collective-permute-done((bf16[128,1536]{1,0:T(8,128)(2,1)S(1)}, bf16[128,1536]{1,0:T(8,128)(2,1)S(1)}, u32[]{:S(2)}, u32[]{:S(2)}) %collective-permute-start.30) | collective-permute-done | bytes 393248 | tf_op jit(solution)/shard_map/ppermute | solution.py:67
  127.1 38.8 %all-gather.3.cloned.1.call-done.refs_8_ = bf16[1536,1024]{1,0:T(8,128)(2,1)} async-done(((bf16[384,1024]{1,0:T(8,128)(2,1)}), bf16[1536,1024]{1,0:T(8,128)(2,1)}) %all-gather.3.cloned.1.call-update) | async-done | bytes 3145744 | tf_op jit(solution)/shard_map/all_gather | solution.py:1121
  165.9 9.6 %ffn_forward.1 = (bf16[1024,1536]{1,0:T(8,128)(2,1)}, bf16[1024,512]{1,0:T(8,128)(2,1)}, bf16[1024,1024]{1,0:T(8,128)(2,1)}, bf16[128,1536]{1,0:T(8,128)(2,1)S(1...) custom-call(bf16[128,1536]{1,0:T(8,128)(2,1)} %copy-done.7, ...), custom_call_target="tpu_custom_call" | custom-call | flops 1 | bytes 1 | tf_op jit(solution)/shard_map/ffn_forward/pallas_call | solution.py:485
  184.6 5.7 %collective-permute-done.40 = bf16[128,1536]{1,0:T(8,128)(2,1)S(1)} collective-permute-done((bf16[128,1536]{1,0:T(8,128)(2,1)}, bf16[128,1536]{1,0:T(8,128)(2,1)S(1)}, u32[]{:S(2)}, u32[]{:S(2)}) %collective-permute-start.40) | collective-permute-done | bytes 393248 | tf_op jit(solution)/shard_map/ppermute | solution.py:67
  190.3 9.7 %collective-permute-done.38 = bf16[128,1536]{1,0:T(8,128)(2,1)S(1)} collective-permute-done((bf16[128,1536]{1,0:T(8,128)(2,1)}, bf16[128,1536]{1,0:T(8,128)(2,1)S(1)}, u32[]{:S(2)}, u32[]{:S(2)}) %collective-permute-start.38) | collective-permute-done | bytes 393248 | tf_op jit(solution)/shard_map/ppermute | solution.py:67
  207.5 8.6 %collective-permute-done.42.refs_2_ = bf16[128,1536]{1,0:T(8,128)(2,1)S(1)} collective-permute-done((bf16[128,1536]{1,0:T(8,128)(2,1)S(1)}, bf16[128,1536]{1,0:T(8,128)(2,1)S(1)}, u32[]{:S(2)}, u32[]{:S(2)}) %collective-permute-start.42) | collective-permute-done | bytes 393248 | tf_op jit(solution)/shard_map/ppermute | solution.py:67
  216.0 5.4 %collective-permute-done.44.refs_4_ = bf16[128,1536]{1,0:T(8,128)(2,1)S(1)} collective-permute-done((bf16[128,1536]{1,0:T(8,128)(2,1)S(1)}, bf16[128,1536]{1,0:T(8,128)(2,1)S(1)}, u32[]{:S(2)}, u32[]{:S(2)}) %collective-permute-start.44) | collective-permute-done | bytes 393248 | tf_op jit(solution)/shard_map/ppermute | solution.py:67
  225.0 8.0 %ffn_backward.1 = (bf16[1024,1536]{1,0:T(8,128)(2,1)S(1)}, bf16[1024,1024]{1,0:T(8,128)(2,1)S(1)}, bf16[128,1536]{1,0:T(8,128)(2,1)S(1)}, bf16[128,1536]{1,0:T(8...) custom-call(bf16[128,1536]{1,0:T(8,128)(2,1)S(1)} %get-tuple-element, ...), custom_call_target="tpu_custom_call" | custom-call | flops 1 | bytes 1 | tf_op jit(solution)/shard_map/ffn_backward/pallas_call | solution.py:534
  237.8 4.9 %convolution_convert_fusion = bf16[1536,1024]{1,0:T(8,128)(2,1)} fusion(bf16[1024,1536]{1,0:T(8,128)(2,1)S(1)} %copy-done.44, bf16[1024,1024]{1,0:T(8,128)(2,1)S(1)} %get-tuple-element.264), kind=kOutput, calls=%fused_computation | convolution fusion | flops 3222798336 | bytes 8388608 | tf_op jit(solution)/shard_map/dot_general | solution.py:52
  246.3 5.8 %convolution_convert_fusion.1 = bf16[512,1536]{1,0:T(8,128)(2,1)} fusion(bf16[1024,512]{1,0:T(8,128)(2,1)} %get-tuple-element.260, bf16[1024,1536]{1,0:T(8,128)(2,1)} %copy-done.8), kind=kOutput, calls=%fused_computation.1 | convolution fusion | flops 1611399168 | bytes 5767168 | tf_op jit(solution)/shard_map/dot_general | solution.py:52
  255.0 8.6 %collective-permute-done.52.refs_2_ = bf16[128,1536]{1,0:T(8,128)(2,1)} collective-permute-done((bf16[128,1536]{1,0:T(8,128)(2,1)}, bf16[128,1536]{1,0:T(8,128)(2,1)}, u32[]{:S(2)}, u32[]{:S(2)}) %collective-permute-start.52) | collective-permute-done | bytes 393248 | tf_op jit(solution)/shard_map/ppermute | solution.py:67
  263.6 5.2 %middle_backward.1 = (f32[128,1536]{1,0:T(8,128)S(1)}, bf16[128,1536]{1,0:T(8,128)(2,1)S(1)}, f32[1,1536]{1,0:T(1,128)S(1)}, bf16[128,384]{1,0:T(8,128)(2,1)S(1)...) custom-call(s32[1]{0:T(128)} %bitcast.me_ref.info_ref, ...), custom_call_target="tpu_custom_call" | custom-call | flops 1 | bytes 1 | tf_op jit(solution)/shard_map/middle_backward/pallas_call | solution.py:804
  286.2 13.0 %attention_backward.1 = (bf16[1024,384]{1,0:T(8,128)(2,1)S(1)}, f32[8,1536]{1,0:T(8,128)S(1)}, bf16[128,1536]{1,0:T(8,128)(2,1)S(1)}, bf16[128,1536]{1,0:T(8,128...) custom-call(s32[2]{0:T(128)S(1)} %pad_add_fusion.2.info_ref, ...), custom_call_target="tpu_custom_call" | custom-call | flops 1 | bytes 1 | tf_op jit(solution)/shard_map/attention_backward/pallas_call | solution.py:398
  299.3 12.6 %collective-permute-done.58.refs_4_ = bf16[192,1536]{1,0:T(8,128)(2,1)S(1)} collective-permute-done((bf16[192,1536]{1,0:T(8,128)(2,1)S(1)}, bf16[192,1536]{1,0:T(8,128)(2,1)S(1)}, u32[]{:S(2)}, u32[]{:S(2)}) %collective-permute-start.58) | collective-permute-done | bytes 589856 | tf_op jit(solution)/shard_map/ppermute | solution.py:67
  311.9 6.2 %attention_packs.1 = bf16[2368,384]{1,0:T(8,128)(2,1)} custom-call(s32[1]{0:T(128)} %bitcast.1.info_ref, bf16[1024,1536]{1,0:T(8,128)(2,1)} %get-tuple-element.211.refs_14_.refs_0_, bf16[1024,384]{1,0:T(8,128)(2,1)S(1)} %get-tuple-element.299.refs_1_, f32[192,1536]{1,0:T(8,128)S(1)} %convert_add_fusion.refs_2_, ...), custom_call_target="tpu_custom_call" | custom-call | flops 1 | bytes 1 | tf_op jit(solution)/shard_map/attention_packs/pallas_call | solution.py:927
  328.1 22.3 %collective-permute-done.74 = bf16[128,1536]{1,0:T(8,128)(2,1)S(1)} collective-permute-done((bf16[128,1536]{1,0:T(8,128)(2,1)S(1)}, bf16[128,1536]{1,0:T(8,128)(2,1)S(1)}, u32[]{:S(2)}, u32[]{:S(2)}) %collective-permute-start.74) | collective-permute-done | bytes 393248 | tf_op jit(solution)/shard_map/ppermute | solution.py:67
  350.4 7.0 %collective-permute-done.75 = bf16[128,1536]{1,0:T(8,128)(2,1)S(1)} collective-permute-done((bf16[128,1536]{1,0:T(8,128)(2,1)}, bf16[128,1536]{1,0:T(8,128)(2,1)S(1)}, u32[]{:S(2)}, u32[]{:S(2)}) %collective-permute-start.75) | collective-permute-done | bytes 393248 | tf_op jit(solution)/shard_map/ppermute | solution.py:67
  366.3 5.3 %collective-permute-done.81.refs_2_ = bf16[128,1536]{1,0:T(8,128)(2,1)S(1)} collective-permute-done((bf16[128,1536]{1,0:T(8,128)(2,1)}, bf16[128,1536]{1,0:T(8,128)(2,1)S(1)}, u32[]{:S(2)}, u32[]{:S(2)}) %collective-permute-start.81) | collective-permute-done | bytes 393248 | tf_op jit(solution)/shard_map/ppermute | solution.py:67
  371.5 9.0 %collective-permute-done.82.refs_4_ = bf16[128,1536]{1,0:T(8,128)(2,1)S(1)} collective-permute-done((bf16[128,1536]{1,0:T(8,128)(2,1)}, bf16[128,1536]{1,0:T(8,128)(2,1)S(1)}, u32[]{:S(2)}, u32[]{:S(2)}) %collective-permute-start.82) | collective-permute-done | bytes 393248 | tf_op jit(solution)/shard_map/ppermute | solution.py:67
  381.1 5.8 %collective-permute-done.79.refs_6_ = bf16[192,1024]{1,0:T(8,128)(2,1)} collective-permute-done((bf16[192,1024]{1,0:T(8,128)(2,1)S(1)}, bf16[192,1024]{1,0:T(8,128)(2,1)}, u32[]{:S(2)}, u32[]{:S(2)}) %collective-permute-start.79) | collective-permute-done | bytes 393248 | tf_op jit(solution)/shard_map/ppermute | solution.py:67
  396.3 3.9 row_grads.1
  400.4 7.1 %column_grads.1 = (f32[384,4096]{1,0:T(8,128)}, f32[384,4096]{1,0:T(8,128)}) custom-call(s32[1]{0:T(128)} %bitcast.me_ref.info_ref, bf16[384,1024]{1,0:T(8,128)(2,1)} %reduce-scatter.8.cloned.1.call-done.refs_0_, bf16[384,1024]{1,0:T(8,128)(2,1)} %collective-permute-done.90.refs_1_, bf16[384,1024]{1,0:T(8,128)(2,1)} %copy-done.11, ...), custom_call_target="tpu_custom_call" | custom-call | flops 1 | bytes 1 | tf_op jit(solution)/shard_map/column_grads/pallas_call | solution.py:631
  407.5 7.8 %collective-permute-done.88.refs_4_ = bf16[592,384]{1,0:T(8,128)(2,1)S(1)} collective-permute-done((bf16[592,384]{1,0:T(8,128)(2,1)}, bf16[592,384]{1,0:T(8,128)(2,1)S(1)}, u32[]{:S(2)}, u32[]{:S(2)}) %collective-permute-start.88) | collective-permute-done | bytes 454688 | tf_op jit(solution)/shard_map/ppermute | solution.py:67
  419.6 8.1 %attention_grads.1 = (f32[384,1536]{1,0:T(8,128)}, f32[384,768]{1,0:T(8,128)}, f32[384,768]{1,0:T(8,128)}, f32[384,1536]{1,0:T(8,128)}, f32[8,384]{1,0:T(8,128)S(1)}, /*index=5*/f32[1,1]{1,0:T(1,128)}) custom-call(s32[1]{0:T(128)} %bitcast.me_ref.info_ref, bf16[592,384]{1,0:T(8,128)(2,1)} %reduce-scatter.4.cloned.1.call-done.refs_0_, ...), custom_call_target="tpu_custom_call" | custom-call | flops 1 | bytes 1 | tf_op jit(solution)/shard_map/attention_grads/pallas_call | solution.py:1011
  (346 shorter events, 139.3 us)
Async XLA Ops:
  7.2 119.9 %all-gather.5.cloned.1.call-start = ((), (), s32[]{:S(2)}) async-start(), calls=%async_computation.4 | async-start | bytes 1966080 | tf_op jit(solution)/shard_map/all_gather | solution.py:1122
  24.7 23.5 %collective-permute-start.7 = (bf16[576,384]{1,0:T(8,128)(2,1)S(1)}, bf16[576,384]{1,0:T(8,128)(2,1)S(1)}, u32[]{:S(2)}, u32[]{:S(2)}) collective-permute-start(bf16[576,384]{1,0:T(8,128)(2,1)S(1)} %dynamic-slice_dynamic-update-slice_fusion.refs_8_), channel_id=1, source_target_pairs={{0,1},{1,0},{2,3},{3,2},{4,5},{5,4},{6,7},{7,6},{8,9},{9,8},{10,11... | collective-permute-start | bytes 1327112 | tf_op jit(solution)/shard_map/ppermute | solution.py:67
  24.7 33.2 %collective-permute-start.8 = (bf16[576,384]{1,0:T(8,128)(2,1)S(1)}, bf16[576,384]{1,0:T(8,128)(2,1)}, u32[]{:S(2)}, u32[]{:S(2)}) collective-permute-start(bf16[576,384]{1,0:T(8,128)(2,1)S(1)} %dynamic-slice_dynamic-update-slice_fusion.refs_8_), channel_id=1, source_target_pairs={{0,2},{1,3},{2,0},{3,1},{4,6},{5,7},{6,4},{7,5},{8,10},{9,11},{10,... | collective-permute-start | bytes 1327112 | tf_op jit(solution)/shard_map/ppermute | solution.py:67
  27.8 30.2 %collective-permute-start.9 = (bf16[576,384]{1,0:T(8,128)(2,1)S(1)}, bf16[576,384]{1,0:T(8,128)(2,1)S(1)}, u32[]{:S(2)}, u32[]{:S(2)}) collective-permute-start(bf16[576,384]{1,0:T(8,128)(2,1)S(1)} %dynamic-slice_dynamic-update-slice_fusion.refs_8_), channel_id=1, source_target_pairs={{0,3},{1,2},{2,1},{3,0},{4,7},{5,6},{6,5},{7,4},{8,11},{9,10},{10,... | collective-permute-start | bytes 1327112 | tf_op jit(solution)/shard_map/ppermute | solution.py:67
  58.8 107.1 %all-gather.3.cloned.1.call-start = ((), (), s32[]{:S(2)}) async-start(), calls=%async_computation.3 | async-start | bytes 3932160 | tf_op jit(solution)/shard_map/all_gather | solution.py:1121
  59.5 261.9 %reduce-scatter.8.cloned.1.call-start = ((), (), s32[]{:S(2)}) async-start(), calls=%async_computation.7 | async-start | bytes 3932160 | tf_op jit(solution)/shard_map/reduce_scatter | solution.py:1154
  63.8 20.4 %collective-permute-start.15 = (bf16[576,384]{1,0:T(8,128)(2,1)S(1)}, bf16[576,384]{1,0:T(8,128)(2,1)S(1)}, u32[]{:S(2)}, u32[]{:S(2)}) collective-permute-start(bf16[576,384]{1,0:T(8,128)(2,1)S(1)} %pad_maximum_fusion.refs_8_), channel_id=1, source_target_pairs={{0,16},{4,20},{8,24},{12,28},{16,0},{20,4},{24,8},{28,12},{1,17},{... | collective-permute-start | bytes 1327112 | tf_op jit(solution)/shard_map/ppermute | solution.py:67
  65.4 20.5 %collective-permute-start.16 = (bf16[576,384]{1,0:T(8,128)(2,1)S(1)}, bf16[576,384]{1,0:T(8,128)(2,1)S(1)}, u32[]{:S(2)}, u32[]{:S(2)}) collective-permute-start(bf16[576,384]{1,0:T(8,128)(2,1)S(1)} %pad_maximum_fusion.refs_8_), channel_id=1, source_target_pairs={{0,24},{4,28},{8,16},{12,20},{16,8},{20,12},{24,0},{28,4},{1,25},{... | collective-permute-start | bytes 1327112 | tf_op jit(solution)/shard_map/ppermute | solution.py:67
  68.5 17.9 %collective-permute-start.13 = (bf16[576,384]{1,0:T(8,128)(2,1)S(1)}, bf16[576,384]{1,0:T(8,128)(2,1)S(1)}, u32[]{:S(2)}, u32[]{:S(2)}) collective-permute-start(bf16[576,384]{1,0:T(8,128)(2,1)S(1)} %pad_maximum_fusion.refs_8_), channel_id=1, source_target_pairs={{0,4},{4,0},{8,12},{12,8},{16,20},{20,16},{24,28},{28,24},{1,5},{5... | collective-permute-start | bytes 1327112 | tf_op jit(solution)/shard_map/ppermute | solution.py:67
  105.9 17.7 %collective-permute-start.30 = (bf16[128,1536]{1,0:T(8,128)(2,1)S(1)}, bf16[128,1536]{1,0:T(8,128)(2,1)S(1)}, u32[]{:S(2)}, u32[]{:S(2)}) collective-permute-start(bf16[128,1536]{1,0:T(8,128)(2,1)S(1)} %get-tuple-element.231.refs_0_), channel_id=1, source_target_pairs={{0,16},{4,20},{8,24},{12,28},{16,0},{20,4},{24,8},{28,12},{1,17},{... | collective-permute-start | bytes 1179656 | tf_op jit(solution)/shard_map/ppermute | solution.py:67
  106.7 18.5 %collective-permute-start.32 = (bf16[128,1536]{1,0:T(8,128)(2,1)S(1)}, bf16[128,1536]{1,0:T(8,128)(2,1)S(1)}, u32[]{:S(2)}, u32[]{:S(2)}) collective-permute-start(bf16[128,1536]{1,0:T(8,128)(2,1)S(1)} %get-tuple-element.231.refs_0_), channel_id=1, source_target_pairs={{0,24},{4,28},{8,16},{12,20},{16,8},{20,12},{24,0},{28,4},{1,25},{... | collective-permute-start | bytes 1179656 | tf_op jit(solution)/shard_map/ppermute | solution.py:67
  180.4 19.5 %collective-permute-start.38 = (bf16[128,1536]{1,0:T(8,128)(2,1)}, bf16[128,1536]{1,0:T(8,128)(2,1)S(1)}, u32[]{:S(2)}, u32[]{:S(2)}) collective-permute-start(bf16[128,1536]{1,0:T(8,128)(2,1)} %add_convert_fusion.10), channel_id=1, source_target_pairs={{0,16},{4,20},{8,24},{12,28},{16,0},{20,4},{24,8},{28,12},{1,17},{... | collective-permute-start | bytes 1179656 | tf_op jit(solution)/shard_map/ppermute | solution.py:67
  206.0 17.3 %collective-permute-start.46 = (bf16[128,1536]{1,0:T(8,128)(2,1)S(1)}, bf16[128,1536]{1,0:T(8,128)(2,1)S(1)}, u32[]{:S(2)}, u32[]{:S(2)}) collective-permute-start(bf16[128,1536]{1,0:T(8,128)(2,1)S(1)} %get-tuple-element.368.refs_0_), channel_id=1, source_target_pairs={{0,24},{4,28},{8,16},{12,20},{16,8},{20,12},{24,0},{28,4},{1,25},{... | collective-permute-start | bytes 1179656 | tf_op jit(solution)/shard_map/ppermute | solution.py:67
  242.7 116.4 %reduce-scatter.6.cloned.1.call-start = ((), (), s32[]{:S(2)}) async-start(), calls=%async_computation.6 | async-start | bytes 1966080 | tf_op jit(solution)/shard_map/reduce_scatter | solution.py:1155
  244.0 19.6 %collective-permute-start.52 = (bf16[128,1536]{1,0:T(8,128)(2,1)}, bf16[128,1536]{1,0:T(8,128)(2,1)}, u32[]{:S(2)}, u32[]{:S(2)}) collective-permute-start(bf16[128,1536]{1,0:T(8,128)(2,1)} %add_convert_fusion.7), channel_id=1, source_target_pairs={{0,16},{4,20},{8,24},{12,28},{16,0},{20,4},{24,8},{28,12},{1,17},{... | collective-permute-start | bytes 1179656 | tf_op jit(solution)/shard_map/ppermute | solution.py:67
  245.7 17.9 %collective-permute-start.50 = (bf16[128,1536]{1,0:T(8,128)(2,1)}, bf16[128,1536]{1,0:T(8,128)(2,1)}, u32[]{:S(2)}, u32[]{:S(2)}) collective-permute-start(bf16[128,1536]{1,0:T(8,128)(2,1)} %add_convert_fusion.8), channel_id=1, source_target_pairs={{0,24},{4,28},{8,16},{12,20},{16,8},{20,12},{24,0},{28,4},{1,25},{... | collective-permute-start | bytes 1179656 | tf_op jit(solution)/shard_map/ppermute | solution.py:67
  252.1 139.2 %reduce-scatter.4.cloned.1.call-start = ((), (), s32[]{:S(2)}) async-start(), calls=%async_computation.5 | async-start | bytes 2273280 | tf_op jit(solution)/shard_map/reduce_scatter | solution.py:1174
  283.4 28.5 %collective-permute-start.58 = (bf16[192,1536]{1,0:T(8,128)(2,1)S(1)}, bf16[192,1536]{1,0:T(8,128)(2,1)S(1)}, u32[]{:S(2)}, u32[]{:S(2)}) collective-permute-start(bf16[192,1536]{1,0:T(8,128)(2,1)S(1)} %add_convert_fusion.1), channel_id=1, source_target_pairs={{0,16},{4,20},{8,24},{12,28},{16,0},{20,4},{24,8},{28,12},{1,17},{... | collective-permute-start | bytes 1769480 | tf_op jit(solution)/shard_map/ppermute | solution.py:67
  285.7 26.2 %collective-permute-start.56 = (bf16[192,1536]{1,0:T(8,128)(2,1)S(1)}, bf16[192,1536]{1,0:T(8,128)(2,1)S(1)}, u32[]{:S(2)}, u32[]{:S(2)}) collective-permute-start(bf16[192,1536]{1,0:T(8,128)(2,1)S(1)} %add_convert_fusion.2), channel_id=1, source_target_pairs={{0,24},{4,28},{8,16},{12,20},{16,8},{20,12},{24,0},{28,4},{1,25},{... | collective-permute-start | bytes 1769480 | tf_op jit(solution)/shard_map/ppermute | solution.py:67
  299.2 19.5 %collective-permute-start.73 = (bf16[128,1536]{1,0:T(8,128)(2,1)}, bf16[128,1536]{1,0:T(8,128)(2,1)}, u32[]{:S(2)}, u32[]{:S(2)}) collective-permute-start(bf16[128,1536]{1,0:T(8,128)(2,1)} %get-tuple-element.310), channel_id=1, source_target_pairs={{0,4},{4,0},{8,12},{12,8},{16,20},{20,16},{24,28},{28,24},{1,5},{5... | collective-permute-start | bytes 1179656 | tf_op jit(solution)/shard_map/ppermute | solution.py:67
  321.4 37.8 %collective-permute-start.77 = (bf16[384,1024]{1,0:T(8,128)(2,1)}, bf16[384,1024]{1,0:T(8,128)(2,1)S(1)}, u32[]{:S(2)}, u32[]{:S(2)}) collective-permute-start(bf16[384,1024]{1,0:T(8,128)(2,1)} %reduce-scatter.8.cloned.1.call-done.refs_0_), channel_id=1, source_target_pairs={{0,8},{4,12},{8,0},{12,4},{16,24},{20,28},{24,16},{28,20},{1,9},{5... | collective-permute-start | bytes 2359304 | tf_op jit(solution)/shard_map/ppermute | solution.py:67
  322.8 36.3 %collective-permute-start.78 = (bf16[384,1024]{1,0:T(8,128)(2,1)}, bf16[384,1024]{1,0:T(8,128)(2,1)}, u32[]{:S(2)}, u32[]{:S(2)}) collective-permute-start(bf16[384,1024]{1,0:T(8,128)(2,1)} %reduce-scatter.8.cloned.1.call-done.refs_0_), channel_id=1, source_target_pairs={{0,16},{4,20},{8,24},{12,28},{16,0},{20,4},{24,8},{28,12},{1,17},{... | collective-permute-start | bytes 2359304 | tf_op jit(solution)/shard_map/ppermute | solution.py:67
  324.6 25.8 %collective-permute-start.74 = (bf16[128,1536]{1,0:T(8,128)(2,1)S(1)}, bf16[128,1536]{1,0:T(8,128)(2,1)S(1)}, u32[]{:S(2)}, u32[]{:S(2)}) collective-permute-start(bf16[128,1536]{1,0:T(8,128)(2,1)S(1)} %add_convert_fusion.5), channel_id=1, source_target_pairs={{0,8},{4,12},{8,0},{12,4},{16,24},{20,28},{24,16},{28,20},{1,9},{5... | collective-permute-start | bytes 1179656 | tf_op jit(solution)/shard_map/ppermute | solution.py:67
  326.3 31.2 %collective-permute-start.75 = (bf16[128,1536]{1,0:T(8,128)(2,1)}, bf16[128,1536]{1,0:T(8,128)(2,1)S(1)}, u32[]{:S(2)}, u32[]{:S(2)}) collective-permute-start(bf16[128,1536]{1,0:T(8,128)(2,1)} %add_convert_fusion.4), channel_id=1, source_target_pairs={{0,16},{4,20},{8,24},{12,28},{16,0},{20,4},{24,8},{28,12},{1,17},{... | collective-permute-start | bytes 1179656 | tf_op jit(solution)/shard_map/ppermute | solution.py:67
  326.6 32.5 %collective-permute-start.76 = (bf16[128,1536]{1,0:T(8,128)(2,1)}, bf16[128,1536]{1,0:T(8,128)(2,1)S(1)}, u32[]{:S(2)}, u32[]{:S(2)}) collective-permute-start(bf16[128,1536]{1,0:T(8,128)(2,1)} %add_convert_fusion.3), channel_id=1, source_target_pairs={{0,24},{4,28},{8,16},{12,20},{16,8},{20,12},{24,0},{28,4},{1,25},{... | collective-permute-start | bytes 1179656 | tf_op jit(solution)/shard_map/ppermute | solution.py:67
  359.9 20.7 %collective-permute-start.82 = (bf16[128,1536]{1,0:T(8,128)(2,1)}, bf16[128,1536]{1,0:T(8,128)(2,1)S(1)}, u32[]{:S(2)}, u32[]{:S(2)}) collective-permute-start(bf16[128,1536]{1,0:T(8,128)(2,1)} %reduce-scatter.6.cloned.1.call-done.refs_0_), channel_id=1, source_target_pairs={{0,16},{4,20},{8,24},{12,28},{16,0},{20,4},{24,8},{28,12},{1,17},{... | collective-permute-start | bytes 1179656 | tf_op jit(solution)/shard_map/ppermute | solution.py:67
  361.6 19.0 %collective-permute-start.83 = (bf16[128,1536]{1,0:T(8,128)(2,1)}, bf16[128,1536]{1,0:T(8,128)(2,1)S(1)}, u32[]{:S(2)}, u32[]{:S(2)}) collective-permute-start(bf16[128,1536]{1,0:T(8,128)(2,1)} %reduce-scatter.6.cloned.1.call-done.refs_0_), channel_id=1, source_target_pairs={{0,24},{4,28},{8,16},{12,20},{16,8},{20,12},{24,0},{28,4},{1,25},{... | collective-permute-start | bytes 1179656 | tf_op jit(solution)/shard_map/ppermute | solution.py:67
  362.8 24.2 %collective-permute-start.79 = (bf16[192,1024]{1,0:T(8,128)(2,1)S(1)}, bf16[192,1024]{1,0:T(8,128)(2,1)}, u32[]{:S(2)}, u32[]{:S(2)}) collective-permute-start(bf16[192,1024]{1,0:T(8,128)(2,1)S(1)} %slice.52), channel_id=1, source_target_pairs={{0,16},{4,20},{8,24},{12,28},{16,0},{20,4},{24,8},{28,12},{1,17},{... | collective-permute-start | bytes 1179656 | tf_op jit(solution)/shard_map/ppermute | solution.py:67
  364.5 22.4 %collective-permute-start.80 = (bf16[192,1024]{1,0:T(8,128)(2,1)S(1)}, bf16[192,1024]{1,0:T(8,128)(2,1)}, u32[]{:S(2)}, u32[]{:S(2)}) collective-permute-start(bf16[192,1024]{1,0:T(8,128)(2,1)S(1)} %slice.53), channel_id=1, source_target_pairs={{0,8},{4,12},{8,0},{12,4},{16,24},{20,28},{24,16},{28,20},{1,9},{5... | collective-permute-start | bytes 1179656 | tf_op jit(solution)/shard_map/ppermute | solution.py:67
  392.9 22.4 %collective-permute-start.88 = (bf16[592,384]{1,0:T(8,128)(2,1)}, bf16[592,384]{1,0:T(8,128)(2,1)S(1)}, u32[]{:S(2)}, u32[]{:S(2)}) collective-permute-start(bf16[592,384]{1,0:T(8,128)(2,1)} %reduce-scatter.4.cloned.1.call-done.refs_0_), channel_id=1, source_target_pairs={{0,16},{4,20},{8,24},{12,28},{16,0},{20,4},{24,8},{28,12},{1,17},{... | collective-permute-start | bytes 1363976 | tf_op jit(solution)/shard_map/ppermute | solution.py:67
  393.3 21.9 %collective-permute-start.89 = (bf16[592,384]{1,0:T(8,128)(2,1)}, bf16[592,384]{1,0:T(8,128)(2,1)S(1)}, u32[]{:S(2)}, u32[]{:S(2)}) collective-permute-start(bf16[592,384]{1,0:T(8,128)(2,1)} %reduce-scatter.4.cloned.1.call-done.refs_0_), channel_id=1, source_target_pairs={{0,24},{4,28},{8,16},{12,20},{16,8},{20,12},{24,0},{28,4},{1,25},{... | collective-permute-start | bytes 1363976 | tf_op jit(solution)/shard_map/ppermute | solution.py:67
  400.3 18.1 %collective-permute-start.69 = (bf16[592,384]{1,0:T(8,128)(2,1)S(1)}, bf16[592,384]{1,0:T(8,128)(2,1)S(1)}, u32[]{:S(2)}, u32[]{:S(2)}) collective-permute-start(bf16[592,384]{1,0:T(8,128)(2,1)S(1)} %copy-done.17), channel_id=1, source_target_pairs={{0,4},{4,0},{8,12},{12,8},{16,20},{20,16},{24,28},{28,24},{1,5},{5... | collective-permute-start | bytes 1363976 | tf_op jit(solution)/shard_map/ppermute | solution.py:67
  (118 other events, 1038.7 us)
Sparse Core Ops, SparseCore 0:
  58.9 42.4 all-gather.4
  103.5 62.3 all-gather.2
  242.8 58.8 reduce-scatter.7
  304.4 35.3 reduce-scatter.5
  342.5 38.2 reduce-scatter.3
where the time goes:
time: 440 us; the launch traced here: 435 us
  waiting for transfers between devices  221 us (50%)
  Pallas kernels  80.8 us (18%)
  starting transfers between devices  66.2 us (15%)
  other arithmetic  25.8 us (6%)
  between operations  15.7 us (4%)
  local copies, waits for them, and re-layouts  14.9 us (3%)
  matrix products  10.6 us (2%)
    ppermute x99, waiting for transfers between devices, partner(): lax.ppermute(x, axis, [(i, i ^ mask) for i in range(lax.axis_size(axis))])  182 us
    ppermute x99, starting transfers between devices, partner(): lax.ppermute(x, axis, [(i, i ^ mask) for i in range(lax.axis_size(axis))])  65.3 us
    all_gather x1, waiting for transfers between devices, local(): gate_up = lax.all_gather(gate_up_own, 'fsdp', axis=0, tiled=True)  38.8 us
    pallas_call x1, Pallas kernels, attention_backward(): pl.pallas_call(functools.partial(attention_backward_kernel, C, tokens, q_...  13 us
    pallas_call x1, Pallas kernels, attention_forward(): pl.pallas_call(functools.partial(attention_forward_kernel, C, Z, tokens,...  11.2 us
    dot_general x2, matrix products, transposed_times(): lax.dot_general(left, right, (((0,), (0,)), ((), ())), preferred_element_...  10.6 us
    pallas_call x1, Pallas kernels, ffn_forward(): pl.pallas_call(functools.partial(ffn_forward_kernel, C, cuts), out_shape=...  9.6 us
    unnamed x95, local copies, waits for them, and re-layouts  9.45 us
  transfers between devices with their start and end apart: 104, of which 46 were waited for; matrix products, arithmetic and copies ran while one was open for 8% of the time, Pallas kernels for 13%

commit v1 on v0

--- a/solution.py
+++ b/solution.py
@@ -87,12 +87,12 @@
 
 
 def far_sends(near):
-    half = near[0].shape[0] // 2
+    half = near[0].shape[0] // 32 * 16
     return [partner(near[0][:half], "ctx", 4), partner(near[1][half:], "ctx", 2)]
 
 
 def square_pieces(x, near, far):
-    half = x.shape[0] // 2
+    half = x.shape[0] // 32 * 16
     mine = [(0, 0, x), (1, 0, near[0]), (2, 0, near[1]), (3, 0, far[0]), (3, half, far[1])]
     other = together([partner(block, "ctx", 1) for _, _, block in mine])
     pieces = []
@@ -304,12 +304,12 @@
     R = C // 2
     mine_refs, other_refs = refs[:R], refs[R:C]
     hbm_refs = refs[C : C + 7]
-    dqkv_ref, gain_ref = refs[C + 7 : C + 9]
+    grad_w_ref, gain_ref = refs[C + 7 : C + 9]
     keep_refs = refs[C + 9 : C + 9 + R]
     give_refs = refs[C + 9 + R : C + 9 + C]
     refs = refs[C + 9 + C :]
     qkv_ref, att_ref, lse_ref, cos_ref, sin_ref, w_ref, n_all_ref = refs[:7]
-    wide_ref, grad_ref, dq_ref, dkv_ref, sems = refs[7:]
+    wide_ref, grad_ref, dq_ref, dkv_ref, dqkv_ref, sems = refs[7:]
     copies = started(sems, 0, *zip(hbm_refs, refs[:7], strict=True))
     me, length = info_ref[0], info_ref[1]
     core = me % 2
@@ -384,6 +384,12 @@
         return part
 
     parts_of(rows_of, keep_refs, give_refs)
+    step = 3 * LANES
+
+    @pl.loop(0, grad_w_ref.shape[0] // step)
+    def _(n):
+        at = pl.ds(pl.multiple_of(n * step, step), step)
+        grad_w_ref[at, :] = transposed_times(n_all_ref[:, at], dqkv_ref[...]).astype(bf16)
 
 
 def attention_backward(mine, other, saved, tables, me, length, q_heads, kv_heads):
@@ -398,7 +404,7 @@
     result = pl.pallas_call(
         functools.partial(attention_backward_kernel, C, tokens, q_heads, kv_heads, 2 * tokens),
         out_shape=[
-            jax.ShapeDtypeStruct((seq, cols), bf16),
+            jax.ShapeDtypeStruct((width, cols), bf16),
             jax.ShapeDtypeStruct((8, width), f32),
         ]
         + [part] * C,
@@ -410,9 +416,10 @@
             pltpu.VMEM((seq, q_heads * LANES), bf16),
             pltpu.VMEM((seq, q_heads * LANES), f32),
             pltpu.VMEM((seq, 2 * kv_heads * LANES), f32),
+            pltpu.VMEM((seq, cols), bf16),
             pltpu.SemaphoreType.DMA((7,)),
         ],
-        compiler_params=pltpu.CompilerParams(vmem_limit_bytes=26 * MIB),
+        compiler_params=pltpu.CompilerParams(vmem_limit_bytes=28 * MIB),
         cost_estimate=cost(seq * width * cols + 4 * seq * seq * heads * LANES, 3 * seq * width),
         name="attention_backward",
     )(jnp.stack([me, length]).astype(jnp.int32), *mine, *other, *in_hbm(*loaded))
@@ -697,14 +704,10 @@
     here = started(sems, 1, (own_hbm, out_ref.at[own_at, :]))
     core = me % 2
     tokens, half = hidden_ref.shape[0], mine_refs[0].shape[1]
-    cols = w_refs[0].shape[1]
-    strips = out_ref.shape[1] // cols
     for i in range(C):
         for j in range(1, Z):
             at = pl.multiple_of((line ^ j) * rows_z + (me ^ i) * piece, piece)
-            for c in range(strips):
-                first = ((j - 1) * strips + c) * piece
-                out_ref[pl.ds(at, piece), c * cols : (c + 1) * cols] = w_refs[i][first : first + piece, :]
+            out_ref[pl.ds(at, piece), :] = w_refs[i][(j - 1) * piece : j * piece, :]
     for copy in here:
         copy.wait()
     saved = started(sems, 0, (out_ref, out_hbm))
@@ -729,12 +732,9 @@
     C = len(w_blocks)
     tokens, width = hidden.shape
     half = mine[0].shape[1]
-    cols = w_blocks[0].shape[1]
-    strips = width // cols
     piece = w_own.shape[0] // C
     if piece % 16 or (2 * half) % LANES:
-        rows = [x.reshape(Z - 1, strips, piece, cols).transpose(0, 2, 1, 3) for x in w_blocks]
-        rows = jnp.stack(unsort([x.reshape(Z - 1, piece, width) for x in rows], me), axis=1)
+        rows = jnp.stack(unsort([x.reshape(Z - 1, piece, width) for x in w_blocks], me), axis=1)
         rows = jnp.concatenate([w_own[None], rows.reshape(Z - 1, C * piece, width)])
         out_all = jnp.concatenate([pick(rows, line ^ j) for j in range(Z)], axis=0)
         heads = []
@@ -860,11 +860,11 @@
 
 def attention_packs_kernel(Z, C, info_ref, *refs):
     R = C // 2
-    n_hbm, dqkv_ref, out_refs = refs[0], refs[1], refs[2 : R + 2]
-    gain_one_ref, gain_two_ref, error_ref, pack_hbm = refs[R + 2 : R + 6]
-    n_ref, sum_ref, tall_ref, sems = refs[R + 6 :]
-    arriving = started(sems, 0, (n_hbm, n_ref))
-    width, cols = n_ref.shape[1], tall_ref.shape[1]
+    grad_ref, out_refs = refs[0], refs[1 : R + 1]
+    gain_one_ref, gain_two_ref, error_ref, pack_hbm, token_ref = refs[R + 1 : R + 6]
+    sum_ref, tall_ref, sems = refs[R + 6 :]
+    token_ref[...] = jnp.zeros_like(token_ref)
+    width, cols = grad_ref.shape
     rows, tall = width // Z, tall_ref.shape[0] // Z
     piece = sum_ref.shape[0] // Z
     out = out_refs[0][...]
@@ -888,27 +888,24 @@
         extra = jnp.where(row == 0, gain_one_ref[0:1, at], jnp.where(row == 1, gain_two_ref[0:1, at], 0.0))
         extra = jnp.where(row == 2, error, extra)
         tall_ref[(j + 1) * tall - EXTRA : (j + 1) * tall, :] = extra.astype(bf16)
-    for copy in arriving:
-        copy.wait()
-
-    @pl.loop(0, Z)
-    def _(j):
-        at = pl.ds(pl.multiple_of(j * rows, LANES), rows)
-        to = pl.ds(pl.multiple_of(j * tall, 16), rows)
-        tall_ref[to, :] = transposed_times(n_ref[:, at], dqkv_ref[...]).astype(bf16)
+
+    @pl.loop(0, rows // 16)
+    def _(n):
+        for j in range(Z):
+            at = pl.ds(pl.multiple_of(j * rows + n * 16, 16), 16)
+            to = pl.ds(pl.multiple_of(j * tall + n * 16, 16), 16)
+            tall_ref[to, :] = grad_ref[at, :]
 
     for copy in started(sems, 0, (tall_ref, pack_hbm)):
         copy.wait()
 
 
-def attention_packs(normed_all, grad_qkv, out_parts, gain_one, gain_two, error, line, Z, C):
-    width = normed_all.shape[1]
-    cols = grad_qkv.shape[1]
+def attention_packs(grad, out_parts, gain_one, gain_two, error, line, Z, C):
+    width, cols = grad.shape
     rows = width // Z
     tall, parts = out_parts[0].shape[0], C // 2
     piece = tall // Z
     if rows != cols or piece % 16:
-        grad = transposed_times(normed_all, grad_qkv).astype(bf16)
         grad_out = total(out_parts[0], out_parts[1:]).astype(bf16)
         lane = jnp.arange(cols, dtype=jnp.int32)
         high = error.astype(bf16)
@@ -922,70 +919,69 @@
             gains = [jnp.pad(x[at].astype(bf16), (0, cols - rows)) for x in (gain_one[0], gain_two[0])]
             extra = jnp.pad(jnp.stack([*gains, error_row]), ((0, EXTRA - 3), (0, 0)))
             packs += [grad[at], *[out[:, c : c + cols] for c in range(0, width, cols)], extra]
-        return jnp.concatenate(packs, axis=0)
+        return jnp.concatenate(packs, axis=0), jnp.zeros((8, LANES), f32)
     shape = (Z * (rows + piece * width // cols + EXTRA), cols)
     return pl.pallas_call(
         functools.partial(attention_packs_kernel, Z, C),
-        out_shape=pltpu.HBM(shape, bf16),
-        in_specs=[SMEM, HBM] + [VMEM] * (parts + 4),
-        out_specs=HBM,
+        out_shape=[pltpu.HBM(shape, bf16), jax.ShapeDtypeStruct((8, LANES), f32)],
+        in_specs=[SMEM] + [VMEM] * (parts + 4),
+        out_specs=[HBM, VMEM],
         scratch_shapes=[
-            pltpu.VMEM(normed_all.shape, bf16),
             pltpu.VMEM((tall, width), bf16),
             pltpu.VMEM(shape, bf16),
             pltpu.SemaphoreType.DMA((1,)),
         ],
         compiler_params=pltpu.CompilerParams(vmem_limit_bytes=16 * MIB),
-        cost_estimate=cost(normed_all.shape[0] * width * cols, 3 * width * width),
+        cost_estimate=cost(0, 3 * width * width),
         name="attention_packs",
-    )(line.reshape(1), *in_hbm(normed_all), grad_qkv, *out_parts, gain_one, gain_two, error.reshape(1, 1))
+    )(line.reshape(1), grad, *out_parts, gain_one, gain_two, error.reshape(1, 1))
 
 
 def attention_grads_kernel(C, rows, q_cols, kv_cols, places, me_ref, *refs):
     count = len(places)
     gain_ref, valid_ref = refs[count : count + 2]
-    query_ref, key_ref, value_ref, out_ref, gains_ref, loss_ref = refs[count + 2 : count + 8]
-    low_ref, sort_ref, extra_ref, in_sems = refs[count + 8 :]
+    *grads_hbm, gains_ref, loss_ref = refs[count + 2 : count + 8]
+    low_ref, extra_ref, query_ref, key_ref, value_ref, out_ref, in_sems, out_sems = refs[count + 8 :]
     me = me_ref[0]
-    cols = sort_ref.shape[2]
+    cols = low_ref.shape[2]
     strips = out_ref.shape[1] // cols
     piece = (low_ref.shape[1] - rows - EXTRA) // strips
     arriving = arrived([(*place, ref) for place, ref in zip(places, refs)], low_ref, in_sems)
     for i in range(C):
         for copy in arriving[i]:
             copy.wait()
-
-        @pl.loop(0, rows // 16)
-        def _(n):
-            rows_n = pl.ds(pl.multiple_of(n * 16, 16), 16)
-            sort_ref[me ^ i, rows_n, :] = low_ref[i, rows_n, :].astype(f32)
-
         at = pl.ds(pl.multiple_of((me ^ i) * piece, piece), piece)
         for c in range(strips):
             strip = low_ref[i, rows + c * piece : rows + (c + 1) * piece, :]
             out_ref[at, c * cols : (c + 1) * cols] = strip.astype(f32)
         extra_ref[me ^ i] = low_ref[i, low_ref.shape[1] - EXTRA :, :].astype(f32)
+    leaving = started(out_sems, 3, (out_ref, grads_hbm[3]))
     extra = extra_ref[0]
     for b in range(1, C):
         extra = extra + extra_ref[b]
     row = lax.broadcasted_iota(jnp.int32, gains_ref.shape, 0)
     gains_ref[...] = extra[:8, :] / jnp.where(row == 0, gain_ref[...], 1.0)
     loss_ref[...] = jnp.sum(extra[2:3, :], axis=1, keepdims=True) / valid_ref[0, 0]
-    lane = lax.broadcasted_iota(jnp.int32, sort_ref.shape[1:], 1)
-    for ref, first, size in (
-        (query_ref, 0, q_cols),
-        (key_ref, q_cols, kv_cols),
-        (value_ref, q_cols + kv_cols, kv_cols),
+    lane = lax.broadcasted_iota(jnp.int32, (rows, cols), 1)
+    for n, (ref, first, size) in enumerate(
+        (
+            (query_ref, 0, q_cols),
+            (key_ref, q_cols, kv_cols),
+            (value_ref, q_cols + kv_cols, kv_cols),
+        )
     ):
         many = cols // size
         for group in range(C // many):
             whole = None
             for j in range(many):
-                x = sort_ref[group * many + j]
+                x = low_ref[me ^ (group * many + j), :rows, :].astype(f32)
                 shift = (j * size - first) % cols
                 x = pltpu.roll(x, shift, 1) if shift else x
                 whole = x if whole is None else jnp.where(lane < j * size, whole, x)
             ref[:, group * cols : (group + 1) * cols] = whole
+        leaving += started(out_sems, n, (ref, grads_hbm[n]))
+    for copy in leaving:
+        copy.wait()
 
 
 def attention_grads(pieces, me, gain, valid_count, C, rows, width, q_cols, kv_cols, kv_copies):
@@ -1008,25 +1004,24 @@
         gains = extra[0, :rows] / gain, extra[1, :rows]
         loss = jnp.sum(extra[2]) / valid_count
         return query, kv_final(q_cols), kv_final(q_cols + kv_cols), out, *gains, loss
+    shapes = [(rows, C * q_cols), (rows, many * kv_cols), (rows, many * kv_cols), (C * piece, width)]
     *grads, gains, loss = pl.pallas_call(
         functools.partial(
             attention_grads_kernel, C, rows, q_cols, kv_cols, [x[:2] for x in pieces]
         ),
         out_shape=[
-            jax.ShapeDtypeStruct((rows, C * q_cols), f32),
-            jax.ShapeDtypeStruct((rows, many * kv_cols), f32),
-            jax.ShapeDtypeStruct((rows, many * kv_cols), f32),
-            jax.ShapeDtypeStruct((C * piece, width), f32),
+            *[pltpu.HBM(x, f32) for x in shapes],
             jax.ShapeDtypeStruct((8, cols), f32),
             jax.ShapeDtypeStruct((1, 1), f32),
         ],
         in_specs=[SMEM] + [HBM] * len(pieces) + [VMEM] * 2,
-        out_specs=[VMEM] * 6,
+        out_specs=[HBM] * 4 + [VMEM] * 2,
         scratch_shapes=[
             pltpu.VMEM((C, tall, cols), bf16),
-            pltpu.VMEM((C, rows, cols), f32),
             pltpu.VMEM((C, EXTRA, cols), f32),
+            *[pltpu.VMEM(x, f32) for x in shapes],
             pltpu.SemaphoreType.DMA((len(pieces),)),
+            pltpu.SemaphoreType.DMA((4,)),
         ],
         compiler_params=pltpu.CompilerParams(vmem_limit_bytes=24 * MIB),
         cost_estimate=cost(0, 8 * rows * C * cols),
@@ -1106,27 +1101,25 @@
         axis=1,
     )
     out_own = lax.dynamic_slice_in_dim(w_out, p * out_piece, out_piece, 0)
-    cols = qkv_own.shape[1]
-    out_own = jnp.concatenate([out_own[:, c : c + cols] for c in range(0, width, cols)], axis=0)
 
     scale_one = norm_scale(hidden_in)
     normed_one = (hidden_in * scale_one * gain_one).astype(bf16)
-    weights_own = jnp.concatenate([qkv_own, out_own], axis=0)
     tables = rope_tables(seq)
     normed_got, weights, tables = lax.optimization_barrier(
-        (plane_sends(normed_one), line_sends(weights_own), tables)
+        (plane_sends(normed_one), line_sends(qkv_own), tables)
     )
     normed_blocks = together(core_blocks([normed_one] + normed_got))
     gate_up_own, down_own = after((gate_up_own, down_own), weights)
     gate_up = lax.all_gather(gate_up_own, "fsdp", axis=0, tiled=True)
     down_rows = lax.all_gather(down_own, "fsdp", axis=0, tiled=True)
-    out_line = jnp.concatenate([x[rows_z:] for x in weights], axis=0)
-    out_got = plane_sends(out_line)
+    out_line = line_sends(after(out_own, weights))
     (normed_all, *saved), mine = attention_forward(
-        normed_blocks, [weights_own] + weights, tables, p, seq_length, z, q_heads, kv_heads
-    )
-
-    out_blocks = together(core_blocks([out_line] + after(out_got, normed_all)))
+        normed_blocks, [qkv_own] + weights, tables, p, seq_length, z, q_heads, kv_heads
+    )
+
+    out_line, normed_all = lax.optimization_barrier((out_line, normed_all))
+    out_line = jnp.concatenate(out_line, axis=0)
+    out_blocks = together(core_blocks([out_line] + together(plane_sends(out_line))))
     mine = after(mine, out_blocks)
     mine = [mine[0]] + together([partner(mine[s], "ctx", 2 * s) for s in range(1, R)])
     other = [partner(x, "ctx", 1) for x in mine]
@@ -1168,37 +1161,40 @@
     chips = chip_sums(keep, give)
     square = packed_ffn and C == 8
     out_got, grad_qkv = lax.optimization_barrier((chip_sends(out_chips), grad_qkv))
-    packs = attention_packs(
-        normed_all, grad_qkv, [out_chips[0]] + out_got, gain_part, grad_gain_two, squares, z, Z, C
+    packs, token = attention_packs(
+        grad_qkv, [out_chips[0]] + out_got, gain_part, grad_gain_two, squares, z, Z, C
     )
     shard_packs = lax.psum_scatter(packs, "fsdp", scatter_dimension=0, tiled=True)
     normed_got = [partner(x, "ctx", 2 * (s + 1)) for s, x in enumerate(after(chips[1:], out_got))]
     near = near_sends(after(shard_gate_up, out_got)) if square else []
-    normed_got, near = lax.optimization_barrier((normed_got, near))
+    normed_got, near, token = lax.optimization_barrier((normed_got, near, token))
     grad_normed_one = total(chips[0], normed_got)
     back_one, _ = norm_back(grad_normed_one, hidden_in, scale_one, gain_one)
     grad_hidden = grad_middle + back_one
 
 
     if square:
-        down_sent = after(shard_down, normed_got)
-        far, down_got = lax.optimization_barrier((far_sends(near), plane_sends(down_sent)))
+        down_near = near_sends(after(shard_down, normed_got))
+        far, down_near = lax.optimization_barrier((far_sends(near), down_near))
         pieces = square_pieces(shard_gate_up, near, far)
-        down_blocks = together(core_blocks([shard_down] + down_got))
-        pack_got = plane_sends(after(shard_packs, down_blocks))
         final_gate, final_up = column_grads(pieces, p, C, Z)
-        final_down = row_grads([(i, 0, x) for i, x in enumerate(down_blocks)], p, C)
-        pack_got, final_gate, final_down = lax.optimization_barrier((pack_got, final_gate, final_down))
-        pack_blocks = together(core_blocks([shard_packs] + pack_got))
+        pack_near = near_sends(after(shard_packs, far))
+        down_far, pack_near, final_gate = lax.optimization_barrier(
+            (far_sends(down_near), pack_near, final_gate)
+        )
+        final_down = row_grads(square_pieces(shard_down, down_near, down_far), p, C)
+        pack_far, final_down, grad_hidden = lax.optimization_barrier(
+            (far_sends(pack_near), final_down, grad_hidden)
+        )
+        pieces = square_pieces(shard_packs, pack_near, pack_far)
     else:
-        pack_blocks = plane_blocks(shard_packs)
+        pieces = [(i, 0, block) for i, block in enumerate(plane_blocks(shard_packs))]
         gate_up, down = [
             jnp.stack(unsort(plane_blocks(x), p)).astype(f32) for x in (shard_gate_up, shard_down)
         ]
         gate_up = gate_up.reshape(C, rows_z, 2, Z, ff_piece).transpose(2, 1, 3, 0, 4)
         final_gate, final_up = gate_up.reshape(2, rows_z, ff)
         final_down = down.reshape(C * ff_piece, width)
-    pieces = [(i, 0, block) for i, block in enumerate(pack_blocks)]
     final_query, final_key, final_value, final_out, *final_gains, loss_value = attention_grads(
         pieces,
         p,

time: 440 us -> 425 us (0.966)
  waiting for transfers between devices: 221 us -> 203 us
  starting transfers between devices: 66.2 us -> 75.6 us
    all_gather x1, waiting for transfers between devices: 38.8 us -> 26.6 us  [local(): gate_up = lax.all_gather(gate_up_own, 'fsdp', axis=0, tiled=True)]
    ppermute x99 -> x106, starting transfers between devices: 65.3 us -> 74.6 us  [partner(): lax.ppermute(x, axis, [(i, i ^ mask) for i in range(lax.axis_size(axis))])]
    ppermute x99 -> x106, waiting for transfers between devices: 182 us -> 176 us  [partner(): lax.ppermute(x, axis, [(i, i ^ mask) for i in range(lax.axis_size(axis))])]
    unnamed x95 -> x116, local copies, waits for them, and re-layouts: 9.45 us -> 9.65 us
  transfers between devices with their start and end apart: 104 -> 111, of which waited for: 46 -> 49; matrix products, arithmetic and copies ran while one was open for 8% -> 7% of each run, Pallas kernels for 13% -> 13%
where the time goes in v1:
time: 425 us; the launch traced here: 421 us
  waiting for transfers between devices  203 us (48%)
  Pallas kernels  79.9 us (19%)
  starting transfers between devices  75.6 us (18%)
  other arithmetic  23 us (5%)
  between operations  15.7 us (4%)
  local copies, waits for them, and re-layouts  13.4 us (3%)
  matrix products  10.6 us (2%)
    ppermute x106, waiting for transfers between devices, partner(): lax.ppermute(x, axis, [(i, i ^ mask) for i in range(lax.axis_size(axis))])  176 us
    ppermute x106, starting transfers between devices, partner(): lax.ppermute(x, axis, [(i, i ^ mask) for i in range(lax.axis_size(axis))])  74.6 us
    all_gather x1, waiting for transfers between devices, local(): gate_up = lax.all_gather(gate_up_own, 'fsdp', axis=0, tiled=True)  26.6 us
    pallas_call x1, Pallas kernels, attention_backward(): pl.pallas_call(functools.partial(attention_backward_kernel, C, tokens, q_...  14.7 us
    pallas_call x1, Pallas kernels, attention_forward(): pl.pallas_call(functools.partial(attention_forward_kernel, C, Z, tokens,...  11.7 us
    dot_general x2, matrix products, transposed_times(): lax.dot_general(left, right, (((0,), (0,)), ((), ())), preferred_element_...  10.6 us
    unnamed x116, local copies, waits for them, and re-layouts  9.65 us
    pallas_call x1, Pallas kernels, ffn_forward(): pl.pallas_call(functools.partial(ffn_forward_kernel, C, cuts), out_shape=...  9.59 us
  transfers between devices with their start and end apart: 111, of which 49 were waited for; matrix products, arithmetic and copies ran while one was open for 7% of the time, Pallas kernels for 13%

profile of v1, /device:TPU:0, one launch (start us, length us, event | category | flops | bytes accessed | tf_op | source)
XLA Modules:
  0.0 421.1 jit_solution(720311038304588804)
XLA Ops:
  18.2 3.9 collective-permute-start.2
  22.8 3.5 collective-permute-done
  42.0 7.3 %collective-permute-done.5.refs_4_ = bf16[128,1536]{1,0:T(8,128)(2,1)S(1)} collective-permute-done((bf16[128,1536]{1,0:T(8,128)(2,1)S(1)}, bf16[128,1536]{1,0:T(8,128)(2,1)S(1)}, u32[]{:S(2)}, u32[]{:S(2)}) %collective-permute-start.5) | collective-permute-done | bytes 393248 | tf_op jit(solution)/shard_map/ppermute | solution.py:67
  57.2 11.7 %attention_forward.1 = (bf16[1024,1536]{1,0:T(8,128)(2,1)}, bf16[1536,384]{1,0:T(8,128)(2,1)}, bf16[1024,512]{1,0:T(8,128)(2,1)}, f32[1024,256]{1,0:T(8,128)}, f...) custom-call(s32[3]{0:T(128)S(1)} %pad_add_fusion.1.info_ref, ...), custom_call_target="tpu_custom_call" | custom-call | flops 1 | bytes 1 | tf_op jit(solution)/shard_map/attention_forward/pallas_call | solution.py:287
  68.9 6.4 %collective-permute-done.14 = bf16[48,1536]{1,0:T(8,128)(2,1)S(1)} collective-permute-done((bf16[48,1536]{1,0:T(8,128)(2,1)S(1)}, bf16[48,1536]{1,0:T(8,128)(2,1)S(1)}, u32[]{:S(2)}, u32[]{:S(2)}) %collective-permute-start.14) | collective-permute-done | bytes 147488 | tf_op jit(solution)/shard_map/ppermute | solution.py:67
  79.0 7.0 %collective-permute-done.17.refs_10_ = bf16[144,1536]{1,0:T(8,128)(2,1)S(1)} collective-permute-done((bf16[144,1536]{1,0:T(8,128)(2,1)S(1)}, bf16[144,1536]{1,0:T(8,128)(2,1)S(1)}, u32[]{:S(2)}, u32[]{:S(2)}) %collective-permute-start.17) | collective-permute-done | bytes 442400 | tf_op jit(solution)/shard_map/ppermute | solution.py:67
  86.3 4.7 %collective-permute-done.19.refs_14_ = bf16[144,1536]{1,0:T(8,128)(2,1)S(1)} collective-permute-done((bf16[144,1536]{1,0:T(8,128)(2,1)S(1)}, bf16[144,1536]{1,0:T(8,128)(2,1)S(1)}, u32[]{:S(2)}, u32[]{:S(2)}) %collective-permute-start.19) | collective-permute-done | bytes 442400 | tf_op jit(solution)/shard_map/ppermute | solution.py:67
  100.1 3.5 collective-permute-done.24.refs_2_
  105.5 4.2 middle_forward.1
  113.9 8.5 %collective-permute-done.31.refs_2_ = bf16[128,1536]{1,0:T(8,128)(2,1)S(1)} collective-permute-done((bf16[128,1536]{1,0:T(8,128)(2,1)S(1)}, bf16[128,1536]{1,0:T(8,128)(2,1)S(1)}, u32[]{:S(2)}, u32[]{:S(2)}) %collective-permute-start.31) | collective-permute-done | bytes 393248 | tf_op jit(solution)/shard_map/ppermute | solution.py:67
  122.9 7.5 %collective-permute-done.35.refs_6_ = bf16[128,1536]{1,0:T(8,128)(2,1)S(1)} collective-permute-done((bf16[128,1536]{1,0:T(8,128)(2,1)S(1)}, bf16[128,1536]{1,0:T(8,128)(2,1)S(1)}, u32[]{:S(2)}, u32[]{:S(2)}) %collective-permute-start.35) | collective-permute-done | bytes 393248 | tf_op jit(solution)/shard_map/ppermute | solution.py:67
  132.3 26.6 %all-gather.3.cloned.1.call-done.refs_8_ = bf16[1536,1024]{1,0:T(8,128)(2,1)} async-done(((bf16[384,1024]{1,0:T(8,128)(2,1)}), bf16[1536,1024]{1,0:T(8,128)(2,1)}) %all-gather.3.cloned.1.call-update) | async-done | bytes 3145744 | tf_op jit(solution)/shard_map/all_gather | solution.py:1113
  158.9 9.6 %ffn_forward.1 = (bf16[1024,1536]{1,0:T(8,128)(2,1)}, bf16[1024,512]{1,0:T(8,128)(2,1)}, bf16[1024,1024]{1,0:T(8,128)(2,1)}, bf16[128,1536]{1,0:T(8,128)(2,1)S(1...) custom-call(bf16[128,1536]{1,0:T(8,128)(2,1)} %copy-done.7, ...), custom_call_target="tpu_custom_call" | custom-call | flops 1 | bytes 1 | tf_op jit(solution)/shard_map/ffn_forward/pallas_call | solution.py:492
  177.6 5.7 %collective-permute-done.43 = bf16[128,1536]{1,0:T(8,128)(2,1)S(1)} collective-permute-done((bf16[128,1536]{1,0:T(8,128)(2,1)}, bf16[128,1536]{1,0:T(8,128)(2,1)S(1)}, u32[]{:S(2)}, u32[]{:S(2)}) %collective-permute-start.43) | collective-permute-done | bytes 393248 | tf_op jit(solution)/shard_map/ppermute | solution.py:67
  183.3 9.7 %collective-permute-done.41 = bf16[128,1536]{1,0:T(8,128)(2,1)S(1)} collective-permute-done((bf16[128,1536]{1,0:T(8,128)(2,1)}, bf16[128,1536]{1,0:T(8,128)(2,1)S(1)}, u32[]{:S(2)}, u32[]{:S(2)}) %collective-permute-start.41) | collective-permute-done | bytes 393248 | tf_op jit(solution)/shard_map/ppermute | solution.py:67
  200.6 8.6 %collective-permute-done.45.refs_2_ = bf16[128,1536]{1,0:T(8,128)(2,1)S(1)} collective-permute-done((bf16[128,1536]{1,0:T(8,128)(2,1)S(1)}, bf16[128,1536]{1,0:T(8,128)(2,1)S(1)}, u32[]{:S(2)}, u32[]{:S(2)}) %collective-permute-start.45) | collective-permute-done | bytes 393248 | tf_op jit(solution)/shard_map/ppermute | solution.py:67
  209.1 5.5 %collective-permute-done.47.refs_4_ = bf16[128,1536]{1,0:T(8,128)(2,1)S(1)} collective-permute-done((bf16[128,1536]{1,0:T(8,128)(2,1)S(1)}, bf16[128,1536]{1,0:T(8,128)(2,1)S(1)}, u32[]{:S(2)}, u32[]{:S(2)}) %collective-permute-start.47) | collective-permute-done | bytes 393248 | tf_op jit(solution)/shard_map/ppermute | solution.py:67
  218.1 8.0 %ffn_backward.1 = (bf16[1024,1536]{1,0:T(8,128)(2,1)S(1)}, bf16[1024,1024]{1,0:T(8,128)(2,1)S(1)}, bf16[128,1536]{1,0:T(8,128)(2,1)S(1)}, bf16[128,1536]{1,0:T(8...) custom-call(bf16[128,1536]{1,0:T(8,128)(2,1)S(1)} %get-tuple-element, ...), custom_call_target="tpu_custom_call" | custom-call | flops 1 | bytes 1 | tf_op jit(solution)/shard_map/ffn_backward/pallas_call | solution.py:541
  230.9 4.9 %convolution_convert_fusion = bf16[1536,1024]{1,0:T(8,128)(2,1)} fusion(bf16[1024,1536]{1,0:T(8,128)(2,1)S(1)} %copy-done.55, bf16[1024,1024]{1,0:T(8,128)(2,1)S(1)} %get-tuple-element.271), kind=kOutput, calls=%fused_computation | convolution fusion | flops 3222798336 | bytes 8388608 | tf_op jit(solution)/shard_map/dot_general | solution.py:52
  239.4 5.8 %convolution_convert_fusion.1 = bf16[512,1536]{1,0:T(8,128)(2,1)} fusion(bf16[1024,512]{1,0:T(8,128)(2,1)} %get-tuple-element.267, bf16[1024,1536]{1,0:T(8,128)(2,1)} %copy-done.8), kind=kOutput, calls=%fused_computation.1 | convolution fusion | flops 1611399168 | bytes 5767168 | tf_op jit(solution)/shard_map/dot_general | solution.py:52
  248.1 8.6 %collective-permute-done.55.refs_2_ = bf16[128,1536]{1,0:T(8,128)(2,1)} collective-permute-done((bf16[128,1536]{1,0:T(8,128)(2,1)}, bf16[128,1536]{1,0:T(8,128)(2,1)}, u32[]{:S(2)}, u32[]{:S(2)}) %collective-permute-start.55) | collective-permute-done | bytes 393248 | tf_op jit(solution)/shard_map/ppermute | solution.py:67
  256.7 5.2 %middle_backward.1 = (f32[128,1536]{1,0:T(8,128)S(1)}, bf16[128,1536]{1,0:T(8,128)(2,1)S(1)}, f32[1,1536]{1,0:T(1,128)S(1)}, bf16[128,384]{1,0:T(8,128)(2,1)S(1)...) custom-call(s32[1]{0:T(128)} %bitcast.me_ref.info_ref, ...), custom_call_target="tpu_custom_call" | custom-call | flops 1 | bytes 1 | tf_op jit(solution)/shard_map/middle_backward/pallas_call | solution.py:804
  279.6 14.7 %attention_backward.1 = (bf16[1536,384]{1,0:T(8,128)(2,1)S(1)}, f32[8,1536]{1,0:T(8,128)S(1)}, bf16[128,1536]{1,0:T(8,128)(2,1)S(1)}, bf16[128,1536]{1,0:T(8,128...) custom-call(s32[2]{0:T(128)S(1)} %pad_add_fusion.2.info_ref, ...), custom_call_target="tpu_custom_call" | custom-call | flops 1 | bytes 1 | tf_op jit(solution)/shard_map/attention_backward/pallas_call | solution.py:404
  294.4 8.9 %collective-permute-done.61.refs_3_ = bf16[192,1536]{1,0:T(8,128)(2,1)S(1)} collective-permute-done((bf16[192,1536]{1,0:T(8,128)(2,1)S(1)}, bf16[192,1536]{1,0:T(8,128)(2,1)S(1)}, u32[]{:S(2)}, u32[]{:S(2)}) %collective-permute-start.61) | collective-permute-done | bytes 589856 | tf_op jit(solution)/shard_map/ppermute | solution.py:67
  303.3 3.3 attention_packs.1
  318.4 21.2 %collective-permute-done.76 = bf16[128,1536]{1,0:T(8,128)(2,1)S(1)} collective-permute-done((bf16[128,1536]{1,0:T(8,128)(2,1)S(1)}, bf16[128,1536]{1,0:T(8,128)(2,1)S(1)}, u32[]{:S(2)}, u32[]{:S(2)}) %collective-permute-start.76) | collective-permute-done | bytes 393248 | tf_op jit(solution)/shard_map/ppermute | solution.py:67
  339.6 8.9 %collective-permute-done.77 = bf16[128,1536]{1,0:T(8,128)(2,1)} collective-permute-done((bf16[128,1536]{1,0:T(8,128)(2,1)}, bf16[128,1536]{1,0:T(8,128)(2,1)}, u32[]{:S(2)}, u32[]{:S(2)}) %collective-permute-start.77) | collective-permute-done | bytes 393248 | tf_op jit(solution)/shard_map/ppermute | solution.py:67
  352.8 8.0 %collective-permute-done.83.refs_2_ = bf16[128,1536]{1,0:T(8,128)(2,1)S(1)} collective-permute-done((bf16[128,1536]{1,0:T(8,128)(2,1)}, bf16[128,1536]{1,0:T(8,128)(2,1)S(1)}, u32[]{:S(2)}, u32[]{:S(2)}) %collective-permute-start.83) | collective-permute-done | bytes 393248 | tf_op jit(solution)/shard_map/ppermute | solution.py:67
  362.2 8.1 %collective-permute-done.81.refs_6_ = bf16[192,1024]{1,0:T(8,128)(2,1)} collective-permute-done((bf16[192,1024]{1,0:T(8,128)(2,1)S(1)}, bf16[192,1024]{1,0:T(8,128)(2,1)}, u32[]{:S(2)}, u32[]{:S(2)}) %collective-permute-start.81) | collective-permute-done | bytes 393248 | tf_op jit(solution)/shard_map/ppermute | solution.py:67
  385.0 7.3 %column_grads.1 = (f32[384,4096]{1,0:T(8,128)}, f32[384,4096]{1,0:T(8,128)}) custom-call(s32[1]{0:T(128)} %bitcast.me_ref.info_ref, bf16[384,1024]{1,0:T(8,128)(2,1)} %reduce-scatter.6.cloned.1.call-done.refs_0_, bf16[384,1024]{1,0:T(8,128)(2,1)} %copy-done.23, bf16[384,1024]{1,0:T(8,128)(2,1)} %copy-done.14, ...), custom_call_target="tpu_custom_call" | custom-call | flops 1 | bytes 1 | tf_op jit(solution)/shard_map/column_grads/pallas_call | solution.py:638
  399.1 4.0 row_grads.1
  406.1 7.6 %attention_grads.1 = (f32[384,1536]{1,0:T(8,128)}, f32[384,768]{1,0:T(8,128)}, f32[384,768]{1,0:T(8,128)}, f32[384,1536]{1,0:T(8,128)}, f32[8,384]{1,0:T(8,128)S(1)}, /*index=5*/f32[1,1]{1,0:T(1,128)}) custom-call(s32[1]{0:T(128)} %bitcast.me_ref.info_ref, bf16[592,384]{1,0:T(8,128)(2,1)} %reduce-scatter.4.cloned.1.call-done.refs_0_, ...), custom_call_target="tpu_custom_call" | custom-call | flops 1 | bytes 1 | tf_op jit(solution)/shard_map/attention_grads/pallas_call | solution.py:1008
  (381 shorter events, 147.1 us)
Async XLA Ops:
  7.2 125.0 %all-gather.5.cloned.1.call-start = ((), (), s32[]{:S(2)}) async-start(), calls=%async_computation.4 | async-start | bytes 1966080 | tf_op jit(solution)/shard_map/all_gather | solution.py:1114
  9.9 22.9 %collective-permute-start.7 = (bf16[384,384]{1,0:T(8,128)(2,1)S(1)}, bf16[384,384]{1,0:T(8,128)(2,1)}, u32[]{:S(2)}, u32[]{:S(2)}) collective-permute-start(bf16[384,384]{1,0:T(8,128)(2,1)S(1)} %pad_maximum_fusion.refs_8_), channel_id=1, source_target_pairs={{0,1},{1,0},{2,3},{3,2},{4,5},{5,4},{6,7},{7,6},{8,9},{9,8},{10,11... | collective-permute-start | bytes 884744 | tf_op jit(solution)/shard_map/ppermute | solution.py:67
  13.0 26.2 %collective-permute-start.8 = (bf16[384,384]{1,0:T(8,128)(2,1)S(1)}, bf16[384,384]{1,0:T(8,128)(2,1)S(1)}, u32[]{:S(2)}, u32[]{:S(2)}) collective-permute-start(bf16[384,384]{1,0:T(8,128)(2,1)S(1)} %pad_maximum_fusion.refs_8_), channel_id=1, source_target_pairs={{0,2},{1,3},{2,0},{3,1},{4,6},{5,7},{6,4},{7,5},{8,10},{9,11},{10,... | collective-permute-start | bytes 884744 | tf_op jit(solution)/shard_map/ppermute | solution.py:67
  31.4 17.9 %collective-permute-start.5 = (bf16[128,1536]{1,0:T(8,128)(2,1)S(1)}, bf16[128,1536]{1,0:T(8,128)(2,1)S(1)}, u32[]{:S(2)}, u32[]{:S(2)}) collective-permute-start(bf16[128,1536]{1,0:T(8,128)(2,1)S(1)} %multiply_convert_fusion.refs_0_), channel_id=1, source_target_pairs={{0,16},{4,20},{8,24},{12,28},{16,0},{20,4},{24,8},{28,12},{1,17},{... | collective-permute-start | bytes 1179656 | tf_op jit(solution)/shard_map/ppermute | solution.py:67
  32.9 16.4 %collective-permute-start.6 = (bf16[128,1536]{1,0:T(8,128)(2,1)S(1)}, bf16[128,1536]{1,0:T(8,128)(2,1)S(1)}, u32[]{:S(2)}, u32[]{:S(2)}) collective-permute-start(bf16[128,1536]{1,0:T(8,128)(2,1)S(1)} %multiply_convert_fusion.refs_0_), channel_id=1, source_target_pairs={{0,24},{4,28},{8,16},{12,20},{16,8},{20,12},{24,0},{28,4},{1,25},{... | collective-permute-start | bytes 1179656 | tf_op jit(solution)/shard_map/ppermute | solution.py:67
  49.3 109.6 %all-gather.3.cloned.1.call-start = ((), (), s32[]{:S(2)}) async-start(), calls=%async_computation.3 | async-start | bytes 3932160 | tf_op jit(solution)/shard_map/all_gather | solution.py:1113
  50.1 260.5 %reduce-scatter.6.cloned.1.call-start = ((), (), s32[]{:S(2)}) async-start(), calls=%async_computation.6 | async-start | bytes 3932160 | tf_op jit(solution)/shard_map/reduce_scatter | solution.py:1147
  53.5 21.9 %collective-permute-start.14 = (bf16[48,1536]{1,0:T(8,128)(2,1)S(1)}, bf16[48,1536]{1,0:T(8,128)(2,1)S(1)}, u32[]{:S(2)}, u32[]{:S(2)}) collective-permute-start(bf16[48,1536]{1,0:T(8,128)(2,1)S(1)} %constant_dynamic-slice_fusion), channel_id=1, source_target_pairs={{0,2},{1,3},{2,0},{3,1},{4,6},{5,7},{6,4},{7,5},{8,10},{9,11},{10,... | collective-permute-start | bytes 442376 | tf_op jit(solution)/shard_map/ppermute | solution.py:67
  54.6 20.7 %collective-permute-start.15 = (bf16[48,1536]{1,0:T(8,128)(2,1)S(1)}, bf16[48,1536]{1,0:T(8,128)(2,1)S(1)}, u32[]{:S(2)}, u32[]{:S(2)}) collective-permute-start(bf16[48,1536]{1,0:T(8,128)(2,1)S(1)} %constant_dynamic-slice_fusion), channel_id=1, source_target_pairs={{0,3},{1,2},{2,1},{3,0},{4,7},{5,6},{6,5},{7,4},{8,11},{9,10},{10,... | collective-permute-start | bytes 442376 | tf_op jit(solution)/shard_map/ppermute | solution.py:67
  112.3 18.1 %collective-permute-start.35 = (bf16[128,1536]{1,0:T(8,128)(2,1)S(1)}, bf16[128,1536]{1,0:T(8,128)(2,1)S(1)}, u32[]{:S(2)}, u32[]{:S(2)}) collective-permute-start(bf16[128,1536]{1,0:T(8,128)(2,1)S(1)} %get-tuple-element.238.refs_0_), channel_id=1, source_target_pairs={{0,24},{4,28},{8,16},{12,20},{16,8},{20,12},{24,0},{28,4},{1,25},{... | collective-permute-start | bytes 1179656 | tf_op jit(solution)/shard_map/ppermute | solution.py:67
  113.9 16.5 %collective-permute-start.30 = (bf16[128,1536]{1,0:T(8,128)(2,1)S(1)}, bf16[128,1536]{1,0:T(8,128)(2,1)S(1)}, u32[]{:S(2)}, u32[]{:S(2)}) collective-permute-start(bf16[128,1536]{1,0:T(8,128)(2,1)S(1)} %get-tuple-element.238.refs_0_), channel_id=1, source_target_pairs={{0,4},{4,0},{8,12},{12,8},{16,20},{20,16},{24,28},{28,24},{1,5},{5... | collective-permute-start | bytes 1179656 | tf_op jit(solution)/shard_map/ppermute | solution.py:67
  173.5 19.5 %collective-permute-start.41 = (bf16[128,1536]{1,0:T(8,128)(2,1)}, bf16[128,1536]{1,0:T(8,128)(2,1)S(1)}, u32[]{:S(2)}, u32[]{:S(2)}) collective-permute-start(bf16[128,1536]{1,0:T(8,128)(2,1)} %add_convert_fusion.10), channel_id=1, source_target_pairs={{0,16},{4,20},{8,24},{12,28},{16,0},{20,4},{24,8},{28,12},{1,17},{... | collective-permute-start | bytes 1179656 | tf_op jit(solution)/shard_map/ppermute | solution.py:67
  175.8 17.2 %collective-permute-start.39 = (bf16[128,1536]{1,0:T(8,128)(2,1)}, bf16[128,1536]{1,0:T(8,128)(2,1)S(1)}, u32[]{:S(2)}, u32[]{:S(2)}) collective-permute-start(bf16[128,1536]{1,0:T(8,128)(2,1)} %add_convert_fusion.11), channel_id=1, source_target_pairs={{0,24},{4,28},{8,16},{12,20},{16,8},{20,12},{24,0},{28,4},{1,25},{... | collective-permute-start | bytes 1179656 | tf_op jit(solution)/shard_map/ppermute | solution.py:67
  176.3 16.7 %collective-permute-start.37 = (bf16[128,1536]{1,0:T(8,128)(2,1)S(1)}, bf16[128,1536]{1,0:T(8,128)(2,1)}, u32[]{:S(2)}, u32[]{:S(2)}) collective-permute-start(bf16[128,1536]{1,0:T(8,128)(2,1)S(1)} %get-tuple-element.244), channel_id=1, source_target_pairs={{0,4},{4,0},{8,12},{12,8},{16,20},{20,16},{24,28},{28,24},{1,5},{5... | collective-permute-start | bytes 1179656 | tf_op jit(solution)/shard_map/ppermute | solution.py:67
  197.6 17.0 %collective-permute-start.47 = (bf16[128,1536]{1,0:T(8,128)(2,1)S(1)}, bf16[128,1536]{1,0:T(8,128)(2,1)S(1)}, u32[]{:S(2)}, u32[]{:S(2)}) collective-permute-start(bf16[128,1536]{1,0:T(8,128)(2,1)S(1)} %get-tuple-element.374.refs_0_), channel_id=1, source_target_pairs={{0,16},{4,20},{8,24},{12,28},{16,0},{20,4},{24,8},{28,12},{1,17},{... | collective-permute-start | bytes 1179656 | tf_op jit(solution)/shard_map/ppermute | solution.py:67
  199.1 17.3 %collective-permute-start.49 = (bf16[128,1536]{1,0:T(8,128)(2,1)S(1)}, bf16[128,1536]{1,0:T(8,128)(2,1)S(1)}, u32[]{:S(2)}, u32[]{:S(2)}) collective-permute-start(bf16[128,1536]{1,0:T(8,128)(2,1)S(1)} %get-tuple-element.374.refs_0_), channel_id=1, source_target_pairs={{0,24},{4,28},{8,16},{12,20},{16,8},{20,12},{24,0},{28,4},{1,25},{... | collective-permute-start | bytes 1179656 | tf_op jit(solution)/shard_map/ppermute | solution.py:67
  235.8 112.7 %reduce-scatter.8.cloned.1.call-start = ((), (), s32[]{:S(2)}) async-start(), calls=%async_computation.7 | async-start | bytes 1966080 | tf_op jit(solution)/shard_map/reduce_scatter | solution.py:1148
  237.1 19.6 %collective-permute-start.55 = (bf16[128,1536]{1,0:T(8,128)(2,1)}, bf16[128,1536]{1,0:T(8,128)(2,1)}, u32[]{:S(2)}, u32[]{:S(2)}) collective-permute-start(bf16[128,1536]{1,0:T(8,128)(2,1)} %add_convert_fusion.7), channel_id=1, source_target_pairs={{0,16},{4,20},{8,24},{12,28},{16,0},{20,4},{24,8},{28,12},{1,17},{... | collective-permute-start | bytes 1179656 | tf_op jit(solution)/shard_map/ppermute | solution.py:67
  238.8 17.9 %collective-permute-start.53 = (bf16[128,1536]{1,0:T(8,128)(2,1)}, bf16[128,1536]{1,0:T(8,128)(2,1)}, u32[]{:S(2)}, u32[]{:S(2)}) collective-permute-start(bf16[128,1536]{1,0:T(8,128)(2,1)} %add_convert_fusion.8), channel_id=1, source_target_pairs={{0,24},{4,28},{8,16},{12,20},{16,8},{20,12},{24,0},{28,4},{1,25},{... | collective-permute-start | bytes 1179656 | tf_op jit(solution)/shard_map/ppermute | solution.py:67
  245.2 133.9 %reduce-scatter.4.cloned.1.call-start = ((), (), s32[]{:S(2)}) async-start(), calls=%async_computation.5 | async-start | bytes 2273280 | tf_op jit(solution)/shard_map/reduce_scatter | solution.py:1167
  273.9 20.5 %collective-permute-start.63 = (bf16[192,1536]{1,0:T(8,128)(2,1)S(1)}, bf16[192,1536]{1,0:T(8,128)(2,1)S(1)}, u32[]{:S(2)}, u32[]{:S(2)}) collective-permute-start(bf16[192,1536]{1,0:T(8,128)(2,1)S(1)} %add_convert_fusion), channel_id=1, source_target_pairs={{0,8},{4,12},{8,0},{12,4},{16,24},{20,28},{24,16},{28,20},{1,9},{5... | collective-permute-start | bytes 1769480 | tf_op jit(solution)/shard_map/ppermute | solution.py:67
  275.2 28.0 %collective-permute-start.61 = (bf16[192,1536]{1,0:T(8,128)(2,1)S(1)}, bf16[192,1536]{1,0:T(8,128)(2,1)S(1)}, u32[]{:S(2)}, u32[]{:S(2)}) collective-permute-start(bf16[192,1536]{1,0:T(8,128)(2,1)S(1)} %add_convert_fusion.1), channel_id=1, source_target_pairs={{0,16},{4,20},{8,24},{12,28},{16,0},{20,4},{24,8},{28,12},{1,17},{... | collective-permute-start | bytes 1769480 | tf_op jit(solution)/shard_map/ppermute | solution.py:67
  276.9 26.4 %collective-permute-start.59 = (bf16[192,1536]{1,0:T(8,128)(2,1)S(1)}, bf16[192,1536]{1,0:T(8,128)(2,1)S(1)}, u32[]{:S(2)}, u32[]{:S(2)}) collective-permute-start(bf16[192,1536]{1,0:T(8,128)(2,1)S(1)} %add_convert_fusion.2), channel_id=1, source_target_pairs={{0,24},{4,28},{8,16},{12,20},{16,8},{20,12},{24,0},{28,4},{1,25},{... | collective-permute-start | bytes 1769480 | tf_op jit(solution)/shard_map/ppermute | solution.py:67
  310.6 37.9 %collective-permute-start.79 = (bf16[384,1024]{1,0:T(8,128)(2,1)}, bf16[384,1024]{1,0:T(8,128)(2,1)S(1)}, u32[]{:S(2)}, u32[]{:S(2)}) collective-permute-start(bf16[384,1024]{1,0:T(8,128)(2,1)} %reduce-scatter.6.cloned.1.call-done.refs_0_), channel_id=1, source_target_pairs={{0,8},{4,12},{8,0},{12,4},{16,24},{20,28},{24,16},{28,20},{1,9},{5... | collective-permute-start | bytes 2359304 | tf_op jit(solution)/shard_map/ppermute | solution.py:67
  312.0 36.5 %collective-permute-start.80 = (bf16[384,1024]{1,0:T(8,128)(2,1)}, bf16[384,1024]{1,0:T(8,128)(2,1)S(1)}, u32[]{:S(2)}, u32[]{:S(2)}) collective-permute-start(bf16[384,1024]{1,0:T(8,128)(2,1)} %reduce-scatter.6.cloned.1.call-done.refs_0_), channel_id=1, source_target_pairs={{0,16},{4,20},{8,24},{12,28},{16,0},{20,4},{24,8},{28,12},{1,17},{... | collective-permute-start | bytes 2359304 | tf_op jit(solution)/shard_map/ppermute | solution.py:67
  314.8 24.8 %collective-permute-start.76 = (bf16[128,1536]{1,0:T(8,128)(2,1)S(1)}, bf16[128,1536]{1,0:T(8,128)(2,1)S(1)}, u32[]{:S(2)}, u32[]{:S(2)}) collective-permute-start(bf16[128,1536]{1,0:T(8,128)(2,1)S(1)} %add_convert_fusion.5), channel_id=1, source_target_pairs={{0,8},{4,12},{8,0},{12,4},{16,24},{20,28},{24,16},{28,20},{1,9},{5... | collective-permute-start | bytes 1179656 | tf_op jit(solution)/shard_map/ppermute | solution.py:67
  315.2 33.2 %collective-permute-start.77 = (bf16[128,1536]{1,0:T(8,128)(2,1)}, bf16[128,1536]{1,0:T(8,128)(2,1)}, u32[]{:S(2)}, u32[]{:S(2)}) collective-permute-start(bf16[128,1536]{1,0:T(8,128)(2,1)} %add_convert_fusion.4), channel_id=1, source_target_pairs={{0,16},{4,20},{8,24},{12,28},{16,0},{20,4},{24,8},{28,12},{1,17},{... | collective-permute-start | bytes 1179656 | tf_op jit(solution)/shard_map/ppermute | solution.py:67
  315.8 32.7 %collective-permute-start.78 = (bf16[128,1536]{1,0:T(8,128)(2,1)}, bf16[128,1536]{1,0:T(8,128)(2,1)}, u32[]{:S(2)}, u32[]{:S(2)}) collective-permute-start(bf16[128,1536]{1,0:T(8,128)(2,1)} %add_convert_fusion.3), channel_id=1, source_target_pairs={{0,24},{4,28},{8,16},{12,20},{16,8},{20,12},{24,0},{28,4},{1,25},{... | collective-permute-start | bytes 1179656 | tf_op jit(solution)/shard_map/ppermute | solution.py:67
  350.0 22.9 %collective-permute-start.89 = (bf16[384,1024]{1,0:T(8,128)(2,1)}, bf16[384,1024]{1,0:T(8,128)(2,1)S(1)}, u32[]{:S(2)}, u32[]{:S(2)}) collective-permute-start(bf16[384,1024]{1,0:T(8,128)(2,1)} %reduce-scatter.6.cloned.1.call-done.refs_0_), channel_id=1, source_target_pairs={{0,4},{4,0},{8,12},{12,8},{16,20},{20,16},{24,28},{28,24},{1,5},{5... | collective-permute-start | bytes 2359304 | tf_op jit(solution)/shard_map/ppermute | solution.py:67
  350.7 19.6 %collective-permute-start.81 = (bf16[192,1024]{1,0:T(8,128)(2,1)S(1)}, bf16[192,1024]{1,0:T(8,128)(2,1)}, u32[]{:S(2)}, u32[]{:S(2)}) collective-permute-start(bf16[192,1024]{1,0:T(8,128)(2,1)S(1)} %slice.36), channel_id=1, source_target_pairs={{0,16},{4,20},{8,24},{12,28},{16,0},{20,4},{24,8},{28,12},{1,17},{... | collective-permute-start | bytes 1179656 | tf_op jit(solution)/shard_map/ppermute | solution.py:67
  352.2 18.1 %collective-permute-start.82 = (bf16[192,1024]{1,0:T(8,128)(2,1)S(1)}, bf16[192,1024]{1,0:T(8,128)(2,1)}, u32[]{:S(2)}, u32[]{:S(2)}) collective-permute-start(bf16[192,1024]{1,0:T(8,128)(2,1)S(1)} %slice.37), channel_id=1, source_target_pairs={{0,8},{4,12},{8,0},{12,4},{16,24},{20,28},{24,16},{28,20},{1,9},{5... | collective-permute-start | bytes 1179656 | tf_op jit(solution)/shard_map/ppermute | solution.py:67
  362.1 20.5 %collective-permute-start.90 = (bf16[384,1024]{1,0:T(8,128)(2,1)S(1)}, bf16[384,1024]{1,0:T(8,128)(2,1)}, u32[]{:S(2)}, u32[]{:S(2)}) collective-permute-start(bf16[384,1024]{1,0:T(8,128)(2,1)S(1)} %collective-permute-done.79.refs_2_), channel_id=1, source_target_pairs={{0,4},{4,0},{8,12},{12,8},{16,20},{20,16},{24,28},{28,24},{1,5},{5... | collective-permute-start | bytes 2359304 | tf_op jit(solution)/shard_map/ppermute | solution.py:67
  (135 other events, 1090.5 us)
Sparse Core Ops, SparseCore 0:
  49.4 45.6 all-gather.4
  97.2 61.6 all-gather.2
  235.9 58.8 reduce-scatter.5
  297.5 35.3 reduce-scatter.7
  335.6 38.2 reduce-scatter.3

commit v2 on v1

--- a/solution.py
+++ b/solution.py
@@ -450,20 +450,16 @@
             ref[:, at] = part[i * tokens : (i + 1) * tokens, :].astype(bf16)
 
 
-def ffn_forward_kernel(C, cuts, *refs):
+def ffn_units_kernel(C, cuts, *refs):
     n_refs = refs[:C]
-    gu_hbm, down_hbm, n_hbm, act_hbm, coef_hbm = refs[C : C + 5]
-    keep_refs = refs[C + 5 : C + 5 + C // 2]
-    give_refs = refs[C + 5 + C // 2 : 2 * C + 5]
-    gu_ref, down_ref, n_all_ref, act_ref, coef_ref, sems = refs[2 * C + 5 :]
+    gu_hbm, n_hbm, coef_hbm, act_ref = refs[C : C + 4]
+    gu_ref, n_all_ref, coef_ref, sems = refs[C + 4 :]
     tokens = n_refs[0].shape[0]
     pairs = [(n_refs[i], n_all_ref.at[i * tokens : (i + 1) * tokens, :]) for i in range(C)]
-    weights = started(sems, 3, (gu_hbm, gu_ref), (down_hbm, down_ref), *pairs)
-    w = down_ref.shape[0] // cuts
-    for copy in weights[2:]:
+    for copy in started(sems, 0, (gu_hbm, gu_ref), *pairs):
         copy.wait()
     saved = started(sems, 0, (n_all_ref, n_hbm))
-    weights[0].wait()
+    w = act_ref.shape[1] // cuts
 
     @pl.loop(0, cuts)
     def _(j):
@@ -476,35 +472,57 @@
         slope = up * (sigmoid * (1.0 + gate * (1.0 - sigmoid)))
         coef_ref[:, at] = jnp.concatenate([slope, silu], axis=1).astype(bf16)
 
-    saved += started(sems, 1, (act_ref, act_hbm), (coef_ref, coef_hbm))
-    weights[1].wait()
-    parts_of(lambda at: times(act_ref[...], down_ref[:, at]), keep_refs, give_refs)
+    saved += started(sems, 1, (coef_ref, coef_hbm))
     for copy in saved:
         copy.wait()
 
 
-def ffn_forward(blocks, gate_up, down, cuts):
+def ffn_units(blocks, gate_up, cuts):
     C = len(blocks)
     tokens, width = blocks[0].shape
-    seq, own = C * tokens, down.shape[0]
-    saved = [((seq, width), bf16), ((seq, own), bf16), ((seq, 2 * own), bf16)]
-    part = jax.ShapeDtypeStruct((tokens, width), bf16)
+    seq, both = C * tokens, gate_up.shape[1]
+    return pl.pallas_call(
+        functools.partial(ffn_units_kernel, C, cuts),
+        out_shape=[
+            pltpu.HBM((seq, width), bf16),
+            pltpu.HBM((seq, both), bf16),
+            jax.ShapeDtypeStruct((seq, both // 2), bf16),
+        ],
+        in_specs=[HBM] * (C + 1),
+        out_specs=[HBM, HBM, VMEM],
+        scratch_shapes=[
+            pltpu.VMEM(gate_up.shape, bf16),
+            pltpu.VMEM((seq, width), bf16),
+            pltpu.VMEM((seq, both), bf16),
+            pltpu.SemaphoreType.DMA((C + 1,)),
+        ],
+        compiler_params=pltpu.CompilerParams(vmem_limit_bytes=20 * MIB),
+        cost_estimate=cost(2 * seq * width * both, 3 * seq * width),
+        name="ffn_units",
+    )(*in_hbm(*blocks, gate_up))
+
+
+def ffn_forward_kernel(C, act_ref, down_hbm, *refs):
+    keep_refs, give_refs, (down_ref, sems) = refs[: C // 2], refs[C // 2 : C], refs[C:]
+    for copy in started(sems, 0, (down_hbm, down_ref)):
+        copy.wait()
+    parts_of(lambda at: times(act_ref[...], down_ref[:, at]), keep_refs, give_refs)
+
+
+def ffn_forward(activated, down, C):
+    seq, own = activated.shape
+    width = down.shape[1]
     result = pl.pallas_call(
-        functools.partial(ffn_forward_kernel, C, cuts),
-        out_shape=[pltpu.HBM(*x) for x in saved] + [part] * C,
-        in_specs=[HBM] * (C + 2),
-        out_specs=[HBM] * 3 + [VMEM] * C,
-        scratch_shapes=[
-            pltpu.VMEM((width, 2 * own), bf16),
-            pltpu.VMEM((own, width), bf16),
-            *[pltpu.VMEM(*x) for x in saved],
-            pltpu.SemaphoreType.DMA((5 + C,)),
-        ],
-        compiler_params=pltpu.CompilerParams(vmem_limit_bytes=24 * MIB),
-        cost_estimate=cost(3 * seq * width * own, 3 * seq * width),
+        functools.partial(ffn_forward_kernel, C),
+        out_shape=[jax.ShapeDtypeStruct((seq // C, width), bf16)] * C,
+        in_specs=[VMEM, HBM],
+        out_specs=[VMEM] * C,
+        scratch_shapes=[pltpu.VMEM(down.shape, bf16), pltpu.SemaphoreType.DMA((1,))],
+        compiler_params=pltpu.CompilerParams(vmem_limit_bytes=12 * MIB),
+        cost_estimate=cost(seq * width * own, seq * width),
         name="ffn_forward",
-    )(*in_hbm(*blocks, gate_up, down))
-    return result[:3], result[3 : 3 + C // 2], result[3 + C // 2 :]
+    )(activated, *in_hbm(down))
+    return result[: C // 2], result[C // 2 :]
 
 
 def ffn_backward_kernel(C, cuts, *refs):
@@ -1069,10 +1087,24 @@
     qkv_cols = q_cols + 2 * kv_cols
     positions = p * tokens + jnp.arange(tokens, dtype=jnp.int32)
 
+    kv_start = (p * KV_HEADS // C) * HEAD_DIM
+    out_piece = rows_z // C
+    qkv_own = jnp.concatenate(
+        [
+            lax.dynamic_slice_in_dim(w_query, p * q_cols, q_cols, 1),
+            lax.dynamic_slice_in_dim(w_key, kv_start, kv_cols, 1),
+            lax.dynamic_slice_in_dim(w_value, kv_start, kv_cols, 1),
+            jnp.zeros((rows_z, -qkv_cols % LANES), bf16),
+        ],
+        axis=1,
+    )
+    out_own = lax.dynamic_slice_in_dim(w_out, p * out_piece, out_piece, 0)
+
     small = jnp.concatenate(
         [gain_attn.astype(f32), gain_ffn.astype(f32), jnp.full((LANES,), seq_length).astype(f32)]
     )
-    small = jnp.stack(unsort(line_blocks(small.reshape(1, -1)), z)).reshape(Z, -1)
+    small = after(small.reshape(1, -1), qkv_own)
+    small = jnp.stack(unsort(line_blocks(small), z)).reshape(Z, -1)
     gain_one = small[:, :rows_z].reshape(width)
     gain_two = small[:, rows_z : 2 * rows_z].reshape(width)
     valid_count = jnp.sum(small[:, 2 * rows_z])
@@ -1089,19 +1121,6 @@
             axis=1,
         )
         down_own = lax.dynamic_slice_in_dim(w_down, p * ff_piece, ff_piece, 0)
-    kv_start = (p * KV_HEADS // C) * HEAD_DIM
-    out_piece = rows_z // C
-    qkv_own = jnp.concatenate(
-        [
-            lax.dynamic_slice_in_dim(w_query, p * q_cols, q_cols, 1),
-            lax.dynamic_slice_in_dim(w_key, kv_start, kv_cols, 1),
-            lax.dynamic_slice_in_dim(w_value, kv_start, kv_cols, 1),
-            jnp.zeros((rows_z, -qkv_cols % LANES), bf16),
-        ],
-        axis=1,
-    )
-    out_own = lax.dynamic_slice_in_dim(w_out, p * out_piece, out_piece, 0)
-
     scale_one = norm_scale(hidden_in)
     normed_one = (hidden_in * scale_one * gain_one).astype(bf16)
     tables = rope_tables(seq)
@@ -1127,10 +1146,8 @@
         mine, other, out_blocks, w_out, hidden_in, gain_two, p, z, Z
     )
 
-    normed_two_blocks = plane_blocks(normed_two_own)
-    (normed_two, activated, coef), keep, give = ffn_forward(
-        normed_two_blocks, gate_up, down_rows, cuts
-    )
+    normed_two, coef, activated = ffn_units(plane_blocks(normed_two_own), gate_up, cuts)
+    keep, give = ffn_forward(activated, after(down_rows, activated), C)
     output = middle + plane_reduce(keep, give)
 
     valid_rows = (positions < seq_length).astype(f32)
@@ -1151,10 +1168,10 @@
     )
 
     out_keep, out_give = out_grads(attended_tokens, after(m_low, pairs), p, C, Z)
-    mine = [pairs[0]] + together([partner(pairs[s], "ctx", 2 * s) for s in range(1, R)])
+    out_chips = chip_sums(out_keep, out_give)
+    mine = [partner(pairs[s], "ctx", 2 * s) for s in range(1, R)]
+    mine = [pairs[0]] + list(after(mine, out_chips))
     other = [partner(x, "ctx", 1) for x in mine]
-    out_chips = chip_sums(out_keep, out_give)
-    mine = after(mine, out_chips)
     grad_qkv, gain_part, keep, give = attention_backward(
         mine, other, (normed_all, *saved), tables, p, seq_length, q_heads, kv_heads
     )

time: 425 us -> 412 us (0.969)
  waiting for transfers between devices: 203 us -> 183 us
    all_gather x1, waiting for transfers between devices: 26.6 us -> 0.01 us  [local(): gate_up = lax.all_gather(gate_up_own, 'fsdp', axis=0, tiled=True)]
    all_gather x1, waiting for transfers between devices: 0.01 us -> 14.5 us  [local(): down_rows = lax.all_gather(down_own, 'fsdp', axis=0, tiled=True)]
    ppermute x106, waiting for transfers between devices: 176 us -> 168 us  [partner(): lax.ppermute(x, axis, [(i, i ^ mask) for i in range(lax.axis_size(axis))])]
    pallas_call x1 -> x2, Pallas kernels: 9.59 us -> 11.9 us  [the longest x1 8.33 us: ffn_units(): pl.pallas_call(functools.partial(ffn_units_kernel, C, cuts), out_shape=[p...]
    unnamed x116 -> x112, local copies, waits for them, and re-layouts: 9.65 us -> 10.7 us
  transfers between devices with their start and end apart: 111 -> 111, of which waited for: 49 -> 48; matrix products, arithmetic and copies ran while one was open for 7% -> 7% of each run, Pallas kernels for 13% -> 15%
where the time goes in v2:
time: 412 us; the launch traced here: 407 us
  waiting for transfers between devices  183 us (44%)
  Pallas kernels  82.1 us (20%)
  starting transfers between devices  78 us (19%)
  other arithmetic  21.6 us (5%)
  local copies, waits for them, and re-layouts  16.3 us (4%)
  between operations  15.9 us (4%)
  matrix products  10.6 us (3%)
    ppermute x106, waiting for transfers between devices, partner(): lax.ppermute(x, axis, [(i, i ^ mask) for i in range(lax.axis_size(axis))])  168 us
    ppermute x106, starting transfers between devices, partner(): lax.ppermute(x, axis, [(i, i ^ mask) for i in range(lax.axis_size(axis))])  77.1 us
    pallas_call x1, Pallas kernels, attention_backward(): pl.pallas_call(functools.partial(attention_backward_kernel, C, tokens, q_...  14.6 us
    all_gather x1, waiting for transfers between devices, local(): down_rows = lax.all_gather(down_own, 'fsdp', axis=0, tiled=True)  14.5 us
    pallas_call x1, Pallas kernels, attention_forward(): pl.pallas_call(functools.partial(attention_forward_kernel, C, Z, tokens,...  11.8 us
    unnamed x112, local copies, waits for them, and re-layouts  10.7 us
    dot_general x2, matrix products, transposed_times(): lax.dot_general(left, right, (((0,), (0,)), ((), ())), preferred_element_...  10.6 us
    pallas_call x1, Pallas kernels, ffn_units(): pl.pallas_call(functools.partial(ffn_units_kernel, C, cuts), out_shape=[p...  8.33 us
  transfers between devices with their start and end apart: 111, of which 48 were waited for; matrix products, arithmetic and copies ran while one was open for 7% of the time, Pallas kernels for 15%

profile of v2, /device:TPU:0, one launch (start us, length us, event | category | flops | bytes accessed | tf_op | source)
XLA Modules:
  0.0 407.2 jit_solution(7498518280456055442)
XLA Ops:
  17.5 3.5 collective-permute-start.8
  26.1 4.2 %collective-permute-done.7.refs_9_ = bf16[384,384]{1,0:T(8,128)(2,1)} collective-permute-done((bf16[384,384]{1,0:T(8,128)(2,1)S(1)}, bf16[384,384]{1,0:T(8,128)(2,1)}, u32[]{:S(2)}, u32[]{:S(2)}) %collective-permute-start.7) | collective-permute-done | bytes 294944 | tf_op jit(solution)/shard_map/ppermute | solution.py:67
  45.0 4.8 %collective-permute-start.13 = (bf16[48,1536]{1,0:T(8,128)(2,1)}, bf16[48,1536]{1,0:T(8,128)(2,1)}, u32[]{:S(2)}, u32[]{:S(2)}) collective-permute-start(bf16[48,1536]{1,0:T(8,128)(2,1)} %constant_dynamic-slice_fusion), channel_id=1, source_target_pairs={{0,1},{1,0},{2,3},{3,2},{4,5},{5,4},{6,7},{7,6},{8,9},{9,8},{10,11... | collective-permute-start | bytes 442376 | tf_op jit(solution)/shard_map/ppermute | solution.py:67
  52.9 11.8 %attention_forward.1 = (bf16[1024,1536]{1,0:T(8,128)(2,1)}, bf16[1536,384]{1,0:T(8,128)(2,1)}, bf16[1024,512]{1,0:T(8,128)(2,1)}, f32[1024,256]{1,0:T(8,128)}, f...) custom-call(s32[3]{0:T(128)S(1)} %pad_add_fusion.1.info_ref, ...), custom_call_target="tpu_custom_call" | custom-call | flops 1 | bytes 1 | tf_op jit(solution)/shard_map/attention_forward/pallas_call | solution.py:287
  64.7 4.8 %collective-permute-done.14 = bf16[48,1536]{1,0:T(8,128)(2,1)} collective-permute-done((bf16[48,1536]{1,0:T(8,128)(2,1)}, bf16[48,1536]{1,0:T(8,128)(2,1)}, u32[]{:S(2)}, u32[]{:S(2)}) %collective-permute-start.14) | collective-permute-done | bytes 147488 | tf_op jit(solution)/shard_map/ppermute | solution.py:67
  75.9 9.1 %collective-permute-done.17.refs_10_ = bf16[144,1536]{1,0:T(8,128)(2,1)S(1)} collective-permute-done((bf16[144,1536]{1,0:T(8,128)(2,1)S(1)}, bf16[144,1536]{1,0:T(8,128)(2,1)S(1)}, u32[]{:S(2)}, u32[]{:S(2)}) %collective-permute-start.17) | collective-permute-done | bytes 442400 | tf_op jit(solution)/shard_map/ppermute | solution.py:67
  85.0 6.0 %collective-permute-done.18.refs_12_ = bf16[144,1536]{1,0:T(8,128)(2,1)S(1)} collective-permute-done((bf16[144,1536]{1,0:T(8,128)(2,1)S(1)}, bf16[144,1536]{1,0:T(8,128)(2,1)S(1)}, u32[]{:S(2)}, u32[]{:S(2)}) %collective-permute-start.18) | collective-permute-done | bytes 442400 | tf_op jit(solution)/shard_map/ppermute | solution.py:67
  105.1 4.2 %middle_forward.1 = (f32[128,1536]{1,0:T(8,128)S(1)}, bf16[128,1536]{1,0:T(8,128)(2,1)S(1)}, bf16[128,1536]{1,0:T(8,128)(2,1)S(1)}, bf16[1536,1536]{1,0:T(8,128)(2,1)}) custom-call(s32[2]{0:T(128)S(1)} %pad_add_fusion.info_ref, bf16[256,192]{1,0:T(8,128)(2,1)S(1)} %get-tuple-element.229.refs_0_, bf16[256,192]{1,0:T(8,128)(2,1)S(1)} %collective-permute-done.23.refs_1_, ...), custom_call_target="tpu_custom_call" | custom-call | flops 1 | bytes 1 | tf_op jit(solution)/shard_map/middle_forward/pallas_call | solution.py:764
  113.5 8.5 %collective-permute-done.31.refs_2_ = bf16[128,1536]{1,0:T(8,128)(2,1)S(1)} collective-permute-done((bf16[128,1536]{1,0:T(8,128)(2,1)S(1)}, bf16[128,1536]{1,0:T(8,128)(2,1)S(1)}, u32[]{:S(2)}, u32[]{:S(2)}) %collective-permute-start.31) | collective-permute-done | bytes 393248 | tf_op jit(solution)/shard_map/ppermute | solution.py:67
  122.0 8.3 %collective-permute-done.33.refs_4_ = bf16[128,1536]{1,0:T(8,128)(2,1)S(1)} collective-permute-done((bf16[128,1536]{1,0:T(8,128)(2,1)S(1)}, bf16[128,1536]{1,0:T(8,128)(2,1)S(1)}, u32[]{:S(2)}, u32[]{:S(2)}) %collective-permute-start.33) | collective-permute-done | bytes 393248 | tf_op jit(solution)/shard_map/ppermute | solution.py:67
  132.8 8.3 %ffn_units.1 = (bf16[1024,1536]{1,0:T(8,128)(2,1)}, bf16[1024,1024]{1,0:T(8,128)(2,1)}, bf16[1024,512]{1,0:T(8,128)(2,1)S(1)}) custom-call(bf16[128,1536]{1,0:T(8,128)(2,1)} %copy-done.8, bf16[128,1536]{1,0:T(8,128)(2,1)} %copy-done.36, bf16[128,1536]{1,0:T(8,128)(2,1)} %copy-done.32, bf16[128,1536]{1,0:T(8,128)(2,1)} %copy-done.37, ...), custom_call_target="tpu_custom_call" | custom-call | flops 1 | bytes 1 | tf_op jit(solution)/shard_map/ffn_units/pallas_call | solution.py:484
  141.1 14.5 %all-gather.5.cloned.1.call-done.down_hbm.refs_9_ = bf16[512,1536]{1,0:T(8,128)(2,1)} async-done(((bf16[128,1536]{1,0:T(8,128)(2,1)}), bf16[512,1536]{1,0:T(8,128)(2,1)}) %all-gather.5.cloned.1.call-update) | async-done | bytes 1572880 | tf_op jit(solution)/shard_map/all_gather | solution.py:1133
  155.6 3.5 ffn_forward.1
  168.2 5.8 %collective-permute-done.43 = bf16[128,1536]{1,0:T(8,128)(2,1)} collective-permute-done((bf16[128,1536]{1,0:T(8,128)(2,1)}, bf16[128,1536]{1,0:T(8,128)(2,1)}, u32[]{:S(2)}, u32[]{:S(2)}) %collective-permute-start.43) | collective-permute-done | bytes 393248 | tf_op jit(solution)/shard_map/ppermute | solution.py:67
  174.1 9.7 %collective-permute-done.41 = bf16[128,1536]{1,0:T(8,128)(2,1)} collective-permute-done((bf16[128,1536]{1,0:T(8,128)(2,1)}, bf16[128,1536]{1,0:T(8,128)(2,1)}, u32[]{:S(2)}, u32[]{:S(2)}) %collective-permute-start.41) | collective-permute-done | bytes 393248 | tf_op jit(solution)/shard_map/ppermute | solution.py:67
  190.4 8.6 %collective-permute-done.45.refs_2_ = bf16[128,1536]{1,0:T(8,128)(2,1)S(1)} collective-permute-done((bf16[128,1536]{1,0:T(8,128)(2,1)S(1)}, bf16[128,1536]{1,0:T(8,128)(2,1)S(1)}, u32[]{:S(2)}, u32[]{:S(2)}) %collective-permute-start.45) | collective-permute-done | bytes 393248 | tf_op jit(solution)/shard_map/ppermute | solution.py:67
  199.0 5.4 %collective-permute-done.47.refs_4_ = bf16[128,1536]{1,0:T(8,128)(2,1)S(1)} collective-permute-done((bf16[128,1536]{1,0:T(8,128)(2,1)S(1)}, bf16[128,1536]{1,0:T(8,128)(2,1)S(1)}, u32[]{:S(2)}, u32[]{:S(2)}) %collective-permute-start.47) | collective-permute-done | bytes 393248 | tf_op jit(solution)/shard_map/ppermute | solution.py:67
  208.0 8.0 %ffn_backward.1 = (bf16[1024,1536]{1,0:T(8,128)(2,1)S(1)}, bf16[1024,1024]{1,0:T(8,128)(2,1)S(1)}, bf16[128,1536]{1,0:T(8,128)(2,1)S(1)}, bf16[128,1536]{1,0:T(8...) custom-call(bf16[128,1536]{1,0:T(8,128)(2,1)S(1)} %get-tuple-element, ...), custom_call_target="tpu_custom_call" | custom-call | flops 1 | bytes 1 | tf_op jit(solution)/shard_map/ffn_backward/pallas_call | solution.py:559
  220.8 4.8 %convolution_convert_fusion = bf16[1536,1024]{1,0:T(8,128)(2,1)} fusion(bf16[1024,1536]{1,0:T(8,128)(2,1)S(1)} %copy-done.53, bf16[1024,1024]{1,0:T(8,128)(2,1)S(1)} %get-tuple-element.271), kind=kOutput, calls=%fused_computation | convolution fusion | flops 3222798336 | bytes 8388608 | tf_op jit(solution)/shard_map/dot_general | solution.py:52
  229.3 5.8 %convolution_convert_fusion.1 = bf16[512,1536]{1,0:T(8,128)(2,1)} fusion(bf16[1024,512]{1,0:T(8,128)(2,1)} %copy-done.3, bf16[1024,1536]{1,0:T(8,128)(2,1)} %copy-done.11), kind=kOutput, calls=%fused_computation.1 | convolution fusion | flops 1611399168 | bytes 5767168 | tf_op jit(solution)/shard_map/dot_general | solution.py:52
  238.8 7.8 %collective-permute-done.55.refs_2_ = bf16[128,1536]{1,0:T(8,128)(2,1)} collective-permute-done((bf16[128,1536]{1,0:T(8,128)(2,1)}, bf16[128,1536]{1,0:T(8,128)(2,1)}, u32[]{:S(2)}, u32[]{:S(2)}) %collective-permute-start.55) | collective-permute-done | bytes 393248 | tf_op jit(solution)/shard_map/ppermute | solution.py:67
  247.6 5.2 %middle_backward.1 = (f32[128,1536]{1,0:T(8,128)S(1)}, bf16[128,1536]{1,0:T(8,128)(2,1)S(1)}, f32[1,1536]{1,0:T(1,128)S(1)}, bf16[128,384]{1,0:T(8,128)(2,1)S(1)...) custom-call(s32[1]{0:T(128)} %bitcast.me_ref.info_ref, ...), custom_call_target="tpu_custom_call" | custom-call | flops 1 | bytes 1 | tf_op jit(solution)/shard_map/middle_backward/pallas_call | solution.py:822
  268.3 14.6 %attention_backward.1 = (bf16[1536,384]{1,0:T(8,128)(2,1)S(1)}, f32[8,1536]{1,0:T(8,128)S(1)}, bf16[128,1536]{1,0:T(8,128)(2,1)S(1)}, bf16[128,1536]{1,0:T(8,128...) custom-call(s32[2]{0:T(128)S(1)} %pad_add_fusion.2.info_ref, ...), custom_call_target="tpu_custom_call" | custom-call | flops 1 | bytes 1 | tf_op jit(solution)/shard_map/attention_backward/pallas_call | solution.py:404
  283.0 8.0 %collective-permute-done.61.refs_3_ = bf16[192,1536]{1,0:T(8,128)(2,1)S(1)} collective-permute-done((bf16[192,1536]{1,0:T(8,128)(2,1)S(1)}, bf16[192,1536]{1,0:T(8,128)(2,1)S(1)}, u32[]{:S(2)}, u32[]{:S(2)}) %collective-permute-start.61) | collective-permute-done | bytes 589856 | tf_op jit(solution)/shard_map/ppermute | solution.py:67
  304.3 23.0 %collective-permute-done.76 = bf16[128,1536]{1,0:T(8,128)(2,1)S(1)} collective-permute-done((bf16[128,1536]{1,0:T(8,128)(2,1)S(1)}, bf16[128,1536]{1,0:T(8,128)(2,1)S(1)}, u32[]{:S(2)}, u32[]{:S(2)}) %collective-permute-start.76) | collective-permute-done | bytes 393248 | tf_op jit(solution)/shard_map/ppermute | solution.py:67
  327.3 8.0 %collective-permute-done.77 = bf16[128,1536]{1,0:T(8,128)(2,1)S(1)} collective-permute-done((bf16[128,1536]{1,0:T(8,128)(2,1)}, bf16[128,1536]{1,0:T(8,128)(2,1)S(1)}, u32[]{:S(2)}, u32[]{:S(2)}) %collective-permute-start.77) | collective-permute-done | bytes 393248 | tf_op jit(solution)/shard_map/ppermute | solution.py:67
  340.7 7.0 %collective-permute-done.83.refs_2_ = bf16[128,1536]{1,0:T(8,128)(2,1)S(1)} collective-permute-done((bf16[128,1536]{1,0:T(8,128)(2,1)}, bf16[128,1536]{1,0:T(8,128)(2,1)S(1)}, u32[]{:S(2)}, u32[]{:S(2)}) %collective-permute-start.83) | collective-permute-done | bytes 393248 | tf_op jit(solution)/shard_map/ppermute | solution.py:67
  349.1 8.1 %collective-permute-done.81.refs_6_ = bf16[192,1024]{1,0:T(8,128)(2,1)} collective-permute-done((bf16[192,1024]{1,0:T(8,128)(2,1)S(1)}, bf16[192,1024]{1,0:T(8,128)(2,1)}, u32[]{:S(2)}, u32[]{:S(2)}) %collective-permute-start.81) | collective-permute-done | bytes 393248 | tf_op jit(solution)/shard_map/ppermute | solution.py:67
  361.7 3.8 collective-permute-done.85.refs_6_
  370.9 7.3 %column_grads.1 = (f32[384,4096]{1,0:T(8,128)}, f32[384,4096]{1,0:T(8,128)}) custom-call(s32[1]{0:T(128)} %bitcast.me_ref.info_ref, bf16[384,1024]{1,0:T(8,128)(2,1)} %reduce-scatter.6.cloned.1.call-done.refs_0_, bf16[384,1024]{1,0:T(8,128)(2,1)} %copy-done.24, bf16[384,1024]{1,0:T(8,128)(2,1)} %copy-done.16, ...), custom_call_target="tpu_custom_call" | custom-call | flops 1 | bytes 1 | tf_op jit(solution)/shard_map/column_grads/pallas_call | solution.py:656
  385.3 4.0 row_grads.1
  392.3 7.5 %attention_grads.1 = (f32[384,1536]{1,0:T(8,128)}, f32[384,768]{1,0:T(8,128)}, f32[384,768]{1,0:T(8,128)}, f32[384,1536]{1,0:T(8,128)}, f32[8,384]{1,0:T(8,128)S(1)}, /*index=5*/f32[1,1]{1,0:T(1,128)}) custom-call(s32[1]{0:T(128)} %bitcast.me_ref.info_ref, bf16[592,384]{1,0:T(8,128)(2,1)} %reduce-scatter.4.cloned.1.call-done.refs_0_, ...), custom_call_target="tpu_custom_call" | custom-call | flops 1 | bytes 1 | tf_op jit(solution)/shard_map/attention_grads/pallas_call | solution.py:1026
  (377 shorter events, 147.5 us)
Async XLA Ops:
  7.2 125.6 %all-gather.3.cloned.1.call-start = ((), (), s32[]{:S(2)}) async-start(), calls=%async_computation.3 | async-start | bytes 3932160 | tf_op jit(solution)/shard_map/all_gather | solution.py:1132
  17.5 24.1 %collective-permute-start.8 = (bf16[384,384]{1,0:T(8,128)(2,1)S(1)}, bf16[384,384]{1,0:T(8,128)(2,1)S(1)}, u32[]{:S(2)}, u32[]{:S(2)}) collective-permute-start(bf16[384,384]{1,0:T(8,128)(2,1)S(1)} %pad_maximum_fusion.refs_8_), channel_id=1, source_target_pairs={{0,2},{1,3},{2,0},{3,1},{4,6},{5,7},{6,4},{7,5},{8,10},{9,11},{10,... | collective-permute-start | bytes 884744 | tf_op jit(solution)/shard_map/ppermute | solution.py:67
  21.7 19.9 %collective-permute-start.9 = (bf16[384,384]{1,0:T(8,128)(2,1)S(1)}, bf16[384,384]{1,0:T(8,128)(2,1)S(1)}, u32[]{:S(2)}, u32[]{:S(2)}) collective-permute-start(bf16[384,384]{1,0:T(8,128)(2,1)S(1)} %pad_maximum_fusion.refs_8_), channel_id=1, source_target_pairs={{0,3},{1,2},{2,1},{3,0},{4,7},{5,6},{6,5},{7,4},{8,11},{9,10},{10,... | collective-permute-start | bytes 884744 | tf_op jit(solution)/shard_map/ppermute | solution.py:67
  23.0 18.6 %collective-permute-start.4 = (bf16[128,1536]{1,0:T(8,128)(2,1)S(1)}, bf16[128,1536]{1,0:T(8,128)(2,1)S(1)}, u32[]{:S(2)}, u32[]{:S(2)}) collective-permute-start(bf16[128,1536]{1,0:T(8,128)(2,1)S(1)} %multiply_convert_fusion.refs_0_), channel_id=1, source_target_pairs={{0,8},{4,12},{8,0},{12,4},{16,24},{20,28},{24,16},{28,20},{1,9},{5... | collective-permute-start | bytes 1179656 | tf_op jit(solution)/shard_map/ppermute | solution.py:67
  24.6 17.2 %collective-permute-start.5 = (bf16[128,1536]{1,0:T(8,128)(2,1)S(1)}, bf16[128,1536]{1,0:T(8,128)(2,1)S(1)}, u32[]{:S(2)}, u32[]{:S(2)}) collective-permute-start(bf16[128,1536]{1,0:T(8,128)(2,1)S(1)} %multiply_convert_fusion.refs_0_), channel_id=1, source_target_pairs={{0,16},{4,20},{8,24},{12,28},{16,0},{20,4},{24,8},{28,12},{1,17},{... | collective-permute-start | bytes 1179656 | tf_op jit(solution)/shard_map/ppermute | solution.py:67
  42.4 113.2 %all-gather.5.cloned.1.call-start = ((), (), s32[]{:S(2)}) async-start(), calls=%async_computation.4 | async-start | bytes 1966080 | tf_op jit(solution)/shard_map/all_gather | solution.py:1133
  45.0 19.8 %collective-permute-start.13 = (bf16[48,1536]{1,0:T(8,128)(2,1)}, bf16[48,1536]{1,0:T(8,128)(2,1)}, u32[]{:S(2)}, u32[]{:S(2)}) collective-permute-start(bf16[48,1536]{1,0:T(8,128)(2,1)} %constant_dynamic-slice_fusion), channel_id=1, source_target_pairs={{0,1},{1,0},{2,3},{3,2},{4,5},{5,4},{6,7},{7,6},{8,9},{9,8},{10,11... | collective-permute-start | bytes 442376 | tf_op jit(solution)/shard_map/ppermute | solution.py:67
  49.8 19.8 %collective-permute-start.14 = (bf16[48,1536]{1,0:T(8,128)(2,1)}, bf16[48,1536]{1,0:T(8,128)(2,1)}, u32[]{:S(2)}, u32[]{:S(2)}) collective-permute-start(bf16[48,1536]{1,0:T(8,128)(2,1)} %constant_dynamic-slice_fusion), channel_id=1, source_target_pairs={{0,2},{1,3},{2,0},{3,1},{4,6},{5,7},{6,4},{7,5},{8,10},{9,11},{10,... | collective-permute-start | bytes 442376 | tf_op jit(solution)/shard_map/ppermute | solution.py:67
  50.7 18.9 %collective-permute-start.15 = (bf16[48,1536]{1,0:T(8,128)(2,1)}, bf16[48,1536]{1,0:T(8,128)(2,1)}, u32[]{:S(2)}, u32[]{:S(2)}) collective-permute-start(bf16[48,1536]{1,0:T(8,128)(2,1)} %constant_dynamic-slice_fusion), channel_id=1, source_target_pairs={{0,3},{1,2},{2,1},{3,0},{4,7},{5,6},{6,5},{7,4},{8,11},{9,10},{10,... | collective-permute-start | bytes 442376 | tf_op jit(solution)/shard_map/ppermute | solution.py:67
  52.3 246.0 %reduce-scatter.6.cloned.1.call-start = ((), (), s32[]{:S(2)}) async-start(), calls=%async_computation.6 | async-start | bytes 3932160 | tf_op jit(solution)/shard_map/reduce_scatter | solution.py:1164
  110.9 19.4 %collective-permute-start.33 = (bf16[128,1536]{1,0:T(8,128)(2,1)S(1)}, bf16[128,1536]{1,0:T(8,128)(2,1)S(1)}, u32[]{:S(2)}, u32[]{:S(2)}) collective-permute-start(bf16[128,1536]{1,0:T(8,128)(2,1)S(1)} %get-tuple-element.237.refs_0_), channel_id=1, source_target_pairs={{0,16},{4,20},{8,24},{12,28},{16,0},{20,4},{24,8},{28,12},{1,17},{... | collective-permute-start | bytes 1179656 | tf_op jit(solution)/shard_map/ppermute | solution.py:67
  112.3 18.0 %collective-permute-start.35 = (bf16[128,1536]{1,0:T(8,128)(2,1)S(1)}, bf16[128,1536]{1,0:T(8,128)(2,1)S(1)}, u32[]{:S(2)}, u32[]{:S(2)}) collective-permute-start(bf16[128,1536]{1,0:T(8,128)(2,1)S(1)} %get-tuple-element.237.refs_0_), channel_id=1, source_target_pairs={{0,24},{4,28},{8,16},{12,20},{16,8},{20,12},{24,0},{28,4},{1,25},{... | collective-permute-start | bytes 1179656 | tf_op jit(solution)/shard_map/ppermute | solution.py:67
  113.5 17.3 %collective-permute-start.30 = (bf16[128,1536]{1,0:T(8,128)(2,1)S(1)}, bf16[128,1536]{1,0:T(8,128)(2,1)S(1)}, u32[]{:S(2)}, u32[]{:S(2)}) collective-permute-start(bf16[128,1536]{1,0:T(8,128)(2,1)S(1)} %get-tuple-element.237.refs_0_), channel_id=1, source_target_pairs={{0,4},{4,0},{8,12},{12,8},{16,20},{20,16},{24,28},{28,24},{1,5},{5... | collective-permute-start | bytes 1179656 | tf_op jit(solution)/shard_map/ppermute | solution.py:67
  164.1 19.6 %collective-permute-start.41 = (bf16[128,1536]{1,0:T(8,128)(2,1)}, bf16[128,1536]{1,0:T(8,128)(2,1)}, u32[]{:S(2)}, u32[]{:S(2)}) collective-permute-start(bf16[128,1536]{1,0:T(8,128)(2,1)} %add_convert_fusion.10), channel_id=1, source_target_pairs={{0,16},{4,20},{8,24},{12,28},{16,0},{20,4},{24,8},{28,12},{1,17},{... | collective-permute-start | bytes 1179656 | tf_op jit(solution)/shard_map/ppermute | solution.py:67
  166.4 17.3 %collective-permute-start.39 = (bf16[128,1536]{1,0:T(8,128)(2,1)}, bf16[128,1536]{1,0:T(8,128)(2,1)S(1)}, u32[]{:S(2)}, u32[]{:S(2)}) collective-permute-start(bf16[128,1536]{1,0:T(8,128)(2,1)} %add_convert_fusion.11), channel_id=1, source_target_pairs={{0,24},{4,28},{8,16},{12,20},{16,8},{20,12},{24,0},{28,4},{1,25},{... | collective-permute-start | bytes 1179656 | tf_op jit(solution)/shard_map/ppermute | solution.py:67
  189.0 17.3 %collective-permute-start.49 = (bf16[128,1536]{1,0:T(8,128)(2,1)S(1)}, bf16[128,1536]{1,0:T(8,128)(2,1)S(1)}, u32[]{:S(2)}, u32[]{:S(2)}) collective-permute-start(bf16[128,1536]{1,0:T(8,128)(2,1)S(1)} %get-tuple-element.370.refs_0_), channel_id=1, source_target_pairs={{0,24},{4,28},{8,16},{12,20},{16,8},{20,12},{24,0},{28,4},{1,25},{... | collective-permute-start | bytes 1179656 | tf_op jit(solution)/shard_map/ppermute | solution.py:67
  225.7 109.7 %reduce-scatter.8.cloned.1.call-start = ((), (), s32[]{:S(2)}) async-start(), calls=%async_computation.7 | async-start | bytes 1966080 | tf_op jit(solution)/shard_map/reduce_scatter | solution.py:1165
  226.9 19.6 %collective-permute-start.55 = (bf16[128,1536]{1,0:T(8,128)(2,1)}, bf16[128,1536]{1,0:T(8,128)(2,1)}, u32[]{:S(2)}, u32[]{:S(2)}) collective-permute-start(bf16[128,1536]{1,0:T(8,128)(2,1)} %add_convert_fusion.7), channel_id=1, source_target_pairs={{0,16},{4,20},{8,24},{12,28},{16,0},{20,4},{24,8},{28,12},{1,17},{... | collective-permute-start | bytes 1179656 | tf_op jit(solution)/shard_map/ppermute | solution.py:67
  228.7 17.9 %collective-permute-start.53 = (bf16[128,1536]{1,0:T(8,128)(2,1)}, bf16[128,1536]{1,0:T(8,128)(2,1)}, u32[]{:S(2)}, u32[]{:S(2)}) collective-permute-start(bf16[128,1536]{1,0:T(8,128)(2,1)} %add_convert_fusion.8), channel_id=1, source_target_pairs={{0,24},{4,28},{8,16},{12,20},{16,8},{20,12},{24,0},{28,4},{1,25},{... | collective-permute-start | bytes 1179656 | tf_op jit(solution)/shard_map/ppermute | solution.py:67
  235.1 130.3 %reduce-scatter.4.cloned.1.call-start = ((), (), s32[]{:S(2)}) async-start(), calls=%async_computation.5 | async-start | bytes 2273280 | tf_op jit(solution)/shard_map/reduce_scatter | solution.py:1184
  261.6 21.4 %collective-permute-start.63 = (bf16[192,1536]{1,0:T(8,128)(2,1)S(1)}, bf16[192,1536]{1,0:T(8,128)(2,1)S(1)}, u32[]{:S(2)}, u32[]{:S(2)}) collective-permute-start(bf16[192,1536]{1,0:T(8,128)(2,1)S(1)} %add_convert_fusion), channel_id=1, source_target_pairs={{0,8},{4,12},{8,0},{12,4},{16,24},{20,28},{24,16},{28,20},{1,9},{5... | collective-permute-start | bytes 1769480 | tf_op jit(solution)/shard_map/ppermute | solution.py:67
  263.2 27.8 %collective-permute-start.61 = (bf16[192,1536]{1,0:T(8,128)(2,1)S(1)}, bf16[192,1536]{1,0:T(8,128)(2,1)S(1)}, u32[]{:S(2)}, u32[]{:S(2)}) collective-permute-start(bf16[192,1536]{1,0:T(8,128)(2,1)S(1)} %add_convert_fusion.1), channel_id=1, source_target_pairs={{0,16},{4,20},{8,24},{12,28},{16,0},{20,4},{24,8},{28,12},{1,17},{... | collective-permute-start | bytes 1769480 | tf_op jit(solution)/shard_map/ppermute | solution.py:67
  263.9 27.1 %collective-permute-start.59 = (bf16[192,1536]{1,0:T(8,128)(2,1)S(1)}, bf16[192,1536]{1,0:T(8,128)(2,1)S(1)}, u32[]{:S(2)}, u32[]{:S(2)}) collective-permute-start(bf16[192,1536]{1,0:T(8,128)(2,1)S(1)} %add_convert_fusion.2), channel_id=1, source_target_pairs={{0,24},{4,28},{8,16},{12,20},{16,8},{20,12},{24,0},{28,4},{1,25},{... | collective-permute-start | bytes 1769480 | tf_op jit(solution)/shard_map/ppermute | solution.py:67
  298.3 37.0 %collective-permute-start.79 = (bf16[384,1024]{1,0:T(8,128)(2,1)}, bf16[384,1024]{1,0:T(8,128)(2,1)S(1)}, u32[]{:S(2)}, u32[]{:S(2)}) collective-permute-start(bf16[384,1024]{1,0:T(8,128)(2,1)} %reduce-scatter.6.cloned.1.call-done.refs_0_), channel_id=1, source_target_pairs={{0,8},{4,12},{8,0},{12,4},{16,24},{20,28},{24,16},{28,20},{1,9},{5... | collective-permute-start | bytes 2359304 | tf_op jit(solution)/shard_map/ppermute | solution.py:67
  298.9 36.4 %collective-permute-start.80 = (bf16[384,1024]{1,0:T(8,128)(2,1)}, bf16[384,1024]{1,0:T(8,128)(2,1)}, u32[]{:S(2)}, u32[]{:S(2)}) collective-permute-start(bf16[384,1024]{1,0:T(8,128)(2,1)} %reduce-scatter.6.cloned.1.call-done.refs_0_), channel_id=1, source_target_pairs={{0,16},{4,20},{8,24},{12,28},{16,0},{20,4},{24,8},{28,12},{1,17},{... | collective-permute-start | bytes 2359304 | tf_op jit(solution)/shard_map/ppermute | solution.py:67
  300.8 26.6 %collective-permute-start.76 = (bf16[128,1536]{1,0:T(8,128)(2,1)S(1)}, bf16[128,1536]{1,0:T(8,128)(2,1)S(1)}, u32[]{:S(2)}, u32[]{:S(2)}) collective-permute-start(bf16[128,1536]{1,0:T(8,128)(2,1)S(1)} %add_convert_fusion.5), channel_id=1, source_target_pairs={{0,8},{4,12},{8,0},{12,4},{16,24},{20,28},{24,16},{28,20},{1,9},{5... | collective-permute-start | bytes 1179656 | tf_op jit(solution)/shard_map/ppermute | solution.py:67
  301.2 34.1 %collective-permute-start.77 = (bf16[128,1536]{1,0:T(8,128)(2,1)}, bf16[128,1536]{1,0:T(8,128)(2,1)S(1)}, u32[]{:S(2)}, u32[]{:S(2)}) collective-permute-start(bf16[128,1536]{1,0:T(8,128)(2,1)} %add_convert_fusion.4), channel_id=1, source_target_pairs={{0,16},{4,20},{8,24},{12,28},{16,0},{20,4},{24,8},{28,12},{1,17},{... | collective-permute-start | bytes 1179656 | tf_op jit(solution)/shard_map/ppermute | solution.py:67
  302.5 32.8 %collective-permute-start.78 = (bf16[128,1536]{1,0:T(8,128)(2,1)}, bf16[128,1536]{1,0:T(8,128)(2,1)}, u32[]{:S(2)}, u32[]{:S(2)}) collective-permute-start(bf16[128,1536]{1,0:T(8,128)(2,1)} %add_convert_fusion.3), channel_id=1, source_target_pairs={{0,24},{4,28},{8,16},{12,20},{16,8},{20,12},{24,0},{28,4},{1,25},{... | collective-permute-start | bytes 1179656 | tf_op jit(solution)/shard_map/ppermute | solution.py:67
  336.9 22.1 %collective-permute-start.89 = (bf16[384,1024]{1,0:T(8,128)(2,1)}, bf16[384,1024]{1,0:T(8,128)(2,1)S(1)}, u32[]{:S(2)}, u32[]{:S(2)}) collective-permute-start(bf16[384,1024]{1,0:T(8,128)(2,1)} %reduce-scatter.6.cloned.1.call-done.refs_0_), channel_id=1, source_target_pairs={{0,4},{4,0},{8,12},{12,8},{16,20},{20,16},{24,28},{28,24},{1,5},{5... | collective-permute-start | bytes 2359304 | tf_op jit(solution)/shard_map/ppermute | solution.py:67
  337.5 19.7 %collective-permute-start.81 = (bf16[192,1024]{1,0:T(8,128)(2,1)S(1)}, bf16[192,1024]{1,0:T(8,128)(2,1)}, u32[]{:S(2)}, u32[]{:S(2)}) collective-permute-start(bf16[192,1024]{1,0:T(8,128)(2,1)S(1)} %slice.36), channel_id=1, source_target_pairs={{0,16},{4,20},{8,24},{12,28},{16,0},{20,4},{24,8},{28,12},{1,17},{... | collective-permute-start | bytes 1179656 | tf_op jit(solution)/shard_map/ppermute | solution.py:67
  340.1 17.1 %collective-permute-start.82 = (bf16[192,1024]{1,0:T(8,128)(2,1)S(1)}, bf16[192,1024]{1,0:T(8,128)(2,1)}, u32[]{:S(2)}, u32[]{:S(2)}) collective-permute-start(bf16[192,1024]{1,0:T(8,128)(2,1)S(1)} %slice.37), channel_id=1, source_target_pairs={{0,8},{4,12},{8,0},{12,4},{16,24},{20,28},{24,16},{28,20},{1,9},{5... | collective-permute-start | bytes 1179656 | tf_op jit(solution)/shard_map/ppermute | solution.py:67
  349.1 19.5 %collective-permute-start.90 = (bf16[384,1024]{1,0:T(8,128)(2,1)S(1)}, bf16[384,1024]{1,0:T(8,128)(2,1)}, u32[]{:S(2)}, u32[]{:S(2)}) collective-permute-start(bf16[384,1024]{1,0:T(8,128)(2,1)S(1)} %collective-permute-done.79.refs_2_), channel_id=1, source_target_pairs={{0,4},{4,0},{8,12},{12,8},{16,20},{20,16},{24,28},{28,24},{1,5},{5... | collective-permute-start | bytes 2359304 | tf_op jit(solution)/shard_map/ppermute | solution.py:67
  (133 other events, 976.1 us)
Sparse Core Ops, SparseCore 0:
  41.9 75.0 all-gather.2
  118.6 36.9 all-gather.4
  225.8 59.0 reduce-scatter.5
  287.6 35.3 reduce-scatter.7
  325.7 38.2 reduce-scatter.3

commit v3 on v2

--- a/solution.py
+++ b/solution.py
@@ -957,9 +957,9 @@
 
 def attention_grads_kernel(C, rows, q_cols, kv_cols, places, me_ref, *refs):
     count = len(places)
-    gain_ref, valid_ref = refs[count : count + 2]
-    *grads_hbm, gains_ref, loss_ref = refs[count + 2 : count + 8]
-    low_ref, extra_ref, query_ref, key_ref, value_ref, out_ref, in_sems, out_sems = refs[count + 8 :]
+    gain_ref, rows_gain_ref, valid_ref = refs[count : count + 3]
+    *grads_hbm, gains_ref, loss_ref = refs[count + 3 : count + 9]
+    low_ref, extra_ref, query_ref, key_ref, value_ref, out_ref, in_sems, out_sems = refs[count + 9 :]
     me = me_ref[0]
     cols = low_ref.shape[2]
     strips = out_ref.shape[1] // cols
@@ -992,7 +992,7 @@
         for group in range(C // many):
             whole = None
             for j in range(many):
-                x = low_ref[me ^ (group * many + j), :rows, :].astype(f32)
+                x = low_ref[me ^ (group * many + j), :rows, :].astype(f32) * rows_gain_ref[...]
                 shift = (j * size - first) % cols
                 x = pltpu.roll(x, shift, 1) if shift else x
                 whole = x if whole is None else jnp.where(lane < j * size, whole, x)
@@ -1011,11 +1011,11 @@
         parts = unsort([x[2] for x in pieces], me)
 
         def kv_final(start):
-            own = [part[:rows, start : start + kv_cols].astype(f32) for part in parts]
+            own = [part[:rows, start : start + kv_cols].astype(f32) * gain[:, None] for part in parts]
             own = [sum(own[n : n + kv_copies]) for n in range(0, C, kv_copies)]
             return jnp.concatenate(own, axis=1)
 
-        query = jnp.concatenate([part[:rows, :q_cols] for part in parts], axis=1).astype(f32)
+        query = jnp.concatenate([part[:rows, :q_cols] for part in parts], axis=1).astype(f32) * gain[:, None]
         outs = [part[rows : tall - EXTRA].reshape(strips, piece, cols).transpose(1, 0, 2) for part in parts]
         out = jnp.concatenate([x.reshape(piece, width) for x in outs], axis=0).astype(f32)
         extra = sum([part[tall - EXTRA :].astype(f32) for part in parts])
@@ -1032,7 +1032,7 @@
             jax.ShapeDtypeStruct((8, cols), f32),
             jax.ShapeDtypeStruct((1, 1), f32),
         ],
-        in_specs=[SMEM] + [HBM] * len(pieces) + [VMEM] * 2,
+        in_specs=[SMEM] + [HBM] * len(pieces) + [VMEM] * 3,
         out_specs=[HBM] * 4 + [VMEM] * 2,
         scratch_shapes=[
             pltpu.VMEM((C, tall, cols), bf16),
@@ -1048,6 +1048,7 @@
         me.reshape(1),
         *in_hbm(*[x[2] for x in pieces]),
         gain.reshape(1, rows),
+        gain.reshape(rows, 1),
         valid_count.reshape(1, 1),
     )
     return *grads, gains[0], gains[1], loss[0, 0]
@@ -1100,14 +1101,14 @@
     )
     out_own = lax.dynamic_slice_in_dim(w_out, p * out_piece, out_piece, 0)
 
+    qkv_own = (qkv_own.astype(f32) * gain_attn.astype(f32)[:, None]).astype(bf16)
+    scale_one = norm_scale(hidden_in)
+    normed_one = (hidden_in * scale_one).astype(bf16)
+
     small = jnp.concatenate(
         [gain_attn.astype(f32), gain_ffn.astype(f32), jnp.full((LANES,), seq_length).astype(f32)]
     )
-    small = after(small.reshape(1, -1), qkv_own)
-    small = jnp.stack(unsort(line_blocks(small), z)).reshape(Z, -1)
-    gain_one = small[:, :rows_z].reshape(width)
-    gain_two = small[:, rows_z : 2 * rows_z].reshape(width)
-    valid_count = jnp.sum(small[:, 2 * rows_z])
+    small = after(small.reshape(1, -1), qkv_own, normed_one)
     ff = w_gate.shape[1]
     ff_piece, own = ff // (Z * C), ff // C
     packed_ffn = ff_piece % LANES == 0
@@ -1121,8 +1122,6 @@
             axis=1,
         )
         down_own = lax.dynamic_slice_in_dim(w_down, p * ff_piece, ff_piece, 0)
-    scale_one = norm_scale(hidden_in)
-    normed_one = (hidden_in * scale_one * gain_one).astype(bf16)
     tables = rope_tables(seq)
     normed_got, weights, tables = lax.optimization_barrier(
         (plane_sends(normed_one), line_sends(qkv_own), tables)
@@ -1132,11 +1131,15 @@
     gate_up = lax.all_gather(gate_up_own, "fsdp", axis=0, tiled=True)
     down_rows = lax.all_gather(down_own, "fsdp", axis=0, tiled=True)
     out_line = line_sends(after(out_own, weights))
+    small_got = line_sends(after(small, weights))
     (normed_all, *saved), mine = attention_forward(
         normed_blocks, [qkv_own] + weights, tables, p, seq_length, z, q_heads, kv_heads
     )
 
-    out_line, normed_all = lax.optimization_barrier((out_line, normed_all))
+    out_line, small_got, normed_all = lax.optimization_barrier((out_line, small_got, normed_all))
+    small = jnp.stack(unsort([small] + small_got, z)).reshape(Z, -1)
+    gain_two = small[:, rows_z : 2 * rows_z].reshape(width)
+    valid_count = jnp.sum(small[:, 2 * rows_z])
     out_line = jnp.concatenate(out_line, axis=0)
     out_blocks = together(core_blocks([out_line] + together(plane_sends(out_line))))
     mine = after(mine, out_blocks)
@@ -1186,7 +1189,7 @@
     near = near_sends(after(shard_gate_up, out_got)) if square else []
     normed_got, near, token = lax.optimization_barrier((normed_got, near, token))
     grad_normed_one = total(chips[0], normed_got)
-    back_one, _ = norm_back(grad_normed_one, hidden_in, scale_one, gain_one)
+    back_one, _ = norm_back(grad_normed_one, hidden_in, scale_one, 1.0)
     grad_hidden = grad_middle + back_one
 
 

time: 412 us -> 411 us (level)
  waiting for transfers between devices: 183 us -> 174 us
    all_gather x1, waiting for transfers between devices: 14.5 us -> 2.05 us  [local(): down_rows = lax.all_gather(down_own, 'fsdp', axis=0, tiled=True)]
    unnamed x112 -> x130, local copies, waits for them, and re-layouts: 10.7 us -> 14.4 us
  transfers between devices with their start and end apart: 111 -> 111, of which waited for: 48 -> 46; matrix products, arithmetic and copies ran while one was open for 7% -> 7% of each run, Pallas kernels for 15% -> 16%
where the time goes in v3:
time: 411 us; the launch traced here: 406 us
  waiting for transfers between devices  174 us (42%)
  Pallas kernels  84.2 us (20%)
  starting transfers between devices  79.1 us (19%)
  other arithmetic  22.2 us (5%)
  local copies, waits for them, and re-layouts  20.1 us (5%)
  between operations  15.8 us (4%)
  matrix products  10 us (2%)
    ppermute x106, waiting for transfers between devices, partner(): lax.ppermute(x, axis, [(i, i ^ mask) for i in range(lax.axis_size(axis))])  172 us
    ppermute x106, starting transfers between devices, partner(): lax.ppermute(x, axis, [(i, i ^ mask) for i in range(lax.axis_size(axis))])  78.2 us
    pallas_call x1, Pallas kernels, attention_backward(): pl.pallas_call(functools.partial(attention_backward_kernel, C, tokens, q_...  14.6 us
    unnamed x130, local copies, waits for them, and re-layouts  14.4 us
    pallas_call x1, Pallas kernels, attention_forward(): pl.pallas_call(functools.partial(attention_forward_kernel, C, Z, tokens,...  11.7 us
    dot_general x2, matrix products, transposed_times(): lax.dot_general(left, right, (((0,), (0,)), ((), ())), preferred_element_...  10 us
    pallas_call x1, Pallas kernels, attention_grads(): pl.pallas_call(functools.partial(attention_grads_kernel, C, rows, q_cols,...  9 us
    pallas_call x1, Pallas kernels, ffn_units(): pl.pallas_call(functools.partial(ffn_units_kernel, C, cuts), out_shape=[p...  8.33 us
  transfers between devices with their start and end apart: 111, of which 46 were waited for; matrix products, arithmetic and copies ran while one was open for 7% of the time, Pallas kernels for 16%

profile of v3, /device:TPU:0, one launch (start us, length us, event | category | flops | bytes accessed | tf_op | source)
XLA Modules:
  0.0 405.7 jit_solution(3297599409064517362)
XLA Ops:
  21.0 4.7 %collective-permute-done.4.refs_9_ = bf16[384,384]{1,0:T(8,128)(2,1)S(1)} collective-permute-done((bf16[384,384]{1,0:T(8,128)(2,1)S(1)}, bf16[384,384]{1,0:T(8,128)(2,1)S(1)}, u32[]{:S(2)}, u32[]{:S(2)}) %collective-permute-start.4) | collective-permute-done | bytes 294944 | tf_op jit(solution)/shard_map/ppermute | solution.py:67
  39.5 5.1 %collective-permute-start.13 = (f32[1,896]{1,0:T(1,128)S(1)}, f32[1,896]{1,0:T(1,128)S(1)}, u32[]{:S(2)}, u32[]{:S(2)}) collective-permute-start(f32[1,896]{1,0:T(1,128)S(1)} %reshape.79), channel_id=1, source_target_pairs={{0,1},{1,0},{2,3},{3,2},{4,5},{5,4},{6,7},{7,6},{8,9},{9,8},{10,11... | collective-permute-start | bytes 10760 | tf_op jit(solution)/shard_map/ppermute | solution.py:67
  53.9 11.7 %attention_forward.1 = (bf16[1024,1536]{1,0:T(8,128)(2,1)}, bf16[1536,384]{1,0:T(8,128)(2,1)}, bf16[1024,512]{1,0:T(8,128)(2,1)}, f32[1024,256]{1,0:T(8,128)}, f...) custom-call(s32[3]{0:T(128)S(1)} %pad_add_fusion.1.info_ref, ...), custom_call_target="tpu_custom_call" | custom-call | flops 1 | bytes 1 | tf_op jit(solution)/shard_map/attention_forward/pallas_call | solution.py:287
  65.6 10.3 %collective-permute-done.14 = f32[1,896]{1,0:T(1,128)S(1)} collective-permute-done((f32[1,896]{1,0:T(1,128)S(1)}, f32[1,896]{1,0:T(1,128)S(1)}, u32[]{:S(2)}, u32[]{:S(2)}) %collective-permute-start.14) | collective-permute-done | bytes 3616 | tf_op jit(solution)/shard_map/ppermute | solution.py:67
  82.3 8.0 %collective-permute-done.17.refs_10_ = bf16[144,1536]{1,0:T(8,128)(2,1)S(1)} collective-permute-done((bf16[144,1536]{1,0:T(8,128)(2,1)S(1)}, bf16[144,1536]{1,0:T(8,128)(2,1)S(1)}, u32[]{:S(2)}, u32[]{:S(2)}) %collective-permute-start.17) | collective-permute-done | bytes 442400 | tf_op jit(solution)/shard_map/ppermute | solution.py:67
  90.3 5.9 %collective-permute-done.18.refs_12_ = bf16[144,1536]{1,0:T(8,128)(2,1)S(1)} collective-permute-done((bf16[144,1536]{1,0:T(8,128)(2,1)S(1)}, bf16[144,1536]{1,0:T(8,128)(2,1)S(1)}, u32[]{:S(2)}, u32[]{:S(2)}) %collective-permute-start.18) | collective-permute-done | bytes 442400 | tf_op jit(solution)/shard_map/ppermute | solution.py:67
  113.8 4.9 %middle_forward.1 = (f32[128,1536]{1,0:T(8,128)S(1)}, bf16[128,1536]{1,0:T(8,128)(2,1)S(1)}, bf16[128,1536]{1,0:T(8,128)(2,1)S(1)}, bf16[1536,1536]{1,0:T(8,128)(2,1)}) custom-call(s32[2]{0:T(128)S(1)} %pad_add_fusion.info_ref, bf16[256,192]{1,0:T(8,128)(2,1)S(1)} %copy-done.16, bf16[256,192]{1,0:T(8,128)(2,1)S(1)} %collective-permute-done.23.refs_1_, ...), custom_call_target="tpu_custom_call" | custom-call | flops 1 | bytes 1 | tf_op jit(solution)/shard_map/middle_forward/pallas_call | solution.py:764
  122.9 8.5 %collective-permute-done.31.refs_2_ = bf16[128,1536]{1,0:T(8,128)(2,1)S(1)} collective-permute-done((bf16[128,1536]{1,0:T(8,128)(2,1)S(1)}, bf16[128,1536]{1,0:T(8,128)(2,1)S(1)}, u32[]{:S(2)}, u32[]{:S(2)}) %collective-permute-start.31) | collective-permute-done | bytes 393248 | tf_op jit(solution)/shard_map/ppermute | solution.py:67
  131.4 8.3 %collective-permute-done.33.refs_4_ = bf16[128,1536]{1,0:T(8,128)(2,1)S(1)} collective-permute-done((bf16[128,1536]{1,0:T(8,128)(2,1)S(1)}, bf16[128,1536]{1,0:T(8,128)(2,1)S(1)}, u32[]{:S(2)}, u32[]{:S(2)}) %collective-permute-start.33) | collective-permute-done | bytes 393248 | tf_op jit(solution)/shard_map/ppermute | solution.py:67
  142.3 8.3 %ffn_units.1 = (bf16[1024,1536]{1,0:T(8,128)(2,1)}, bf16[1024,1024]{1,0:T(8,128)(2,1)}, bf16[1024,512]{1,0:T(8,128)(2,1)S(1)}) custom-call(bf16[128,1536]{1,0:T(8,128)(2,1)} %copy-done.12, bf16[128,1536]{1,0:T(8,128)(2,1)} %copy-done.45, bf16[128,1536]{1,0:T(8,128)(2,1)} %copy-done.41, bf16[128,1536]{1,0:T(8,128)(2,1)} %copy-done.46, ...), custom_call_target="tpu_custom_call" | custom-call | flops 1 | bytes 1 | tf_op jit(solution)/shard_map/ffn_units/pallas_call | solution.py:484
  152.7 3.5 ffn_forward.1
  164.6 6.5 %collective-permute-done.43 = bf16[128,1536]{1,0:T(8,128)(2,1)} collective-permute-done((bf16[128,1536]{1,0:T(8,128)(2,1)}, bf16[128,1536]{1,0:T(8,128)(2,1)}, u32[]{:S(2)}, u32[]{:S(2)}) %collective-permute-start.43) | collective-permute-done | bytes 393248 | tf_op jit(solution)/shard_map/ppermute | solution.py:67
  171.1 9.7 %collective-permute-done.41 = bf16[128,1536]{1,0:T(8,128)(2,1)} collective-permute-done((bf16[128,1536]{1,0:T(8,128)(2,1)}, bf16[128,1536]{1,0:T(8,128)(2,1)}, u32[]{:S(2)}, u32[]{:S(2)}) %collective-permute-start.41) | collective-permute-done | bytes 393248 | tf_op jit(solution)/shard_map/ppermute | solution.py:67
  187.5 8.6 %collective-permute-done.45.refs_2_ = bf16[128,1536]{1,0:T(8,128)(2,1)S(1)} collective-permute-done((bf16[128,1536]{1,0:T(8,128)(2,1)S(1)}, bf16[128,1536]{1,0:T(8,128)(2,1)S(1)}, u32[]{:S(2)}, u32[]{:S(2)}) %collective-permute-start.45) | collective-permute-done | bytes 393248 | tf_op jit(solution)/shard_map/ppermute | solution.py:67
  196.1 5.4 %collective-permute-done.47.refs_4_ = bf16[128,1536]{1,0:T(8,128)(2,1)S(1)} collective-permute-done((bf16[128,1536]{1,0:T(8,128)(2,1)S(1)}, bf16[128,1536]{1,0:T(8,128)(2,1)S(1)}, u32[]{:S(2)}, u32[]{:S(2)}) %collective-permute-start.47) | collective-permute-done | bytes 393248 | tf_op jit(solution)/shard_map/ppermute | solution.py:67
  205.1 8.0 %ffn_backward.1 = (bf16[1024,1536]{1,0:T(8,128)(2,1)S(1)}, bf16[1024,1024]{1,0:T(8,128)(2,1)S(1)}, bf16[128,1536]{1,0:T(8,128)(2,1)S(1)}, bf16[128,1536]{1,0:T(8...) custom-call(bf16[128,1536]{1,0:T(8,128)(2,1)S(1)} %get-tuple-element, ...), custom_call_target="tpu_custom_call" | custom-call | flops 1 | bytes 1 | tf_op jit(solution)/shard_map/ffn_backward/pallas_call | solution.py:559
  217.9 4.9 %convolution_convert_fusion = bf16[1536,1024]{1,0:T(8,128)(2,1)} fusion(bf16[1024,1536]{1,0:T(8,128)(2,1)S(1)} %copy-done.62, bf16[1024,1024]{1,0:T(8,128)(2,1)S(1)} %get-tuple-element.273), kind=kOutput, calls=%fused_computation | convolution fusion | flops 3222798336 | bytes 8388608 | tf_op jit(solution)/shard_map/dot_general | solution.py:52
  226.4 5.2 %convolution_convert_fusion.1 = bf16[512,1536]{1,0:T(8,128)(2,1)} fusion(bf16[1024,512]{1,0:T(8,128)(2,1)} %copy-done.3, bf16[1024,1536]{1,0:T(8,128)(2,1)} %copy-done.17), kind=kOutput, calls=%fused_computation.1 | convolution fusion | flops 1611399168 | bytes 5767168 | tf_op jit(solution)/shard_map/dot_general | solution.py:52
  231.8 3.2 collective-permute-done.57.refs_3_
  235.8 7.8 %collective-permute-done.55.refs_2_ = bf16[128,1536]{1,0:T(8,128)(2,1)} collective-permute-done((bf16[128,1536]{1,0:T(8,128)(2,1)}, bf16[128,1536]{1,0:T(8,128)(2,1)}, u32[]{:S(2)}, u32[]{:S(2)}) %collective-permute-start.55) | collective-permute-done | bytes 393248 | tf_op jit(solution)/shard_map/ppermute | solution.py:67
  244.6 5.2 %middle_backward.1 = (f32[128,1536]{1,0:T(8,128)S(1)}, bf16[128,1536]{1,0:T(8,128)(2,1)S(1)}, f32[1,1536]{1,0:T(1,128)S(1)}, bf16[128,384]{1,0:T(8,128)(2,1)S(1)...) custom-call(s32[1]{0:T(128)} %bitcast.me_ref.info_ref, ...), custom_call_target="tpu_custom_call" | custom-call | flops 1 | bytes 1 | tf_op jit(solution)/shard_map/middle_backward/pallas_call | solution.py:822
  265.4 14.6 %attention_backward.1 = (bf16[1536,384]{1,0:T(8,128)(2,1)S(1)}, f32[8,1536]{1,0:T(8,128)S(1)}, bf16[128,1536]{1,0:T(8,128)(2,1)S(1)}, bf16[128,1536]{1,0:T(8,128...) custom-call(s32[2]{0:T(128)S(1)} %pad_add_fusion.2.info_ref, ...), custom_call_target="tpu_custom_call" | custom-call | flops 1 | bytes 1 | tf_op jit(solution)/shard_map/attention_backward/pallas_call | solution.py:404
  280.1 8.0 %collective-permute-done.61.refs_3_ = bf16[192,1536]{1,0:T(8,128)(2,1)S(1)} collective-permute-done((bf16[192,1536]{1,0:T(8,128)(2,1)S(1)}, bf16[192,1536]{1,0:T(8,128)(2,1)S(1)}, u32[]{:S(2)}, u32[]{:S(2)}) %collective-permute-start.61) | collective-permute-done | bytes 589856 | tf_op jit(solution)/shard_map/ppermute | solution.py:67
  288.1 3.2 attention_packs.1
  301.3 23.0 %collective-permute-done.76 = bf16[128,1536]{1,0:T(8,128)(2,1)S(1)} collective-permute-done((bf16[128,1536]{1,0:T(8,128)(2,1)S(1)}, bf16[128,1536]{1,0:T(8,128)(2,1)S(1)}, u32[]{:S(2)}, u32[]{:S(2)}) %collective-permute-start.76) | collective-permute-done | bytes 393248 | tf_op jit(solution)/shard_map/ppermute | solution.py:67
  324.3 8.0 %collective-permute-done.77 = bf16[128,1536]{1,0:T(8,128)(2,1)S(1)} collective-permute-done((bf16[128,1536]{1,0:T(8,128)(2,1)}, bf16[128,1536]{1,0:T(8,128)(2,1)S(1)}, u32[]{:S(2)}, u32[]{:S(2)}) %collective-permute-start.77) | collective-permute-done | bytes 393248 | tf_op jit(solution)/shard_map/ppermute | solution.py:67
  337.6 7.0 %collective-permute-done.83.refs_2_ = bf16[128,1536]{1,0:T(8,128)(2,1)S(1)} collective-permute-done((bf16[128,1536]{1,0:T(8,128)(2,1)}, bf16[128,1536]{1,0:T(8,128)(2,1)S(1)}, u32[]{:S(2)}, u32[]{:S(2)}) %collective-permute-start.83) | collective-permute-done | bytes 393248 | tf_op jit(solution)/shard_map/ppermute | solution.py:67
  346.1 8.1 %collective-permute-done.81.refs_6_ = bf16[192,1024]{1,0:T(8,128)(2,1)} collective-permute-done((bf16[192,1024]{1,0:T(8,128)(2,1)S(1)}, bf16[192,1024]{1,0:T(8,128)(2,1)}, u32[]{:S(2)}, u32[]{:S(2)}) %collective-permute-start.81) | collective-permute-done | bytes 393248 | tf_op jit(solution)/shard_map/ppermute | solution.py:67
  358.6 3.8 collective-permute-done.85.refs_6_
  368.0 7.3 %column_grads.1 = (f32[384,4096]{1,0:T(8,128)}, f32[384,4096]{1,0:T(8,128)}) custom-call(s32[1]{0:T(128)} %bitcast.me_ref.info_ref, bf16[384,1024]{1,0:T(8,128)(2,1)} %reduce-scatter.6.cloned.1.call-done.refs_0_, bf16[384,1024]{1,0:T(8,128)(2,1)} %copy-done.33, bf16[384,1024]{1,0:T(8,128)(2,1)} %copy-done.25, ...), custom_call_target="tpu_custom_call" | custom-call | flops 1 | bytes 1 | tf_op jit(solution)/shard_map/column_grads/pallas_call | solution.py:656
  382.2 4.0 row_grads.1
  389.3 9.0 %attention_grads.1 = (f32[384,1536]{1,0:T(8,128)}, f32[384,768]{1,0:T(8,128)}, f32[384,768]{1,0:T(8,128)}, f32[384,1536]{1,0:T(8,128)}, f32[8,384]{1,0:T(8,128)S(1)}, /*index=5*/f32[1,1]{1,0:T(1,128)}) custom-call(s32[1]{0:T(128)} %bitcast.me_ref.info_ref, bf16[592,384]{1,0:T(8,128)(2,1)} %reduce-scatter.4.cloned.1.call-done.refs_0_, ...), custom_call_target="tpu_custom_call" | custom-call | flops 1 | bytes 1 | tf_op jit(solution)/shard_map/attention_grads/pallas_call | solution.py:1026
  (395 shorter events, 150.1 us)
Async XLA Ops:
  7.2 135.0 %all-gather.3.cloned.1.call-start = ((), (), s32[]{:S(2)}) async-start(), calls=%async_computation.3 | async-start | bytes 3932160 | tf_op jit(solution)/shard_map/all_gather | solution.py:1131
  13.1 23.5 %collective-permute-start.5 = (bf16[384,384]{1,0:T(8,128)(2,1)S(1)}, bf16[384,384]{1,0:T(8,128)(2,1)S(1)}, u32[]{:S(2)}, u32[]{:S(2)}) collective-permute-start(bf16[384,384]{1,0:T(8,128)(2,1)S(1)} %multiply_convert_fusion.1.refs_8_), channel_id=1, source_target_pairs={{0,2},{1,3},{2,0},{3,1},{4,6},{5,7},{6,4},{7,5},{8,10},{9,11},{10,... | collective-permute-start | bytes 884744 | tf_op jit(solution)/shard_map/ppermute | solution.py:67
  15.7 20.9 %collective-permute-start.6 = (bf16[384,384]{1,0:T(8,128)(2,1)S(1)}, bf16[384,384]{1,0:T(8,128)(2,1)S(1)}, u32[]{:S(2)}, u32[]{:S(2)}) collective-permute-start(bf16[384,384]{1,0:T(8,128)(2,1)S(1)} %multiply_convert_fusion.1.refs_8_), channel_id=1, source_target_pairs={{0,3},{1,2},{2,1},{3,0},{4,7},{5,6},{6,5},{7,4},{8,11},{9,10},{10,... | collective-permute-start | bytes 884744 | tf_op jit(solution)/shard_map/ppermute | solution.py:67
  17.6 18.9 %collective-permute-start.1 = (bf16[128,1536]{1,0:T(8,128)(2,1)S(1)}, bf16[128,1536]{1,0:T(8,128)(2,1)S(1)}, u32[]{:S(2)}, u32[]{:S(2)}) collective-permute-start(bf16[128,1536]{1,0:T(8,128)(2,1)S(1)} %multiply_convert_fusion.refs_0_), channel_id=1, source_target_pairs={{0,8},{4,12},{8,0},{12,4},{16,24},{20,28},{24,16},{28,20},{1,9},{5... | collective-permute-start | bytes 1179656 | tf_op jit(solution)/shard_map/ppermute | solution.py:67
  19.4 18.2 %collective-permute-start.2 = (bf16[128,1536]{1,0:T(8,128)(2,1)S(1)}, bf16[128,1536]{1,0:T(8,128)(2,1)S(1)}, u32[]{:S(2)}, u32[]{:S(2)}) collective-permute-start(bf16[128,1536]{1,0:T(8,128)(2,1)S(1)} %multiply_convert_fusion.refs_0_), channel_id=1, source_target_pairs={{0,16},{4,20},{8,24},{12,28},{16,0},{20,4},{24,8},{28,12},{1,17},{... | collective-permute-start | bytes 1179656 | tf_op jit(solution)/shard_map/ppermute | solution.py:67
  37.7 115.0 %all-gather.5.cloned.1.call-start = ((), (), s32[]{:S(2)}) async-start(), calls=%async_computation.4 | async-start | bytes 1966080 | tf_op jit(solution)/shard_map/all_gather | solution.py:1132
  46.3 29.7 %collective-permute-start.10 = (bf16[48,1536]{1,0:T(8,128)(2,1)}, bf16[48,1536]{1,0:T(8,128)(2,1)}, u32[]{:S(2)}, u32[]{:S(2)}) collective-permute-start(bf16[48,1536]{1,0:T(8,128)(2,1)} %constant_dynamic-slice_fusion.4), channel_id=1, source_target_pairs={{0,1},{1,0},{2,3},{3,2},{4,5},{5,4},{6,7},{7,6},{8,9},{9,8},{10,11... | collective-permute-start | bytes 442376 | tf_op jit(solution)/shard_map/ppermute | solution.py:67
  46.3 29.7 %collective-permute-start.11 = (bf16[48,1536]{1,0:T(8,128)(2,1)}, bf16[48,1536]{1,0:T(8,128)(2,1)}, u32[]{:S(2)}, u32[]{:S(2)}) collective-permute-start(bf16[48,1536]{1,0:T(8,128)(2,1)} %constant_dynamic-slice_fusion.4), channel_id=1, source_target_pairs={{0,2},{1,3},{2,0},{3,1},{4,6},{5,7},{6,4},{7,5},{8,10},{9,11},{10,... | collective-permute-start | bytes 442376 | tf_op jit(solution)/shard_map/ppermute | solution.py:67
  49.3 26.6 %collective-permute-start.12 = (bf16[48,1536]{1,0:T(8,128)(2,1)}, bf16[48,1536]{1,0:T(8,128)(2,1)}, u32[]{:S(2)}, u32[]{:S(2)}) collective-permute-start(bf16[48,1536]{1,0:T(8,128)(2,1)} %constant_dynamic-slice_fusion.4), channel_id=1, source_target_pairs={{0,3},{1,2},{2,1},{3,0},{4,7},{5,6},{6,5},{7,4},{8,11},{9,10},{10,... | collective-permute-start | bytes 442376 | tf_op jit(solution)/shard_map/ppermute | solution.py:67
  50.7 25.3 %collective-permute-start.14 = (f32[1,896]{1,0:T(1,128)S(1)}, f32[1,896]{1,0:T(1,128)S(1)}, u32[]{:S(2)}, u32[]{:S(2)}) collective-permute-start(f32[1,896]{1,0:T(1,128)S(1)} %reshape.79), channel_id=1, source_target_pairs={{0,2},{1,3},{2,0},{3,1},{4,6},{5,7},{6,4},{7,5},{8,10},{9,11},{10,... | collective-permute-start | bytes 10760 | tf_op jit(solution)/shard_map/ppermute | solution.py:67
  50.8 25.1 %collective-permute-start.15 = (f32[1,896]{1,0:T(1,128)S(1)}, f32[1,896]{1,0:T(1,128)}, u32[]{:S(2)}, u32[]{:S(2)}) collective-permute-start(f32[1,896]{1,0:T(1,128)S(1)} %reshape.79), channel_id=1, source_target_pairs={{0,3},{1,2},{2,1},{3,0},{4,7},{5,6},{6,5},{7,4},{8,11},{9,10},{10,... | collective-permute-start | bytes 10760 | tf_op jit(solution)/shard_map/ppermute | solution.py:67
  53.3 242.0 %reduce-scatter.6.cloned.1.call-start = ((), (), s32[]{:S(2)}) async-start(), calls=%async_computation.6 | async-start | bytes 3932160 | tf_op jit(solution)/shard_map/reduce_scatter | solution.py:1167
  120.4 19.4 %collective-permute-start.33 = (bf16[128,1536]{1,0:T(8,128)(2,1)S(1)}, bf16[128,1536]{1,0:T(8,128)(2,1)S(1)}, u32[]{:S(2)}, u32[]{:S(2)}) collective-permute-start(bf16[128,1536]{1,0:T(8,128)(2,1)S(1)} %get-tuple-element.239.refs_0_), channel_id=1, source_target_pairs={{0,16},{4,20},{8,24},{12,28},{16,0},{20,4},{24,8},{28,12},{1,17},{... | collective-permute-start | bytes 1179656 | tf_op jit(solution)/shard_map/ppermute | solution.py:67
  121.8 18.0 %collective-permute-start.35 = (bf16[128,1536]{1,0:T(8,128)(2,1)S(1)}, bf16[128,1536]{1,0:T(8,128)(2,1)S(1)}, u32[]{:S(2)}, u32[]{:S(2)}) collective-permute-start(bf16[128,1536]{1,0:T(8,128)(2,1)S(1)} %get-tuple-element.239.refs_0_), channel_id=1, source_target_pairs={{0,24},{4,28},{8,16},{12,20},{16,8},{20,12},{24,0},{28,4},{1,25},{... | collective-permute-start | bytes 1179656 | tf_op jit(solution)/shard_map/ppermute | solution.py:67
  122.9 17.3 %collective-permute-start.30 = (bf16[128,1536]{1,0:T(8,128)(2,1)S(1)}, bf16[128,1536]{1,0:T(8,128)(2,1)S(1)}, u32[]{:S(2)}, u32[]{:S(2)}) collective-permute-start(bf16[128,1536]{1,0:T(8,128)(2,1)S(1)} %get-tuple-element.239.refs_0_), channel_id=1, source_target_pairs={{0,4},{4,0},{8,12},{12,8},{16,20},{20,16},{24,28},{28,24},{1,5},{5... | collective-permute-start | bytes 1179656 | tf_op jit(solution)/shard_map/ppermute | solution.py:67
  161.1 19.6 %collective-permute-start.41 = (bf16[128,1536]{1,0:T(8,128)(2,1)}, bf16[128,1536]{1,0:T(8,128)(2,1)}, u32[]{:S(2)}, u32[]{:S(2)}) collective-permute-start(bf16[128,1536]{1,0:T(8,128)(2,1)} %add_convert_fusion.10), channel_id=1, source_target_pairs={{0,16},{4,20},{8,24},{12,28},{16,0},{20,4},{24,8},{28,12},{1,17},{... | collective-permute-start | bytes 1179656 | tf_op jit(solution)/shard_map/ppermute | solution.py:67
  186.1 17.3 %collective-permute-start.49 = (bf16[128,1536]{1,0:T(8,128)(2,1)S(1)}, bf16[128,1536]{1,0:T(8,128)(2,1)S(1)}, u32[]{:S(2)}, u32[]{:S(2)}) collective-permute-start(bf16[128,1536]{1,0:T(8,128)(2,1)S(1)} %get-tuple-element.372.refs_0_), channel_id=1, source_target_pairs={{0,24},{4,28},{8,16},{12,20},{16,8},{20,12},{24,0},{28,4},{1,25},{... | collective-permute-start | bytes 1179656 | tf_op jit(solution)/shard_map/ppermute | solution.py:67
  222.8 109.6 %reduce-scatter.8.cloned.1.call-start = ((), (), s32[]{:S(2)}) async-start(), calls=%async_computation.7 | async-start | bytes 1966080 | tf_op jit(solution)/shard_map/reduce_scatter | solution.py:1168
  224.0 19.6 %collective-permute-start.55 = (bf16[128,1536]{1,0:T(8,128)(2,1)}, bf16[128,1536]{1,0:T(8,128)(2,1)}, u32[]{:S(2)}, u32[]{:S(2)}) collective-permute-start(bf16[128,1536]{1,0:T(8,128)(2,1)} %add_convert_fusion.7), channel_id=1, source_target_pairs={{0,16},{4,20},{8,24},{12,28},{16,0},{20,4},{24,8},{28,12},{1,17},{... | collective-permute-start | bytes 1179656 | tf_op jit(solution)/shard_map/ppermute | solution.py:67
  225.7 17.9 %collective-permute-start.53 = (bf16[128,1536]{1,0:T(8,128)(2,1)}, bf16[128,1536]{1,0:T(8,128)(2,1)}, u32[]{:S(2)}, u32[]{:S(2)}) collective-permute-start(bf16[128,1536]{1,0:T(8,128)(2,1)} %add_convert_fusion.8), channel_id=1, source_target_pairs={{0,24},{4,28},{8,16},{12,20},{16,8},{20,12},{24,0},{28,4},{1,25},{... | collective-permute-start | bytes 1179656 | tf_op jit(solution)/shard_map/ppermute | solution.py:67
  231.6 131.2 %reduce-scatter.4.cloned.1.call-start = ((), (), s32[]{:S(2)}) async-start(), calls=%async_computation.5 | async-start | bytes 2273280 | tf_op jit(solution)/shard_map/reduce_scatter | solution.py:1187
  258.7 21.4 %collective-permute-start.63 = (bf16[192,1536]{1,0:T(8,128)(2,1)S(1)}, bf16[192,1536]{1,0:T(8,128)(2,1)S(1)}, u32[]{:S(2)}, u32[]{:S(2)}) collective-permute-start(bf16[192,1536]{1,0:T(8,128)(2,1)S(1)} %add_convert_fusion), channel_id=1, source_target_pairs={{0,8},{4,12},{8,0},{12,4},{16,24},{20,28},{24,16},{28,20},{1,9},{5... | collective-permute-start | bytes 1769480 | tf_op jit(solution)/shard_map/ppermute | solution.py:67
  260.3 27.8 %collective-permute-start.61 = (bf16[192,1536]{1,0:T(8,128)(2,1)S(1)}, bf16[192,1536]{1,0:T(8,128)(2,1)S(1)}, u32[]{:S(2)}, u32[]{:S(2)}) collective-permute-start(bf16[192,1536]{1,0:T(8,128)(2,1)S(1)} %add_convert_fusion.1), channel_id=1, source_target_pairs={{0,16},{4,20},{8,24},{12,28},{16,0},{20,4},{24,8},{28,12},{1,17},{... | collective-permute-start | bytes 1769480 | tf_op jit(solution)/shard_map/ppermute | solution.py:67
  261.0 27.0 %collective-permute-start.59 = (bf16[192,1536]{1,0:T(8,128)(2,1)S(1)}, bf16[192,1536]{1,0:T(8,128)(2,1)S(1)}, u32[]{:S(2)}, u32[]{:S(2)}) collective-permute-start(bf16[192,1536]{1,0:T(8,128)(2,1)S(1)} %add_convert_fusion.2), channel_id=1, source_target_pairs={{0,24},{4,28},{8,16},{12,20},{16,8},{20,12},{24,0},{28,4},{1,25},{... | collective-permute-start | bytes 1769480 | tf_op jit(solution)/shard_map/ppermute | solution.py:67
  295.3 37.0 %collective-permute-start.79 = (bf16[384,1024]{1,0:T(8,128)(2,1)}, bf16[384,1024]{1,0:T(8,128)(2,1)S(1)}, u32[]{:S(2)}, u32[]{:S(2)}) collective-permute-start(bf16[384,1024]{1,0:T(8,128)(2,1)} %reduce-scatter.6.cloned.1.call-done.refs_0_), channel_id=1, source_target_pairs={{0,8},{4,12},{8,0},{12,4},{16,24},{20,28},{24,16},{28,20},{1,9},{5... | collective-permute-start | bytes 2359304 | tf_op jit(solution)/shard_map/ppermute | solution.py:67
  295.9 36.4 %collective-permute-start.80 = (bf16[384,1024]{1,0:T(8,128)(2,1)}, bf16[384,1024]{1,0:T(8,128)(2,1)}, u32[]{:S(2)}, u32[]{:S(2)}) collective-permute-start(bf16[384,1024]{1,0:T(8,128)(2,1)} %reduce-scatter.6.cloned.1.call-done.refs_0_), channel_id=1, source_target_pairs={{0,16},{4,20},{8,24},{12,28},{16,0},{20,4},{24,8},{28,12},{1,17},{... | collective-permute-start | bytes 2359304 | tf_op jit(solution)/shard_map/ppermute | solution.py:67
  297.7 26.6 %collective-permute-start.76 = (bf16[128,1536]{1,0:T(8,128)(2,1)S(1)}, bf16[128,1536]{1,0:T(8,128)(2,1)S(1)}, u32[]{:S(2)}, u32[]{:S(2)}) collective-permute-start(bf16[128,1536]{1,0:T(8,128)(2,1)S(1)} %add_convert_fusion.5), channel_id=1, source_target_pairs={{0,8},{4,12},{8,0},{12,4},{16,24},{20,28},{24,16},{28,20},{1,9},{5... | collective-permute-start | bytes 1179656 | tf_op jit(solution)/shard_map/ppermute | solution.py:67
  298.2 34.1 %collective-permute-start.77 = (bf16[128,1536]{1,0:T(8,128)(2,1)}, bf16[128,1536]{1,0:T(8,128)(2,1)S(1)}, u32[]{:S(2)}, u32[]{:S(2)}) collective-permute-start(bf16[128,1536]{1,0:T(8,128)(2,1)} %add_convert_fusion.4), channel_id=1, source_target_pairs={{0,16},{4,20},{8,24},{12,28},{16,0},{20,4},{24,8},{28,12},{1,17},{... | collective-permute-start | bytes 1179656 | tf_op jit(solution)/shard_map/ppermute | solution.py:67
  299.5 32.8 %collective-permute-start.78 = (bf16[128,1536]{1,0:T(8,128)(2,1)}, bf16[128,1536]{1,0:T(8,128)(2,1)}, u32[]{:S(2)}, u32[]{:S(2)}) collective-permute-start(bf16[128,1536]{1,0:T(8,128)(2,1)} %add_convert_fusion.3), channel_id=1, source_target_pairs={{0,24},{4,28},{8,16},{12,20},{16,8},{20,12},{24,0},{28,4},{1,25},{... | collective-permute-start | bytes 1179656 | tf_op jit(solution)/shard_map/ppermute | solution.py:67
  333.9 22.2 %collective-permute-start.89 = (bf16[384,1024]{1,0:T(8,128)(2,1)}, bf16[384,1024]{1,0:T(8,128)(2,1)S(1)}, u32[]{:S(2)}, u32[]{:S(2)}) collective-permute-start(bf16[384,1024]{1,0:T(8,128)(2,1)} %reduce-scatter.6.cloned.1.call-done.refs_0_), channel_id=1, source_target_pairs={{0,4},{4,0},{8,12},{12,8},{16,20},{20,16},{24,28},{28,24},{1,5},{5... | collective-permute-start | bytes 2359304 | tf_op jit(solution)/shard_map/ppermute | solution.py:67
  334.5 19.7 %collective-permute-start.81 = (bf16[192,1024]{1,0:T(8,128)(2,1)S(1)}, bf16[192,1024]{1,0:T(8,128)(2,1)}, u32[]{:S(2)}, u32[]{:S(2)}) collective-permute-start(bf16[192,1024]{1,0:T(8,128)(2,1)S(1)} %slice.32), channel_id=1, source_target_pairs={{0,16},{4,20},{8,24},{12,28},{16,0},{20,4},{24,8},{28,12},{1,17},{... | collective-permute-start | bytes 1179656 | tf_op jit(solution)/shard_map/ppermute | solution.py:67
  346.0 19.7 %collective-permute-start.90 = (bf16[384,1024]{1,0:T(8,128)(2,1)S(1)}, bf16[384,1024]{1,0:T(8,128)(2,1)}, u32[]{:S(2)}, u32[]{:S(2)}) collective-permute-start(bf16[384,1024]{1,0:T(8,128)(2,1)S(1)} %collective-permute-done.79.refs_2_), channel_id=1, source_target_pairs={{0,4},{4,0},{8,12},{12,8},{16,20},{20,16},{24,28},{28,24},{1,5},{5... | collective-permute-start | bytes 2359304 | tf_op jit(solution)/shard_map/ppermute | solution.py:67
  (142 other events, 1076.5 us)
Sparse Core Ops, SparseCore 0:
  37.8 76.2 all-gather.2
  115.6 37.0 all-gather.4
  222.9 60.7 reduce-scatter.5
  286.4 35.3 reduce-scatter.7
  324.4 38.2 reduce-scatter.3
